TPU v7x, 32 devices: a whole 2x2x4 slice. The times are simulated.
32 devices in a mesh: fsdp: 32 (over z, y, x, core).
Axes of the slice: x: 2, y: 2, z: 4, core: 2. Of those that a mesh axis runs over, the one named last changes fastest.
Arguments:
- tokens: bfloat16 [8192, 768], P('fsdp'), may hold values from -6 to 6
- row_kind: int32 [32], P('fsdp'), may hold values from 0 to 1, as said below
- w_qkv: bfloat16 [2, 768, 2304], P(None, 'fsdp'), may hold values from -0.21875 to 0.21875
- w_out: bfloat16 [2, 768, 768], P(None, 'fsdp'), may hold values from -0.875 to 0.875
- w_up: bfloat16 [2, 768, 3072], P(None, 'fsdp'), may hold values from -0.21875 to 0.21875
- w_down: bfloat16 [2, 3072, 768], P(None, 'fsdp'), may hold values from -0.109375 to 0.109375
- bias_vectors: bfloat16 [2, 6, 768], P(None, None, 'fsdp'), may hold values from -3 to 3
- gains: bfloat16 [2, 2, 768], P(None, None, 'fsdp'), may hold values from 0.25 to 1.75
- bias_up: bfloat16 [2, 3072], P(None, 'fsdp'), may hold values from -3 to 3
- cotangent: bfloat16 [8192, 768], P('fsdp'), may hold values from -6 to 6
Outputs:
- mixed: bfloat16 [8192, 768], P('fsdp')
- grad_tokens: float32 [8192, 768], P('fsdp')
- grad_w_qkv: float32 [2, 768, 2304], P(None, 'fsdp')
- grad_w_out: float32 [2, 768, 768], P(None, 'fsdp')
- grad_w_up: float32 [2, 768, 3072], P(None, 'fsdp')
- grad_w_down: float32 [2, 3072, 768], P(None, 'fsdp')
- grad_bias_vectors: float32 [2, 6, 768], P(None, None, 'fsdp')
- grad_gains: float32 [2, 2, 768], P(None, None, 'fsdp')
- grad_bias_up: float32 [2, 3072], P(None, 'fsdp')
Inputs may be any that keep to these rules, and one draw needn't show every extreme that they name: row_kind[i] equals row_kind[i + 1] for every even i. Pair 0, pair 8192 // 1024 and the last pair hold long rows, pair 1 holds short rows.
All inputs are finite; a program needn't handle non-finite values.
Results may differ from a plain program's by a relative error of at most 0.018.
Values may be sent and summed in bfloat16 or wider, within the bound.
No kernel may reach another device: no remote copies, remote signals or barrier semaphores. Data moves between devices by JAX's collectives and lax.ppermute only.
A program may use at most 256 MiB of HBM per device.

v0:
```python
import functools

import jax
import jax.numpy as jnp
from jax import lax
from jax.experimental import pallas as pl
from jax.experimental.pallas import tpu as pltpu
from jax.sharding import PartitionSpec as P

HEADS = 12
HEAD_DIM = 64
LAYERS = 2
SHORT = 128
AXIS = "fsdp"

EPSILON = 1e-05
MASKED_SCORE = -1e30
BF = jnp.bfloat16
F32 = jnp.float32
LATENCY = 2.5
UNIT = 1.48
ATTN, FFN = 0, 1
OPEN_SENDS = 4
VMEM_LIMIT = 24 * 2**20
DIRECT = (False, False, False, False)
ORDER = (
    0, 16, 6, 1, 11, 17, 7, 18, 2, 21, 8, 12, 19, 9, 13, 3, 22, 20, 23, 10, 14, 24, 26,
    15, 27, 4, 28, 29, 25, 30, 5, 31, 33, 34, 35, 37, 36, 47, 32, 48, 38, 49, 39, 42, 51,
    43, 50, 52, 40, 44, 56, 53, 45, 57, 58, 54, 41, 55, 46, 59, 61, 60,
)


def dot(left, right):
    return jnp.dot(left, right, preferred_element_type=F32)


def dot_tn(left, right):
    return lax.dot_general(left, right, (((0,), (0,)), ((), ())), preferred_element_type=F32)


def dot_nt(left, right):
    return lax.dot_general(left, right, (((1,), (1,)), ((), ())), preferred_element_type=F32)


def swap(value, mask):
    pairs = [(source, source ^ mask) for source in range(lax.axis_size(AXIS))]
    return lax.ppermute(value, AXIS, pairs)


def merge(mine, theirs, bit, axis):
    first = jnp.where(bit == 0, mine, theirs)
    second = jnp.where(bit == 0, theirs, mine)
    return jnp.stack([first, second], axis=axis)


def pick(pair, index, axis):
    return lax.dynamic_index_in_dim(pair, index, axis, keepdims=False)


class Chips:
    def __init__(self):
        device = lax.axis_index(AXIS)
        self.count = lax.axis_size(AXIS) // 2
        self.core = device % 2
        self.chip = device // 2
        self.step = self.count // 4
        self.top = self.chip // self.step
        self.low = list(range(self.count.bit_length() - 3))

    def bit(self, place):
        return (self.chip // 2**place) % 2

    def plane_bit(self, step):
        return jnp.where(self.core == 0, self.bit(step), self.bit(len(self.low) - 1 - step))

    def plane_swap(self, value, step):
        masks = (2 * 2**step, 2 * 2 ** (len(self.low) - 1 - step))
        pairs = [(source, source ^ masks[source % 2]) for source in range(2 * self.count)]
        return lax.ppermute(value, AXIS, pairs)

    def half_places(self, step, own):
        bit = self.plane_bit(step)
        bit = bit if own else 1 - bit
        index = jnp.arange(2**step)
        return jnp.where(self.core == 0, 2**step * bit + index, 2 * index + bit)


class Sequence:
    def __init__(self):
        self.last = None

    def gate(self, values):
        if self.last is None:
            return values
        values, _ = lax.optimization_barrier((values, self.last))
        return values

    def mark(self, values):
        self.last = values


class State:
    def __getattr__(self, name):
        value = {}
        setattr(self, name, value)
        return value


class Plan:
    def __init__(self):
        self.pieces = []

    def add(self, name, rank, cost, needs, run, sends=()):
        self.pieces.append((name, rank, cost, needs, run, sends))

    def greedy(self):
        now = 0.0
        ready = {}
        free = {}
        open_sends = {}
        waiting = list(range(len(self.pieces)))
        order = []

        def fits(piece):
            held = sum(weight for label, weight in open_sends.items() if label not in piece[3])
            added = sum(weight for _, _, weight in piece[5])
            return added == 0 or held + added <= OPEN_SENDS

        while waiting:
            known = []
            for place in waiting:
                piece = self.pieces[place]
                if all(need in ready for need in piece[3]):
                    time = max([ready[need] for need in piece[3]], default=0.0)
                    known.append((time, piece[1], place))
            known = [entry for entry in known if fits(self.pieces[entry[2]])] or known
            able = [entry[1:] for entry in known if entry[0] <= now]
            place = min(able)[1] if able else min(known)[2]
            name, _, cost, needs, _, sends = self.pieces[place]
            now = max([now] + [ready[need] for need in needs]) + cost
            ready[name] = now
            for need in needs:
                open_sends.pop(need, None)
            for label, links, weight in sends:
                ready[label] = 0.0
                for link, length in links:
                    free[link] = max(now, free.get(link, 0.0)) + length
                    ready[label] = max(ready[label], free[link] + LATENCY)
                if weight > 0:
                    open_sends[label] = weight
            waiting.remove(place)
            order.append(place)
        return order

    def run(self):
        order = ORDER if len(ORDER) == len(self.pieces) else self.greedy()
        for place in order:
            self.pieces[place][4]()


class Gather:
    def __init__(self, chips, sequence, direct, piece):
        self.chips, self.sequence = chips, sequence
        self.direct = direct
        self.piece = piece
        self.steps_done = 0
        self.held = None

    def start(self):
        self.piece = self.sequence.gate(self.piece)
        self.sequence.mark(self.piece)
        if self.direct:
            self.coming = [swap(self.piece, 2 * self.chips.step * k) for k in (1, 2, 3)]
            self.steps_done = 1
        else:
            self.coming = swap(self.piece, 2 * 2 * self.chips.step)

    def advance(self):
        chips = self.chips
        coming = self.sequence.gate(self.coming)
        step = self.steps_done
        self.steps_done += 1
        if step == 0:
            self.held = merge_rows(self.piece[None, None], coming[None, None], chips.top // 2, 0)
            self.held = self.held.reshape((2,) + self.piece.shape)
            self.sequence.mark(self.held)
            self.coming = swap(self.held, 2 * chips.step)
            return
        if step == 1:
            if self.direct:
                parts = [self.piece] + coming
                parts = [merge(parts[i], parts[i + 1], chips.top % 2, 0) for i in (0, 2)]
                held = merge(parts[0], parts[1], chips.top // 2, 0)
            else:
                held = merge_rows(self.held[:, None], coming[:, None], chips.top % 2, 0)
            self.held = held.reshape((4, 1) + self.piece.shape)
        else:
            bit = chips.plane_bit(step - 2)
            self.held = merge_rows(self.held, coming, bit, chips.core)
        self.sequence.mark(self.held)
        self.coming = chips.plane_swap(self.held, step - 1)

    def finish(self, ranges):
        chips = self.chips
        while self.steps_done <= len(chips.low):
            self.advance()
        coming = self.sequence.gate(self.coming)
        bit = chips.plane_bit(self.steps_done - 2)
        results = merge_rows(self.held, coming, bit, chips.core, ranges)
        results = [whole.reshape((chips.count,) + whole.shape[2:]) for whole in results]
        self.sequence.mark(results)
        return results


def merge_kernel(ranges, place_ref, mine_ref, theirs_ref, *out_refs):
    half = mine_ref.shape[1]
    for lead in range(mine_ref.shape[0]):
        for index in range(half):
            for (start, stop), out_ref in zip(ranges, out_refs):
                out_ref[lead, place_ref[index]] = mine_ref[lead, index, start:stop]
                out_ref[lead, place_ref[half + index]] = theirs_ref[lead, index, start:stop]


def merge_rows(mine, theirs, bit, inner, ranges=None):
    half = mine.shape[1]
    cuts = ranges or [(0, mine.shape[2])]
    if all(edge % 16 == 0 for cut in cuts for edge in cut):
        index = jnp.arange(half)

        def place(own):
            return jnp.where(inner == 1, 2 * index + own, half * own + index)

        places = jnp.concatenate([place(bit), place(1 - bit)]).astype(jnp.int32)
        shapes = [
            jax.ShapeDtypeStruct((mine.shape[0], 2 * half, stop - start, mine.shape[3]), BF)
            for start, stop in cuts
        ]
        results = kernel_call(
            functools.partial(merge_kernel, cuts), shapes, [], places, mine, theirs
        )
    else:
        results = []
        for start, stop in cuts:
            cut = [value[:, :, start:stop] for value in (mine, theirs)]
            outer = merge(*cut, bit, 1)
            outer = outer.reshape((mine.shape[0], 2 * half) + outer.shape[3:])
            results.append(
                jnp.where(inner == 1, merge(*cut, bit, 2).reshape(outer.shape), outer)
            )
    return results if ranges else results[0]


class Scatter:
    def __init__(self, chips, sequence, count):
        self.chips, self.sequence = chips, sequence
        self.steps_done = 0
        self.arrays = [None] * count
        self.coming = [None] * count

    def start(self, part, arrays):
        chips = self.chips
        step = len(chips.low) - 1
        shape = (4, 2 ** len(chips.low))
        arrays = [value.reshape(shape + value.shape[1:]) for value in arrays]
        self.arrays[part] = arrays
        sent = send_rows(arrays, chips.half_places(step, False))
        self.coming[part] = chips.plane_swap(sent, step)
        self.sent = sent

    def advance(self):
        chips = self.chips
        coming = self.sequence.gate(self.coming)
        self.steps_done += 1
        step = len(chips.low) - 1 - self.steps_done
        if self.steps_done == 1:
            self.heights = [value.shape[2] for part in self.arrays for value in part]
            kept = chips.half_places(step + 1, True)
        else:
            self.arrays, coming = [[self.kept]], [coming]
            kept = jnp.arange(self.kept.shape[1])
        if step >= 0:
            sides = [chips.half_places(step, own) for own in (False, True)]
        else:
            bit = chips.top % 2 if step == -1 else chips.top // 2
            sides = [jnp.reshape(1 - bit, (1,)), jnp.reshape(bit, (1,))]
            lead = 2 if step == -1 else 1
            self.arrays = [
                [value.reshape((lead, 2) + value.shape[-2:]) for value in part]
                for part in self.arrays
            ]
            coming = [got.reshape((lead, 2) + got.shape[-2:]) for got in coming]
            kept = jnp.arange(2)
        sent, self.kept = fold_rows(self.arrays, coming, kept, sides)
        self.sequence.mark(sent)
        if step >= 0:
            self.coming = chips.plane_swap(sent, step)
        else:
            self.coming = swap(sent, 2 * chips.step if step == -1 else 4 * chips.step)

    def finish(self):
        coming = self.sequence.gate(self.coming)
        total = self.kept[0, 0] + coming[0, 0].astype(F32)
        self.sequence.mark(total)
        ends = [sum(self.heights[:i]) for i in range(len(self.heights) + 1)]
        return [total[start:stop] for start, stop in zip(ends[:-1], ends[1:])]


def send_kernel(heights, place_ref, *refs):
    *array_refs, sent_ref = refs
    for lead in range(sent_ref.shape[0]):
        for index in range(sent_ref.shape[1]):
            row = 0
            for height, ref in zip(heights, array_refs):
                sent_ref[lead, index, row : row + height] = ref[lead, place_ref[index]]
                row += height


def send_rows(arrays, places):
    heights = [value.shape[2] for value in arrays]
    shape = (arrays[0].shape[0], places.shape[0], sum(heights), arrays[0].shape[3])
    if any(height % 16 for height in heights):
        return jnp.concatenate([jnp.take(value, places, axis=1) for value in arrays], axis=2)
    (sent,) = kernel_call(
        functools.partial(send_kernel, heights), [jax.ShapeDtypeStruct(shape, BF)], [],
        places.astype(jnp.int32), *arrays,
    )
    return sent


def fold_kernel(layout, place_ref, *refs):
    *refs, sent_ref, kept_ref = refs
    count = sent_ref.shape[1]
    for lead in range(sent_ref.shape[0]):
        for index in range(count):
            for array, got, start, height, row in layout:
                for side, out_ref in enumerate((sent_ref, kept_ref)):
                    place = 2 * (count * side + index)
                    mine = refs[array][lead, place_ref[place]]
                    theirs = refs[got][lead, place_ref[place + 1], start : start + height]
                    total = mine.astype(F32) + theirs.astype(F32)
                    out_ref[lead, index, row : row + height] = total.astype(out_ref.dtype)


def fold_rows(parts, coming, kept, sides):
    arrays = [value for part in parts for value in part]
    layout = []
    row = 0
    for part, got in zip(range(len(parts)), range(len(arrays), len(arrays) + len(coming))):
        start = 0
        for value in parts[part]:
            height = value.shape[2]
            layout.append((len(layout), got, start, height, row))
            start += height
            row += height
    shape = (arrays[0].shape[0], sides[0].shape[0], row, arrays[0].shape[3])
    if any(value.shape[2] % 16 for value in arrays):
        totals = []
        for array, got, start, height, _ in layout:
            theirs = coming[got - len(arrays)][:, :, start : start + height]
            totals.append(jnp.take(arrays[array], kept, axis=1).astype(F32) + theirs.astype(F32))
        total = jnp.concatenate(totals, axis=2)
        return [jnp.take(total, side, axis=1).astype(kind) for side, kind in zip(sides, (BF, F32))]
    places = [jnp.stack([jnp.take(kept, side), side], axis=1).reshape(-1) for side in sides]
    return kernel_call(
        functools.partial(fold_kernel, layout),
        [jax.ShapeDtypeStruct(shape, kind) for kind in (BF, F32)], [],
        jnp.concatenate(places).astype(jnp.int32), *arrays, *coming,
    )


ROOT_HALF = 0.7071067811865476
DENSITY = 0.3989422804014327


def unit_rows(values):
    centre = values - jnp.mean(values, axis=1, keepdims=True)
    scale = lax.rsqrt(jnp.mean(centre * centre, axis=1, keepdims=True) + EPSILON)
    return centre * scale, scale


def norm_kernel(base_ref, mine_ref, theirs_ref, vec_ref, sum_ref, out_ref, out_b_ref):
    def chunk_step(chunk, carry):
        rows = pl.ds(pl.multiple_of(chunk * SHORT, SHORT), SHORT)
        total = base_ref[rows, :] + (
            mine_ref[rows, :].astype(F32) + theirs_ref[rows, :].astype(F32)
        ) + vec_ref[3:4, :]
        sum_ref[rows, :] = total
        unit, _ = unit_rows(total)
        output = unit * vec_ref[7:8, :] + vec_ref[5:6, :]
        out_ref[rows, :] = output
        out_b_ref[rows, :] = output.astype(BF)
        return carry

    lax.fori_loop(0, base_ref.shape[0] // SHORT, chunk_step, 0)


def hidden_kernel(
    x_ref, mine_ref, theirs_ref, vec_ref, bias_ref, up0_ref, up1_ref, down_ref,
    sum_ref, normed_ref, normed_b_ref, act_ref, slope_ref, partial_ref,
):
    def chunk_step(chunk, carry):
        rows = pl.ds(pl.multiple_of(chunk * SHORT, SHORT), SHORT)
        total = x_ref[rows, :] + (
            mine_ref[rows, :].astype(F32) + theirs_ref[rows, :].astype(F32) + vec_ref[2:3, :]
        )
        sum_ref[rows, :] = total
        unit, _ = unit_rows(total)
        normed = unit * vec_ref[6:7, :] + vec_ref[4:5, :]
        normed_ref[rows, :] = normed
        normed_b_ref[rows, :] = normed.astype(BF)
        return carry

    lax.fori_loop(0, x_ref.shape[0] // SHORT, chunk_step, 0)
    width = up0_ref.shape[1]
    step = 256
    for panel, up_ref in enumerate((up0_ref, up1_ref)):
        for start in range(0, width, step):
            place = panel * width + start
            pre = dot(normed_b_ref[...], up_ref[:, start : start + step])
            pre = pre + bias_ref[:, place : place + step]
            share = 0.5 + 0.5 * lax.erf(pre * ROOT_HALF)
            slope = share + pre * (DENSITY * jnp.exp(pre * pre * -0.5))
            act_ref[:, place : place + step] = (pre * share).astype(BF)
            slope_ref[:, place : place + step] = slope.astype(BF)
    partial_ref[...] = dot(act_ref[...], down_ref[...]).astype(BF)


def norm_back(upstream, total, gain):
    unit, scale = unit_rows(total)
    scaled = upstream * gain
    first = jnp.mean(scaled, axis=1, keepdims=True)
    second = jnp.mean(scaled * unit, axis=1, keepdims=True)
    return (
        scale * (scaled - first - unit * second),
        jnp.sum(upstream * unit, axis=0, keepdims=True),
        jnp.sum(upstream, axis=0, keepdims=True),
    )


def back_second_kernel(has_base, *refs):
    base_refs, refs = refs[: 3 if has_base else 1], refs[3 if has_base else 1 :]
    sum_ref, vec_ref, act_ref, d_second_ref, d_ffn_ref, g_down_ref, sums_ref = refs
    sums_ref[...] = jnp.zeros_like(sums_ref)

    def chunk_step(chunk, carry):
        rows = pl.ds(pl.multiple_of(chunk * SHORT, SHORT), SHORT)
        upstream = base_refs[0][rows, :].astype(F32)
        if has_base:
            upstream = upstream + (
                base_refs[1][rows, :].astype(F32) + base_refs[2][rows, :].astype(F32)
            )
        d_second, d_gain, d_shift = norm_back(upstream, sum_ref[rows, :], vec_ref[7:8, :])
        d_second_ref[rows, :] = d_second
        d_ffn = d_second.astype(BF)
        d_ffn_ref[rows, :] = d_ffn
        sums_ref[1:2, :] += jnp.sum(d_ffn.astype(F32), axis=0, keepdims=True)
        sums_ref[3:4, :] += d_shift
        sums_ref[5:6, :] += d_gain
        return carry

    lax.fori_loop(0, sum_ref.shape[0] // SHORT, chunk_step, 0)
    g_down_ref[...] = dot_tn(act_ref[...], d_ffn_ref[...]).astype(BF)


def back_hidden_kernel(
    d_ffn_ref, slope_ref, normed_b_ref, down_ref, up0_ref, up1_ref,
    g_up0_ref, g_up1_ref, partial_ref, sums_ref, d_pre_ref,
):
    hidden = slope_ref.shape[1]
    step = 256
    for place in range(0, hidden, step):
        d_act = dot_nt(d_ffn_ref[...], down_ref[place : place + step, :])
        d_pre = (d_act * slope_ref[:, place : place + step].astype(F32)).astype(BF)
        d_pre_ref[:, place : place + step] = d_pre
        sums_ref[:, place : place + step] = jnp.sum(d_pre.astype(F32), axis=0, keepdims=True)
    width = up0_ref.shape[1]
    g_up0_ref[...] = dot_tn(normed_b_ref[...], d_pre_ref[:, :width]).astype(BF)
    g_up1_ref[...] = dot_tn(normed_b_ref[...], d_pre_ref[:, width:]).astype(BF)
    partial_ref[...] = (
        dot_nt(d_pre_ref[:, :width], up0_ref[...]) + dot_nt(d_pre_ref[:, width:], up1_ref[...])
    ).astype(BF)


def back_first(
    d_second_ref, mine_ref, theirs_ref, sum_ref, vec_ref, d_first_ref, dbranch_ref, sums_ref
):
    sums_ref[...] = jnp.zeros_like(sums_ref)

    def chunk_step(chunk, carry):
        rows = pl.ds(pl.multiple_of(chunk * SHORT, SHORT), SHORT)
        upstream = d_second_ref[rows, :] + (
            mine_ref[rows, :].astype(F32) + theirs_ref[rows, :].astype(F32)
        )
        d_first, d_gain, d_shift = norm_back(upstream, sum_ref[rows, :], vec_ref[6:7, :])
        d_first_ref[rows, :] = d_first
        d_branch = d_first.astype(BF)
        dbranch_ref[rows, :] = d_branch
        sums_ref[0:1, :] += jnp.sum(d_branch.astype(F32), axis=0, keepdims=True)
        sums_ref[2:3, :] += d_shift
        sums_ref[4:5, :] += d_gain
        return carry

    lax.fori_loop(0, sum_ref.shape[0] // SHORT, chunk_step, 0)


def head_lanes(value, head):
    lane = lax.broadcasted_iota(jnp.int32, value.shape, 1)
    return (lane // (value.shape[1] // 2)) == head


def mask_row(kind, chunk, count):
    place = lax.broadcasted_iota(jnp.int32, (1, count), 1)
    allowed = (place // SHORT == chunk) | (kind == 1)
    return jnp.where(allowed, 0.0, MASKED_SCORE)


def attention_kernel(
    kind_ref, x_ref, wa_ref, wb_ref, bias_ref, wo_ref, partial_ref, qkv_ref, context_ref, lse_ref
):
    count = x_ref.shape[0]
    wide = wa_ref.shape[1]
    pair = 2 * HEAD_DIM
    kind = kind_ref[0]
    x = x_ref[...]
    bias = bias_ref[...]
    qkv_ref[:, :wide] = (dot(x, wa_ref[...]) + bias[:, :wide]).astype(BF)
    qkv_ref[:, wide:] = (dot(x, wb_ref[...]) + bias[:, wide:]).astype(BF)
    for p in range(HEADS // 4):
        keys = qkv_ref[:, (3 * p + 1) * pair : (3 * p + 2) * pair]
        values = qkv_ref[:, (3 * p + 2) * pair : (3 * p + 3) * pair]

        def chunk_step(chunk, carry):
            rows = pl.ds(pl.multiple_of(chunk * SHORT, SHORT), SHORT)
            queries = qkv_ref[rows, 3 * p * pair : (3 * p + 1) * pair] * jnp.asarray(0.125, BF)
            mask = mask_row(kind, chunk, count)
            found = []
            stats = lse_ref[rows, :] if p > 0 else jnp.zeros((SHORT, 128), F32)
            lane = lax.broadcasted_iota(jnp.int32, stats.shape, 1)
            for head in range(2):
                mine = jnp.where(head_lanes(queries, head), queries, jnp.zeros_like(queries))
                scores = dot_nt(mine, keys) + mask
                top = jnp.max(scores, axis=1, keepdims=True)
                powers = jnp.exp(scores - top)
                total = jnp.sum(powers, axis=1, keepdims=True)
                probs = powers * (1.0 / total)
                found.append(dot(probs.astype(BF), values))
                stats = jnp.where(lane == 2 * p + head, top + jnp.log(total), stats)
            lse_ref[rows, :] = stats
            both = jnp.where(head_lanes(found[0], 0), found[0], found[1])
            context_ref[rows, p * pair : (p + 1) * pair] = both.astype(BF)
            return carry

        lax.fori_loop(0, count // SHORT, chunk_step, 0)
    partial_ref[...] = dot(context_ref[...], wo_ref[...]).astype(BF)


def attention_backward_kernel(
    kind_ref, d_second_ref, mine_ref, theirs_ref, sum_ref, vec_ref,
    x_ref, qkv_ref, context_ref, lse_ref, wa_ref, wb_ref, wo_ref,
    ga_ref, gb_ref, gout_ref, partial_ref, sums_ref, d_first_ref, norm_sums_ref,
    dbranch_ref, dcontext_ref, dqkv_ref, dk_ref, dv_ref,
):
    back_first(
        d_second_ref, mine_ref, theirs_ref, sum_ref, vec_ref,
        d_first_ref, dbranch_ref, norm_sums_ref,
    )
    count = x_ref.shape[0]
    wide = wa_ref.shape[1]
    pair = 2 * HEAD_DIM
    kind = kind_ref[0]
    d_branch = dbranch_ref[...]
    dcontext_ref[...] = dot_nt(d_branch, wo_ref[...]).astype(BF)
    gout_ref[...] = dot_tn(context_ref[...], d_branch).astype(BF)
    for p in range(HEADS // 4):
        keys = qkv_ref[:, (3 * p + 1) * pair : (3 * p + 2) * pair]
        values = qkv_ref[:, (3 * p + 2) * pair : (3 * p + 3) * pair]
        dk_ref[...] = jnp.zeros_like(dk_ref)
        dv_ref[...] = jnp.zeros_like(dv_ref)

        def chunk_step(chunk, carry):
            rows = pl.ds(pl.multiple_of(chunk * SHORT, SHORT), SHORT)
            queries = qkv_ref[rows, 3 * p * pair : (3 * p + 1) * pair] * jnp.asarray(0.125, BF)
            d_context = dcontext_ref[rows, p * pair : (p + 1) * pair]
            mask = mask_row(kind, chunk, count)
            stats = lse_ref[rows, :]
            found = []
            for head in range(2):
                mine = jnp.where(head_lanes(queries, head), queries, jnp.zeros_like(queries))
                theirs = jnp.where(
                    head_lanes(d_context, head), d_context, jnp.zeros_like(d_context)
                )
                lse = stats[:, 2 * p + head : 2 * p + head + 1]
                probs = jnp.exp(dot_nt(mine, keys) + mask - lse)
                d_probs = dot_nt(theirs, values)
                row_dot = jnp.sum(d_probs * probs, axis=1, keepdims=True)
                d_scores = (probs * (d_probs - row_dot)).astype(BF)
                found.append(
                    (
                        dot(d_scores, keys) * 0.125,
                        dot_tn(d_scores, queries),
                        dot_tn(probs.astype(BF), d_context),
                    )
                )
            merged = [
                jnp.where(head_lanes(one, 0), one, other) for one, other in zip(*found)
            ]
            dqkv_ref[rows, 3 * p * pair : (3 * p + 1) * pair] = merged[0].astype(BF)
            dk_ref[...] += merged[1]
            dv_ref[...] += merged[2]
            return carry

        lax.fori_loop(0, count // SHORT, chunk_step, 0)
        dqkv_ref[:, (3 * p + 1) * pair : (3 * p + 2) * pair] = dk_ref[...].astype(BF)
        dqkv_ref[:, (3 * p + 2) * pair : (3 * p + 3) * pair] = dv_ref[...].astype(BF)
    d_a = dqkv_ref[:, :wide]
    d_b = dqkv_ref[:, wide:]
    x = x_ref[...]
    ga_ref[...] = dot_tn(x, d_a).astype(BF)
    gb_ref[...] = dot_tn(x, d_b).astype(BF)
    partial_ref[...] = (dot_nt(d_a, wa_ref[...]) + dot_nt(d_b, wb_ref[...])).astype(BF)
    sums_ref[:, :wide] = jnp.sum(d_a.astype(F32), axis=0, keepdims=True)
    sums_ref[:, wide:] = jnp.sum(d_b.astype(F32), axis=0, keepdims=True)


def kernel_call(body, shapes, scratch, *operands):
    in_vmem = pl.BlockSpec(memory_space=pltpu.VMEM)
    in_smem = pl.BlockSpec(memory_space=pltpu.SMEM)
    return pl.pallas_call(
        body,
        out_shape=shapes,
        in_specs=[in_smem if value.dtype == jnp.int32 else in_vmem for value in operands],
        out_specs=[in_vmem] * len(shapes),
        scratch_shapes=scratch,
        compiler_params=pltpu.CompilerParams(vmem_limit_bytes=VMEM_LIMIT),
        cost_estimate=pl.CostEstimate(flops=0, bytes_accessed=0, transcendentals=0),
    )(*operands)


def attention(row_kind, inputs_b, w_a, w_b, bias, w_out):
    count, width = inputs_b.shape
    half = w_out.shape[0]
    shapes = [
        jax.ShapeDtypeStruct((count, width), BF),
        jax.ShapeDtypeStruct((count, 3 * half), BF),
        jax.ShapeDtypeStruct((count, half), BF),
        jax.ShapeDtypeStruct((count, 128), F32),
    ]
    return kernel_call(
        attention_kernel, shapes, [], row_kind, inputs_b, w_a, w_b, bias, w_out
    )


def attention_backward(
    row_kind, d_second, mine, theirs, first_sum, vec, inputs_b, qkv, context, lse, w_a, w_b, w_out
):
    count, width = inputs_b.shape
    half = w_out.shape[0]
    shapes = [
        jax.ShapeDtypeStruct(w_a.shape, BF),
        jax.ShapeDtypeStruct(w_b.shape, BF),
        jax.ShapeDtypeStruct(w_out.shape, BF),
        jax.ShapeDtypeStruct((count, width), BF),
        jax.ShapeDtypeStruct((1, 3 * half), F32),
        jax.ShapeDtypeStruct((count, width), F32),
        jax.ShapeDtypeStruct((8, width), F32),
    ]
    scratch = [
        pltpu.VMEM((count, width), BF),
        pltpu.VMEM((count, half), BF),
        pltpu.VMEM((count, 3 * half), BF),
        pltpu.VMEM((count, 2 * HEAD_DIM), F32),
        pltpu.VMEM((count, 2 * HEAD_DIM), F32),
    ]
    return kernel_call(
        attention_backward_kernel, shapes, scratch, row_kind, d_second, mine, theirs, first_sum,
        vec, inputs_b, qkv, context, lse, w_a, w_b, w_out,
    )


def norm_rows(base, mine, theirs, vec):
    shapes = [jax.ShapeDtypeStruct(base.shape, kind) for kind in (F32, F32, BF)]
    return kernel_call(norm_kernel, shapes, [], base, mine, theirs, vec)


def hidden_layer(x, mine, theirs, vec, bias, up0, up1, down):
    count, hidden = x.shape[0], down.shape[0]
    shapes = [jax.ShapeDtypeStruct(x.shape, kind) for kind in (F32, F32, BF)]
    shapes += [jax.ShapeDtypeStruct((count, hidden), BF)] * 2
    shapes.append(jax.ShapeDtypeStruct(x.shape, BF))
    return kernel_call(
        hidden_kernel, shapes, [], x, mine, theirs, vec, bias, up0, up1, down
    )


def back_second(upstream, total, vec, act):
    shapes = [
        jax.ShapeDtypeStruct(total.shape, F32),
        jax.ShapeDtypeStruct(total.shape, BF),
        jax.ShapeDtypeStruct((act.shape[1], total.shape[1]), BF),
        jax.ShapeDtypeStruct((8, total.shape[1]), F32),
    ]
    body = functools.partial(back_second_kernel, len(upstream) > 1)
    return kernel_call(body, shapes, [], *upstream, total, vec, act)


def back_hidden(d_ffn, slope, normed_b, down, up0, up1):
    count, hidden = slope.shape
    width = normed_b.shape[1]
    shapes = [
        jax.ShapeDtypeStruct(up0.shape, BF),
        jax.ShapeDtypeStruct(up1.shape, BF),
        jax.ShapeDtypeStruct((count, width), BF),
        jax.ShapeDtypeStruct((1, hidden), F32),
    ]
    scratch = [pltpu.VMEM((count, hidden), BF)]
    return kernel_call(
        back_hidden_kernel, shapes, scratch, d_ffn, slope, normed_b, down, up0, up1
    )


def hidden_order(width, hidden_rows):
    group = width // (2 * hidden_rows)
    target = jnp.arange(width)
    source = (
        (target % (width // 2)) // hidden_rows * (2 * hidden_rows)
        + target // (width // 2) * hidden_rows
        + target % hidden_rows
    )
    del group
    return jnp.arange(width)[:, None] == source[None, :]


def shards(tokens, row_kind, w_qkv, w_out, w_up, w_down, bias_vectors, gains, bias_up, cotangent):
    chips = Chips()
    sequence = Sequence()
    core = chips.core
    count = chips.count
    device = 2 * chips.chip + core
    row_type = row_kind[0]
    rows, width = w_out.shape[1:]
    hidden = w_up.shape[2]
    hidden_rows = w_down.shape[1]
    half = width // 2
    panels = hidden // 2 // width
    own = tokens.shape[0]
    order = hidden_order(width, hidden_rows)

    pairs = HEADS // 4
    lane = half // pairs
    plan = Plan()
    state = State()

    def ordered(mine, theirs):
        return jnp.where(core == 0, mine, theirs), jnp.where(core == 0, theirs, mine)

    def pack_qkv():
        cols = w_qkv.reshape(LAYERS, rows, 3, 2, pairs, lane)

        def side(which):
            return jnp.swapaxes(pick(cols, which, 3), 2, 3).reshape(LAYERS, rows, 3 * half)

        feature = jnp.arange(width)[None, :] - rows * device == jnp.arange(rows)[:, None]
        unit = jnp.arange(hidden // 2)[None, :] - hidden_rows * chips.chip
        unit = unit == jnp.arange(hidden_rows)[:, None]
        table = jnp.concatenate([bias_vectors, gains], axis=1).reshape(LAYERS * 8, rows)
        table = dot(table, feature.astype(BF)).astype(BF)
        units = dot(bias_up, unit.astype(BF)).astype(BF)
        got = swap(side(1 - core), 1)
        table = table + swap(table, 1)
        cols = merge(side(core), got, core, 1)
        for layer in range(LAYERS):
            last = cols[layer, :, :, width:]
            vectors = [table[8 * layer : 8 * layer + 8]]
            vectors += [units[layer : layer + 1, i * width :][:, :width] for i in range(panels)]
            vectors.append(jnp.zeros((8 - panels, width), BF))
            state.gathers[ATTN, layer] = Gather(
                chips, sequence, DIRECT[layer],
                jnp.concatenate(
                    [
                        cols[layer, :, :, :width].reshape(2 * rows, width),
                        jnp.concatenate([last[0], last[1]], axis=1),
                        w_out[layer],
                        *vectors,
                    ],
                    axis=0,
                ),
            )
        sequence.mark([state.gathers[ATTN, layer].piece for layer in range(LAYERS)])

    groups = hidden // width

    def pack_up():
        value = sequence.gate(w_up).reshape(LAYERS * rows, hidden)
        stacked = jnp.concatenate(
            [value[:, i * width : (i + 1) * width] for i in range(groups)], axis=0
        )
        stacked = dot(stacked, order.astype(BF)).astype(BF)
        mine, sent = ordered(stacked[:, :half], stacked[:, half:])
        first, second = ordered(mine, swap(sent, 1))
        for layer in range(LAYERS):
            parts = []
            for i in range(panels):
                for value in (first, second):
                    cut = [
                        value[((2 * i + j) * LAYERS + layer) * rows :][:rows] for j in range(2)
                    ]
                    parts.append(jnp.concatenate(cut, axis=1))
            state.gathers[FFN, layer] = Gather(
                chips, sequence, DIRECT[LAYERS + layer],
                jnp.concatenate(parts + [w_down[layer]], axis=0),
            )
        sequence.mark([state.gathers[FFN, layer].piece for layer in range(LAYERS)])

    def read_vectors(layer, table):
        table = jnp.sum(table.astype(F32), axis=0)
        vec = table[:8]
        bias_q, bias_v = (
            jnp.where(core == 0, vec[i : i + 1, :half], vec[i : i + 1, half:]) for i in range(2)
        )
        bias = []
        for p in range(pairs):
            cut = slice(p * lane, (p + 1) * lane)
            bias += [bias_q[:, cut], jnp.zeros((1, lane), F32), bias_v[:, cut]]
        state.vec[layer] = vec
        state.bias_qkv[layer] = jnp.concatenate(bias, axis=1)
        state.bias_up[layer] = jnp.concatenate(
            [table[8 + i : 9 + i] for i in range(panels)], axis=1
        )

    def tokens_start():
        value = sequence.gate(tokens)
        sequence.mark(value)
        state.pair_tokens = (value, swap(value, 1))

    def tokens_end():
        values = sequence.gate(state.pair_tokens)
        state.x_b[0] = jnp.concatenate(ordered(*values), axis=0)
        state.x[0] = state.x_b[0].astype(F32)
        sequence.mark(state.x_b[0])

    def cotangent_start():
        value = sequence.gate(cotangent)
        sequence.mark(value)
        state.pair_cotangent = (value, swap(value, 1))

    def cotangent_end():
        values = sequence.gate(state.pair_cotangent)
        state.upstream = (jnp.concatenate(ordered(*values), axis=0),)
        sequence.mark(state.upstream)

    def out_exchange(layer):
        ends = [0, 2 * rows, 4 * rows, 4 * rows + 16]
        first, second, table = state.gathers[ATTN, layer].finish(list(zip(ends[:-1], ends[1:])))
        last, out_all = second[:, :rows], second[:, rows:]
        w_b = jnp.swapaxes(last.reshape(count, rows, 2, half), 1, 2)
        out_all = out_all.reshape(2, count // 2, rows, width)
        sent, w_b = pick(out_all, 1 - core, 0), w_b.reshape(width, half)
        read_vectors(layer, table)
        sequence.mark((sent, w_b, state.vec[layer]))
        full_out = merge(pick(out_all, core, 0), swap(sent, 1), core, 1).reshape(half, width)
        state.w_attn[layer] = (first.reshape(width, width), w_b, full_out)

    def hidden_weights(layer):
        ends = [2 * rows * i for i in range(panels + 1)]
        ends.append(ends[-1] + hidden_rows)
        *ups, down = state.gathers[FFN, layer].finish(list(zip(ends[:-1], ends[1:])))
        state.w_hidden[layer] = (
            down.reshape(hidden // 2, width), *(value.reshape(width, width) for value in ups)
        )

    def run_attention(layer):
        x_b, weights = sequence.gate((state.x_b[layer], state.w_attn[layer]))
        w_a, w_b, full_out = weights
        partial, *saved = attention(row_kind, x_b, w_a, w_b, state.bias_qkv[layer], full_out)
        sequence.mark(partial)
        state.w_attn[layer] = weights
        state.saved[layer] = (x_b, *saved)
        state.branch = (partial, swap(partial, 1))

    def run_hidden(layer):
        mine, theirs = sequence.gate(state.branch)
        down, up0, up1 = state.w_hidden[layer]
        first_sum, state.normed, *kept, partial = hidden_layer(
            state.x[layer], mine, theirs, state.vec[layer], state.bias_up[layer], up0, up1, down
        )
        sequence.mark(partial)
        state.first_sum[layer] = first_sum
        state.kept[layer] = kept
        state.branch = (partial, swap(partial, 1))

    def run_norm(layer):
        mine, theirs = sequence.gate(state.branch)
        second, x, x_b = norm_rows(state.normed, mine, theirs, state.vec[layer])
        state.second[layer], state.x[layer + 1], state.x_b[layer + 1] = second, x, x_b
        sequence.mark(second)

    def run_back_second(layer):
        upstream = sequence.gate(state.upstream)
        if layer < LAYERS - 1:
            upstream = (state.d_first, *upstream)
        act = state.kept[layer][1]
        d_second, d_ffn, g_down, sums = back_second(
            upstream, state.second[layer], state.vec[layer], act
        )
        state.d_second, state.d_ffn = d_second, d_ffn
        state.sums2[layer] = sums
        bundle = state.scatters[FFN, layer]
        bundle.start(0, [g_down.reshape(count, hidden_rows, width)])
        sequence.mark((d_ffn, bundle.sent))

    def run_back_hidden(layer):
        d_ffn = sequence.gate(state.d_ffn)
        normed_b, _, slope = state.kept[layer]
        *g_up, partial, units = back_hidden(d_ffn, slope, normed_b, *state.w_hidden[layer])
        bundle = state.scatters[FFN, layer]
        bundle.start(1, [value.reshape(count, 2 * rows, width) for value in g_up])
        sequence.mark((partial, bundle.sent))
        state.units[layer] = units
        state.branch = (partial, swap(partial, 1))

    def run_back_attention(layer):
        mine, theirs = sequence.gate(state.branch)
        x_b, qkv, context, lse = state.saved[layer]
        g_a, g_b, g_out, partial, sums, state.d_first, state.sums1[layer] = attention_backward(
            row_kind, state.d_second, mine, theirs, state.first_sum[layer], state.vec[layer],
            x_b, qkv, context, lse, *state.w_attn[layer],
        )
        sequence.mark(partial)
        state.pair[layer] = jnp.concatenate(
            [
                jnp.concatenate(
                    [sums[:, (3 * p + t) * lane :][:, :lane] for p in range(pairs)], axis=1
                )
                for t in (0, 2)
            ],
            axis=0,
        )
        if layer > 0:
            state.upstream = (partial, swap(partial, 1))
        else:
            mine, sent = ordered(partial[:own], partial[own:])
            state.upstream = (mine, swap(sent, 1))
        state.g_attn[layer] = (g_a, g_b, g_out)

    def sum_rows(layer):
        pair = state.pair[layer]
        nothing = jnp.zeros_like(pair)
        pair = jnp.concatenate(ordered(pair, nothing), axis=1)
        units = [state.units[layer][:, i * width :][:, :width] for i in range(panels)]
        small = jnp.concatenate([state.sums1[layer] + state.sums2[layer], pair, *units], axis=0)
        small = jnp.pad(small.astype(BF), ((0, 16 - small.shape[0]), (0, 0)))
        line = jnp.arange(16)[:, None]
        place = jnp.arange(width)[None, :]
        owner = jnp.where(
            line < 10, place // (2 * rows), ((line - 10) * width + place) // hidden_rows
        )
        mine = owner[None] == jnp.arange(count)[:, None, None]
        return jnp.where(mine, small[None], jnp.zeros((), BF))

    def back_terms(layer):
        g_a, g_b, g_out = sequence.gate(state.g_attn[layer])
        bundle = state.scatters[ATTN, layer]
        out_pair = g_out.reshape(count // 2, 2, rows, width)
        out_got = swap(pick(out_pair, 1 - core, 1), 1)
        out = merge(pick(out_pair, core, 1), out_got, core, 0).reshape(count, rows, width)
        g_b = g_b.reshape(count, 2, rows, half)
        last = jnp.concatenate([g_b[:, 0], g_b[:, 1]], axis=2)
        rest = jnp.concatenate([last, out, sum_rows(layer)], axis=1)
        rest = lax.optimization_barrier(rest)
        bundle.start(0, [g_a.reshape(count, 2 * rows, width), rest])
        sequence.mark(bundle.sent)

    def grad_end():
        mine, theirs = sequence.gate(state.upstream)
        d_first = lax.dynamic_slice_in_dim(state.d_first, core * own, own)
        state.grad_tokens = d_first + (mine.astype(F32) + theirs.astype(F32))
        sequence.mark(state.grad_tokens)

    def mixed_end():
        value = sequence.gate(state.x_b[LAYERS])
        state.mixed = lax.dynamic_slice_in_dim(value, core * own, own)
        sequence.mark(state.mixed)

    def finish_hidden(layer):
        down, *ups = state.scatters[FFN, layer].finish()
        sides = [
            jnp.concatenate([up[side * rows :][:rows] for up in ups], axis=1)
            for side in range(2)
        ]
        mine, sent = ordered(*sides)
        state.up_pair[layer] = (mine, swap(sent, 1))
        state.down[layer] = down

    def end_hidden(layer):
        first, second = ordered(*sequence.gate(state.up_pair[layer]))
        stacked = jnp.concatenate(
            [
                jnp.concatenate(
                    [value[:, i * half : (i + 1) * half] for value in (first, second)], axis=1
                )
                for i in range(groups)
            ],
            axis=0,
        )
        stacked = lax.dot_general(
            stacked, order.astype(F32), (((1,), (1,)), ((), ())),
            precision=lax.Precision.HIGHEST, preferred_element_type=F32,
        )
        state.up[layer] = jnp.concatenate(
            [stacked[i * rows : (i + 1) * rows] for i in range(groups)], axis=1
        )
        sequence.mark(state.up[layer])

    def finish_attention(layer):
        first, rest = state.scatters[ATTN, layer].finish()
        last, out, small = rest[:rows], rest[rows : 2 * rows], rest[2 * rows :]
        sides = [
            jnp.concatenate(
                [first[side * rows :][:rows], last[:, side * half :][:, :half]], axis=1
            )
            for side in range(2)
        ]
        mine, sent = ordered(*sides)
        pair = jnp.pad(small[8:], ((0, 0), (0, mine.shape[1] - width)))
        sent = jnp.concatenate([sent, pair], axis=0)
        state.qkv_pair[layer] = (mine, swap(sent, 1))
        state.out[layer] = out
        state.small_rows[layer] = small

    def end_attention(layer):
        mine, theirs = sequence.gate(state.qkv_pair[layer])
        small = state.small_rows[layer]
        small = jnp.concatenate([theirs[rows : rows + 2, :width] + small[8:10], small], axis=0)
        features = lax.dynamic_slice_in_dim(small, rows * device, rows, axis=1)
        per_row = width // hidden_rows
        units = lax.dynamic_slice(
            small,
            (12 + chips.chip // per_row, hidden_rows * (chips.chip % per_row)),
            (1, hidden_rows),
        )
        state.vectors[layer] = features[:6]
        state.gains[layer] = features[6:8]
        state.unit_sums[layer] = units[0]
        values = ordered(mine, theirs[:rows])
        state.qkv[layer] = jnp.concatenate(
            [
                value[:, (3 * p + t) * lane :][:, :lane]
                for t in range(3)
                for value in values
                for p in range(pairs)
            ],
            axis=1,
        )
        sequence.mark(state.qkv[layer])

    def call(function, *args):
        return lambda: function(*args)

    low = len(chips.low)
    size = (1.0, 2.0)
    add = plan.add

    def pair_send(label):
        return [(label, (("p", 0.0),), 1)]

    def plane(length):
        return (("x", length), ("y", length))

    add("pq", 0, 6.0, [], pack_qkv)
    add("pu", 2, 3.0, [("g", ATTN, 0)], pack_up)
    add("tok", 8, 0.5, ["pu"], tokens_start, pair_send("x0"))
    add("te", 7, 1.5, ["x0"], tokens_end)
    add("cot", 9, 0.5, [("m", 1, 0)], cotangent_start, pair_send("ct"))
    add("ce", 9, 1.2, ["ct"], cotangent_end)
    bundles = [(ATTN, 0), (FFN, 0), (ATTN, 1), (FFN, 1)]
    for rank, (kind, layer) in enumerate(bundles):
        needs = ["pq" if kind == ATTN else "pu"]

        def start(kind=kind, layer=layer):
            state.gathers[kind, layer].start()

        def advance(kind=kind, layer=layer):
            state.gathers[kind, layer].advance()

        units = 7.0 / 3 if kind == ATTN else 4.0
        z = UNIT * 2 * units
        if DIRECT[LAYERS * kind + layer]:
            need = ("z", kind, layer)
            links = (("z", 1.5 * z), ("w", 2 * z))
            add(("g", kind, layer), 1 + rank, 5.0, needs, start, [(need, links, 3)])
        else:
            need = ("y", kind, layer)
            links = (("z", 0.5 * z), ("w", z + 1.5))
            add(("g", kind, layer), 1 + rank, 3.5, needs, start, [(need, links, 1)])
            sent = ("z", kind, layer)
            add(("h", kind, layer), 1 + rank, 2.2, [need], advance, [(sent, (("z", z),), 1)])
            need = sent
        length = UNIT * 2 * units
        for step in range(low):
            sent = ("xy", kind, layer, step)
            add(
                ("gs", kind, layer, step), 1 + rank, 2.5 + 0.3 * kind, [need], advance,
                [(sent, plane(length), 1)],
            )
            need = sent
            length *= 2
        if kind == ATTN:
            add(
                ("go", layer), 1 + rank, 4.5, [need], call(out_exchange, layer),
                pair_send(("w", kind, layer)),
            )
        else:
            add(("w", kind, layer), 1 + rank, 1.6, [need], call(hidden_weights, layer))
    need = "te"
    for layer in range(LAYERS):
        add(
            ("m", 0, layer), 10, 12.7, [need, ("w", ATTN, layer)],
            call(run_attention, layer), pair_send(("p", 0, layer)),
        )
        add(
            ("m", 1, layer), 10, 6.0, [("p", 0, layer), ("w", FFN, layer)],
            call(run_hidden, layer), pair_send(("p", 1, layer)),
        )
        need = ("m", 2, layer)
        add(need, 10, 3.0, [("p", 1, layer)], call(run_norm, layer))
    add("mix", 20, 1.0, [need], mixed_end)

    needs = [need, "ce"]
    for layer in reversed(range(LAYERS)):
        state.scatters[FFN, layer] = Scatter(chips, sequence, 2)
        state.scatters[ATTN, layer] = Scatter(chips, sequence, 1)
        add(
            ("b", 0, layer), 10, 5.0, needs, call(run_back_second, layer),
            [(("r", FFN, layer, 0), plane(UNIT * 8), 1)],
        )
        add(
            ("b", 1, layer), 10, 6.5, [("b", 0, layer)], call(run_back_hidden, layer),
            [(("r", FFN, layer, 1), plane(UNIT * 8), 1)] + pair_send(("p", 2, layer)),
        )
        add(
            ("b", 2, layer), 10, 17.2, [("p", 2, layer)], call(run_back_attention, layer),
            pair_send(("p", 3, layer)),
        )
        add(
            ("b", 3, layer), 9.5, 6.0, [("b", 2, layer)], call(back_terms, layer),
            [(("r", ATTN, layer, 0), plane(UNIT * 28 / 3), 1)],
        )
        needs = [("p", 3, layer)]
        for kind in (FFN, ATTN):
            need = [("r", kind, layer, part) for part in range(1 + kind)]
            rank = 1 + 2 * (LAYERS - 1 - layer) + (kind == ATTN)

            def reduce(kind=kind, layer=layer):
                state.scatters[kind, layer].advance()

            units = 7.0 / 3 if kind == ATTN else 4.0
            length = UNIT * 2 * units
            for step in range(low - 1):
                sent = ("r", kind, layer, 2 + step)
                add(
                    ("rs", kind, layer, step), rank, 2.8 + 0.4 * kind, need, reduce,
                    [(sent, plane(length), 1)],
                )
                need = [sent]
                length /= 2
            z = UNIT * 2 * units
            sent = ("rz", kind, layer)
            add(("rs", kind, layer, low), rank, 2.2, need, reduce, [(sent, (("z", z),), 1)])
            need = sent
            links = (("z", 0.5 * z), ("w", z + 1.5))
            sent = ("ry", kind, layer)
            add(("rs", kind, layer, low + 1), rank, 3.5, [need], reduce, [(sent, links, 1)])
            last = finish_hidden if kind == FFN else finish_attention
            add(
                ("rf", kind, layer), 19, 2.0, [sent], call(last, layer),
                pair_send(("re", kind, layer)),
            )
            last = end_hidden if kind == FFN else end_attention
            add(("ro", kind, layer), 20, 2.5, [("re", kind, layer)], call(last, layer))
    add("grad", 18, 1.2, needs, grad_end)
    plan.run()

    def stacked(values):
        return jnp.stack([values[layer] for layer in range(LAYERS)])

    return (
        state.mixed,
        state.grad_tokens,
        stacked(state.qkv),
        stacked(state.out),
        stacked(state.up),
        stacked(state.down),
        stacked(state.vectors),
        stacked(state.gains),
        stacked(state.unit_sums),
    )


def solution(mesh):
    placed = (
        P("fsdp", None),
        P("fsdp"),
        P(None, "fsdp", None),
        P(None, "fsdp", None),
        P(None, "fsdp", None),
        P(None, "fsdp", None),
        P(None, None, "fsdp"),
        P(None, None, "fsdp"),
        P(None, "fsdp"),
        P("fsdp", None),
    )
    return jax.shard_map(
        shards,
        mesh=mesh,
        in_specs=placed,
        out_specs=(
            P("fsdp", None),
            P("fsdp", None),
            P(None, "fsdp", None),
            P(None, "fsdp", None),
            P(None, "fsdp", None),
            P(None, "fsdp", None),
            P(None, None, "fsdp"),
            P(None, None, "fsdp"),
            P(None, "fsdp"),
        ),
        check_vma=False,
    )
```

profile of v0, /device:TPU:1, one launch (start us, length us, event | category | flops | bytes accessed | tf_op | source)
XLA Modules:
  0.0 363.2 jit_solution(16043331747342457390)
XLA Ops:
  5.2 3.5 collective-permute-start.2
  11.9 4.8 %collective-permute-done.2 = bf16[112,768]{1,0:T(8,128)(2,1)S(1)} collective-permute-done((bf16[112,768]{1,0:T(8,128)(2,1)S(1)}, bf16[112,768]{1,0:T(8,128)(2,1)S(1)}, u32[]{:S(2)}, u32[]{:S(2)}) %collective-permute-start.2) | collective-permute-done | bytes 172064 | tf_op jit(solution)/shard_map/ppermute | solution.py:47
  18.3 3.1 collective-permute-start.5
  21.4 7.5 %collective-permute-done.5 = bf16[112,768]{1,0:T(8,128)(2,1)S(1)} collective-permute-done((bf16[112,768]{1,0:T(8,128)(2,1)S(1)}, bf16[112,768]{1,0:T(8,128)(2,1)S(1)}, u32[]{:S(2)}, u32[]{:S(2)}) %collective-permute-start.5) | collective-permute-done | bytes 172064 | tf_op jit(solution)/shard_map/ppermute | solution.py:47
  31.4 4.2 %collective-permute-start.8 = (bf16[2,112,768]{2,1,0:T(8,128)(2,1)S(1)}, bf16[2,112,768]{2,1,0:T(8,128)(2,1)S(1)}, u32[]{:S(2)}, u32[]{:S(2)}) collective-permute-start(bf16[2,112,768]{2,1,0:T(8,128)(2,1)S(1)} %bitcast.337), channel_id=1, source_target_pairs={{0,8},{1,9},{2,10},{3,11},{4,12},{5,13},{6,14},{7,15},{8,0},{9,1},... | collective-permute-start | bytes 1032200 | tf_op jit(solution)/shard_map/ppermute | solution.py:47
  36.1 11.9 %collective-permute-done.8 = bf16[2,112,768]{2,1,0:T(8,128)(2,1)S(1)} collective-permute-done((bf16[2,112,768]{2,1,0:T(8,128)(2,1)S(1)}, bf16[2,112,768]{2,1,0:T(8,128)(2,1)S(1)}, u32[]{:S(2)}, u32[]{:S(2)}) %collective-permute-start.8) | collective-permute-done | bytes 344096 | tf_op jit(solution)/shard_map/ppermute | solution.py:47
  52.1 1.7 shard_map.174.mine_ref
  53.8 2.3 collective-permute-start.15
  56.4 1.3 collective-permute-start.6
  58.8 1.7 shard_map.175.mine_ref
  60.5 2.3 collective-permute-start.12
  63.7 10.3 %collective-permute-done.9 = bf16[2,192,768]{2,1,0:T(8,128)(2,1)S(1)} collective-permute-done((bf16[2,192,768]{2,1,0:T(8,128)(2,1)S(1)}, bf16[2,192,768]{2,1,0:T(8,128)(2,1)S(1)}, u32[]{:S(2)}, u32[]{:S(2)}) %collective-permute-start.9) | collective-permute-done | bytes 589856 | tf_op jit(solution)/shard_map/ppermute | solution.py:47
  74.0 1.6 shard_map.176
  75.6 1.2 broadcast_select_fusion.5
  78.0 2.1 collective-permute-start.14
  80.2 1.9 shard_map.178
  84.3 2.9 reshape.421
  87.3 2.1 copy.52
  91.8 3.2 collective-permute-start.22
  95.0 1.7 shard_map.179
  97.2 1.9 shard_map.180
  105.2 1.9 shard_map.181.mine_ref
  107.2 3.0 collective-permute-start.20
  111.2 9.1 %collective-permute-done.17.theirs_ref = bf16[4,1,192,768]{3,2,1,0:T(8,128)(2,1)} collective-permute-done((bf16[4,1,192,768]{3,2,1,0:T(8,128)(2,1)}, bf16[4,1,192,768]{3,2,1,0:T(8,128)(2,1)}, u32[]{:S(2)}, u32[]{:S(2)}) %collective-permute-start.17) | collective-permute-done | bytes 1179680 | tf_op jit(solution)/shard_map/ppermute | solution.py:79
  120.3 1.8 shard_map.182.mine_ref
  122.1 12.0 %shard_map.183 = (bf16[512,768]{1,0:T(8,128)(2,1)S(1)}, bf16[512,1152]{1,0:T(8,128)(2,1)S(1)}, bf16[512,384]{1,0:T(8,128)(2,1)S(1)}, f32[512,128]{1,0:T(8,128)S(1)}) custom-call(s32[1]{0:T(128)S(6)} %copy.129.kind_ref, bf16[512,768]{1,0:T(8,128)(2,1)S(1)} %get-tuple-element.213.x_ref, bf16[768,768]{1,0:T(8,128)(2,1)S(1)} %bitcast.317, ...), custom_call_target="tpu_custom_call" | custom-call | tf_op jit(solution)/shard_map/pallas_call | solution.py:628
  139.0 2.2 collective-permute-done.20.theirs_ref
  142.1 4.5 %shard_map.185 = (f32[512,768]{1,0:T(8,128)S(1)}, f32[512,768]{1,0:T(8,128)S(1)}, bf16[512,768]{1,0:T(8,128)(2,1)S(1)}, bf16[512,1536]{1,0:T(8,128)(2,1)S(1)}, b...) custom-call(f32[512,768]{1,0:T(8,128)S(1)} %get-tuple-element.477.x_ref, ...), custom_call_target="tpu_custom_call" | custom-call | tf_op jit(solution)/shard_map/pallas_call | solution.py:628
  146.6 1.2 copy-done.34
  148.8 1.3 fusion.51
  152.4 12.2 %shard_map.187 = (bf16[512,768]{1,0:T(8,128)(2,1)S(1)}, bf16[512,1152]{1,0:T(8,128)(2,1)S(1)}, bf16[512,384]{1,0:T(8,128)(2,1)S(1)}, f32[512,128]{1,0:T(8,128)S(1)}) custom-call(s32[1]{0:T(128)S(6)} %copy.129.kind_ref, bf16[512,768]{1,0:T(8,128)(2,1)S(1)} %get-tuple-element.233.x_ref, bf16[768,768]{1,0:T(8,128)(2,1)S(1)} %bitcast.319, ...), custom_call_target="tpu_custom_call" | custom-call | tf_op jit(solution)/shard_map/pallas_call | solution.py:628
  167.0 4.5 %shard_map.189 = (f32[512,768]{1,0:T(8,128)S(1)}, f32[512,768]{1,0:T(8,128)S(1)}, bf16[512,768]{1,0:T(8,128)(2,1)S(1)}, bf16[512,1536]{1,0:T(8,128)(2,1)S(1)}, b...) custom-call(f32[512,768]{1,0:T(8,128)S(1)} %get-tuple-element.229.x_ref, ...), custom_call_target="tpu_custom_call" | custom-call | tf_op jit(solution)/shard_map/pallas_call | solution.py:628
  173.9 2.3 shard_map.190
  177.0 2.9 shard_map.191
  180.6 3.9 %shard_map.193 = (bf16[768,768]{1,0:T(8,128)(2,1)S(1)}, bf16[768,768]{1,0:T(8,128)(2,1)S(1)}, bf16[512,768]{1,0:T(8,128)(2,1)S(1)}, f32[1,1536]{1,0:T(1,128)S(1)}) custom-call(bf16[512,768]{1,0:T(8,128)(2,1)S(1)} %get-tuple-element.257.d_ffn_ref, bf16[512,1536]{1,0:T(8,128)(2,1)S(1)} %get-tuple-element.258.slope_ref, ...), custom_call_target="tpu_custom_call" | custom-call | tf_op jit(solution)/shard_map/pallas_call | solution.py:628
  185.1 1.3 collective-permute-start.29
  187.4 17.7 %shard_map.195 = (bf16[768,768]{1,0:T(8,128)(2,1)S(1)}, bf16[768,384]{1,0:T(8,128)(2,1)S(1)}, bf16[384,768]{1,0:T(8,128)(2,1)S(1)}, bf16[512,768]{1,0:T(8,128)(2...) custom-call(s32[1]{0:T(128)S(6)} %copy.129.kind_ref, ...), custom_call_target="tpu_custom_call" | custom-call | tf_op jit(solution)/shard_map/pallas_call | solution.py:628
  206.0 7.1 %collective-permute-done.30.refs_4_ = bf16[4,2,96,768]{3,2,1,0:T(8,128)(2,1)S(1)} collective-permute-done((bf16[4,2,96,768]{3,2,1,0:T(8,128)(2,1)S(1)}, bf16[4,2,96,768]{3,2,1,0:T(8,128)(2,1)S(1)}, u32[]{:S(2)}, u32[]{:S(2)}) %collective-permute-start.30) | collective-permute-done | bytes 1179680 | tf_op jit(solution)/shard_map/ppermute | solution.py:79
  213.1 2.1 shard_map.196
  217.9 1.7 shard_map.197
  219.6 1.2 collective-permute-start.35
  220.8 1.4 copy-done.27
  222.3 1.4 copy-done.29
  223.7 1.4 copy-done.31
  225.8 4.6 %shard_map.198 = (f32[512,768]{1,0:T(8,128)S(1)}, bf16[512,768]{1,0:T(8,128)(2,1)S(1)}, bf16[1536,768]{1,0:T(8,128)(2,1)S(1)}, f32[8,768]{1,0:T(8,128)S(1)}) custom-call(f32[512,768]{1,0:T(8,128)S(1)} %copy-done.31, bf16[512,768]{1,0:T(8,128)(2,1)} %get-tuple-element.284.refs_1_, bf16[512,768]{1,0:T(8,128)(2,1)} %collective-permute-done.28.refs_2_, ...), custom_call_target="tpu_custom_call" | custom-call | tf_op jit(solution)/shard_map/pallas_call | solution.py:628
  235.2 4.8 %shard_map.200 = (bf16[768,768]{1,0:T(8,128)(2,1)S(1)}, bf16[768,768]{1,0:T(8,128)(2,1)S(1)}, bf16[512,768]{1,0:T(8,128)(2,1)}, f32[1,1536]{1,0:T(1,128)S(1)}) custom-call(bf16[512,768]{1,0:T(8,128)(2,1)S(1)} %get-tuple-element.291.d_ffn_ref, bf16[512,1536]{1,0:T(8,128)(2,1)S(1)} %copy-done.35, bf16[512,768]{1,0:T(8,128)(2,1)S(1)} %copy-done.42, ...), custom_call_target="tpu_custom_call" | custom-call | tf_op jit(solution)/shard_map/pallas_call | solution.py:628
  243.0 1.3 copy-done.12
  244.2 1.3 copy-done.15
  247.2 1.6 shard_map.202
  250.5 1.3 copy-done.39
  252.8 18.2 %shard_map.203 = (bf16[768,768]{1,0:T(8,128)(2,1)S(1)}, bf16[768,384]{1,0:T(8,128)(2,1)S(1)}, bf16[384,768]{1,0:T(8,128)(2,1)S(1)}, bf16[512,768]{1,0:T(8,128)(2...) custom-call(s32[1]{0:T(128)S(6)} %copy.129.kind_ref, f32[512,768]{1,0:T(8,128)S(1)} %copy-done.37, ...), custom_call_target="tpu_custom_call" | custom-call | tf_op jit(solution)/shard_map/pallas_call | solution.py:628
  272.9 1.8 shard_map.205
  275.4 1.8 collective-permute-done.39.refs_4_
  279.4 6.1 %collective-permute-done.37 = bf16[4,1,112,768]{3,2,1,0:T(8,128)(2,1)S(1)} collective-permute-done((bf16[4,1,112,768]{3,2,1,0:T(8,128)(2,1)S(1)}, bf16[4,1,112,768]{3,2,1,0:T(8,128)(2,1)S(1)}, u32[]{:S(2)}, u32[]{:S(2)}) %collective-permute-start.37) | collective-permute-done | bytes 688160 | tf_op jit(solution)/shard_map/ppermute | solution.py:79
  287.0 3.3 collective-permute-start.52
  291.8 13.6 %collective-permute-done.42 = bf16[2,1,112,768]{3,2,0,1:T(8,128)(2,1)S(1)} collective-permute-done((bf16[2,1,112,768]{3,2,0,1:T(8,128)(2,1)S(1)}, bf16[2,1,112,768]{3,2,0,1:T(8,128)(2,1)S(1)}, u32[]{:S(2)}, u32[]{:S(2)}) %collective-permute-start.42) | collective-permute-done | bytes 344096 | tf_op jit(solution)/shard_map/ppermute | solution.py:47
  307.2 1.6 collective-permute-start.46
  311.1 1.3 fusion.1
  314.6 10.3 %collective-permute-done.46 = bf16[2,1,192,768]{3,2,0,1:T(8,128)(2,1)S(1)} collective-permute-done((bf16[2,1,192,768]{3,2,0,1:T(8,128)(2,1)S(1)}, bf16[2,1,192,768]{3,2,0,1:T(8,128)(2,1)S(1)}, u32[]{:S(2)}, u32[]{:S(2)}) %collective-permute-start.46) | collective-permute-done | bytes 589856 | tf_op jit(solution)/shard_map/ppermute | solution.py:47
  326.6 2.0 collective-permute-start.49
  330.6 2.2 collective-permute-start.47
  332.9 13.9 %collective-permute-done.47 = bf16[2,1,112,768]{3,2,0,1:T(8,128)(2,1)S(1)} collective-permute-done((bf16[2,1,112,768]{3,2,0,1:T(8,128)(2,1)S(1)}, bf16[2,1,112,768]{3,2,0,1:T(8,128)(2,1)S(1)}, u32[]{:S(2)}, u32[]{:S(2)}) %collective-permute-start.47) | collective-permute-done | bytes 344096 | tf_op jit(solution)/shard_map/ppermute | solution.py:47
  349.7 1.3 fusion
  351.9 5.4 %collective-permute-done.48 = bf16[1,1,112,768]{3,2,1,0:T(8,128)(2,1)S(1)} collective-permute-done((bf16[1,1,112,768]{3,2,1,0:T(8,128)(2,1)S(1)}, bf16[1,1,112,768]{3,2,1,0:T(8,128)(2,1)S(1)}, u32[]{:S(2)}, u32[]{:S(2)}) %collective-permute-start.48) | collective-permute-done | bytes 172064 | tf_op jit(solution)/shard_map/ppermute | solution.py:47
  (465 shorter events, 88.8 us)
Async XLA Ops:
  2.1 1.6 collective-permute-start
  2.4 1.3 collective-permute-start.1
  4.7 4.0 %collective-permute-start.3 = (bf16[192,384]{1,0:T(8,128)(2,1)S(1)}, bf16[192,384]{1,0:T(8,128)(2,1)S(1)}, u32[]{:S(2)}, u32[]{:S(2)}) collective-permute-start(bf16[192,384]{1,0:T(8,128)(2,1)S(1)} %broadcast_select_fusion.8), channel_id=1, source_target_pairs={{0,1},{1,0},{2,3},{3,2},{4,5},{5,4},{6,7},{7,6},{8,9},{9,8},{10,11... | collective-permute-start | bytes 442376 | tf_op jit(solution)/shard_map/ppermute | solution.py:47
  5.2 11.6 %collective-permute-start.2 = (bf16[112,768]{1,0:T(8,128)(2,1)S(1)}, bf16[112,768]{1,0:T(8,128)(2,1)S(1)}, u32[]{:S(2)}, u32[]{:S(2)}) collective-permute-start(bf16[112,768]{1,0:T(8,128)(2,1)S(1)} %concatenate.236), channel_id=1, source_target_pairs={{0,16},{1,17},{2,18},{3,19},{4,20},{5,21},{6,22},{7,23},{8,24},{9,... | collective-permute-start | bytes 516104 | tf_op jit(solution)/shard_map/ppermute | solution.py:47
  11.9 36.7 %copy-start.50 = (bf16[192,768]{1,0:T(8,128)(2,1)}, bf16[192,768]{1,0:T(8,128)(2,1)S(1)}, u32[]{:S(2)}) copy-start(bf16[192,768]{1,0:T(8,128)(2,1)S(1)} %get-tuple-element.189) | copy-start | bytes 884740
  17.4 12.5 %collective-permute-start.4 = (bf16[2,112,768]{2,1,0:T(8,128)(2,1)S(1)}, bf16[2,112,768]{2,1,0:T(8,128)(2,1)S(1)}, u32[]{:S(2)}, u32[]{:S(2)}) collective-permute-start(bf16[2,112,768]{2,1,0:T(8,128)(2,1)S(1)} %bitcast.339), channel_id=1, source_target_pairs={{0,8},{1,9},{2,10},{3,11},{4,12},{5,13},{6,14},{7,15},{8,0},{9,1},... | collective-permute-start | bytes 1032200 | tf_op jit(solution)/shard_map/ppermute | solution.py:47
  18.3 10.6 %collective-permute-start.5 = (bf16[112,768]{1,0:T(8,128)(2,1)S(1)}, bf16[112,768]{1,0:T(8,128)(2,1)S(1)}, u32[]{:S(2)}, u32[]{:S(2)}) collective-permute-start(bf16[112,768]{1,0:T(8,128)(2,1)S(1)} %concatenate.238), channel_id=1, source_target_pairs={{0,16},{1,17},{2,18},{3,19},{4,20},{5,21},{6,22},{7,23},{8,24},{9,... | collective-permute-start | bytes 516104 | tf_op jit(solution)/shard_map/ppermute | solution.py:47
  30.4 21.6 %collective-permute-start.11 = (bf16[4,1,112,768]{3,2,1,0:T(8,128)(2,1)S(1)}, bf16[4,1,112,768]{3,2,1,0:T(8,128)(2,1)S(1)}, u32[]{:S(2)}, u32[]{:S(2)}) collective-permute-start(bf16[4,1,112,768]{3,2,1,0:T(8,128)(2,1)S(1)} %bitcast.325), channel_id=1, source_target_pairs={{0,2},{1,5},{2,0},{3,7},{4,6},{5,1},{6,4},{7,3},{8,10},{9,13},{10,... | collective-permute-start | bytes 2064392 | tf_op jit(solution)/shard_map/ppermute | solution.py:79
  31.4 16.6 %collective-permute-start.8 = (bf16[2,112,768]{2,1,0:T(8,128)(2,1)S(1)}, bf16[2,112,768]{2,1,0:T(8,128)(2,1)S(1)}, u32[]{:S(2)}, u32[]{:S(2)}) collective-permute-start(bf16[2,112,768]{2,1,0:T(8,128)(2,1)S(1)} %bitcast.337), channel_id=1, source_target_pairs={{0,8},{1,9},{2,10},{3,11},{4,12},{5,13},{6,14},{7,15},{8,0},{9,1},... | collective-permute-start | bytes 1032200 | tf_op jit(solution)/shard_map/ppermute | solution.py:47
  35.5 13.3 %collective-permute-start.7 = (bf16[192,768]{1,0:T(8,128)(2,1)S(1)}, bf16[192,768]{1,0:T(8,128)(2,1)S(1)}, u32[]{:S(2)}, u32[]{:S(2)}) collective-permute-start(bf16[192,768]{1,0:T(8,128)(2,1)S(1)} %get-tuple-element.189), channel_id=1, source_target_pairs={{0,16},{1,17},{2,18},{3,19},{4,20},{5,21},{6,22},{7,23},{8,24},{9,... | collective-permute-start | bytes 884744 | tf_op jit(solution)/shard_map/ppermute | solution.py:47
  48.6 10.1 %collective-permute-start.10 = (bf16[4,1,112,768]{3,2,1,0:T(8,128)(2,1)S(1)}, bf16[4,1,112,768]{3,2,1,0:T(8,128)(2,1)S(1)}, u32[]{:S(2)}, u32[]{:S(2)}) collective-permute-start(bf16[4,1,112,768]{3,2,1,0:T(8,128)(2,1)S(1)} %bitcast.327), channel_id=1, source_target_pairs={{0,2},{1,5},{2,0},{3,7},{4,6},{5,1},{6,4},{7,3},{8,10},{9,13},{10,... | collective-permute-start | bytes 2064392 | tf_op jit(solution)/shard_map/ppermute | solution.py:79
  53.8 26.4 %collective-permute-start.15 = (bf16[4,2,112,768]{3,2,1,0:T(8,128)(2,1)}, bf16[4,2,112,768]{3,2,1,0:T(8,128)(2,1)}, u32[]{:S(2)}, u32[]{:S(2)}) collective-permute-start(bf16[4,2,112,768]{3,2,1,0:T(8,128)(2,1)} %shard_map.174.mine_ref), channel_id=1, source_target_pairs={{0,4},{1,3},{2,6},{3,1},{4,0},{5,7},{6,2},{7,5},{8,12},{9,11},{10,... | collective-permute-start | bytes 4128776 | tf_op jit(solution)/shard_map/ppermute | solution.py:79
  56.1 17.9 %collective-permute-start.9 = (bf16[2,192,768]{2,1,0:T(8,128)(2,1)S(1)}, bf16[2,192,768]{2,1,0:T(8,128)(2,1)S(1)}, u32[]{:S(2)}, u32[]{:S(2)}) collective-permute-start(bf16[2,192,768]{2,1,0:T(8,128)(2,1)S(1)} %bitcast.329), channel_id=1, source_target_pairs={{0,8},{1,9},{2,10},{3,11},{4,12},{5,13},{6,14},{7,15},{8,0},{9,1},... | collective-permute-start | bytes 1769480 | tf_op jit(solution)/shard_map/ppermute | solution.py:47
  56.4 19.3 %collective-permute-start.6 = (bf16[256,768]{1,0:T(8,128)(2,1)}, bf16[256,768]{1,0:T(8,128)(2,1)}, u32[]{:S(2)}, u32[]{:S(2)}) collective-permute-start(bf16[256,768]{1,0:T(8,128)(2,1)} %param.10), channel_id=1, source_target_pairs={{0,1},{1,0},{2,3},{3,2},{4,5},{5,4},{6,7},{7,6},{8,9},{9,8},{10,11... | collective-permute-start | bytes 1179656 | tf_op jit(solution)/shard_map/ppermute | solution.py:47
  60.5 36.7 %collective-permute-start.12 = (bf16[4,2,112,768]{3,2,1,0:T(8,128)(2,1)}, bf16[4,2,112,768]{3,2,1,0:T(8,128)(2,1)}, u32[]{:S(2)}, u32[]{:S(2)}) collective-permute-start(bf16[4,2,112,768]{3,2,1,0:T(8,128)(2,1)} %shard_map.175.mine_ref), channel_id=1, source_target_pairs={{0,4},{1,3},{2,6},{3,1},{4,0},{5,7},{6,2},{7,5},{8,12},{9,11},{10,... | collective-permute-start | bytes 4128776 | tf_op jit(solution)/shard_map/ppermute | solution.py:79
  63.5 13.5 %collective-permute-start.13 = (bf16[192,768]{1,0:T(8,128)(2,1)}, bf16[192,768]{1,0:T(8,128)(2,1)S(1)}, u32[]{:S(2)}, u32[]{:S(2)}) collective-permute-start(bf16[192,768]{1,0:T(8,128)(2,1)} %get-tuple-element.194), channel_id=1, source_target_pairs={{0,16},{1,17},{2,18},{3,19},{4,20},{5,21},{6,22},{7,23},{8,24},{9,... | collective-permute-start | bytes 884744 | tf_op jit(solution)/shard_map/ppermute | solution.py:47
  78.0 17.0 %collective-permute-start.14 = (bf16[2,192,768]{2,1,0:T(8,128)(2,1)S(1)}, bf16[2,192,768]{2,1,0:T(8,128)(2,1)S(1)}, u32[]{:S(2)}, u32[]{:S(2)}) collective-permute-start(bf16[2,192,768]{2,1,0:T(8,128)(2,1)S(1)} %bitcast.331), channel_id=1, source_target_pairs={{0,8},{1,9},{2,10},{3,11},{4,12},{5,13},{6,14},{7,15},{8,0},{9,1},... | collective-permute-start | bytes 1769480 | tf_op jit(solution)/shard_map/ppermute | solution.py:47
  80.2 25.0 %collective-permute-start.18 = (bf16[4,1,192,768]{3,2,1,0:T(8,128)(2,1)}, bf16[4,1,192,768]{3,2,1,0:T(8,128)(2,1)}, u32[]{:S(2)}, u32[]{:S(2)}) collective-permute-start(bf16[4,1,192,768]{3,2,1,0:T(8,128)(2,1)} %bitcast.42.mine_ref), channel_id=1, source_target_pairs={{0,2},{1,5},{2,0},{3,7},{4,6},{5,1},{6,4},{7,3},{8,10},{9,13},{10,... | collective-permute-start | bytes 3538952 | tf_op jit(solution)/shard_map/ppermute | solution.py:79
  91.8 57.0 %collective-permute-start.22 = (bf16[8,24,768]{2,1,0:T(8,128)(2,1)}, bf16[8,24,768]{2,1,0:T(8,128)(2,1)}, u32[]{:S(2)}, u32[]{:S(2)}) collective-permute-start(bf16[8,24,768]{2,1,0:T(8,128)(2,1)} %dynamic-slice_bitcast_fusion.3), channel_id=1, source_target_pairs={{0,1},{1,0},{2,3},{3,2},{4,5},{5,4},{6,7},{7,6},{8,9},{9,8},{10,11... | collective-permute-start | bytes 884744 | tf_op jit(solution)/shard_map/ppermute | solution.py:47
  96.7 23.7 %collective-permute-start.17 = (bf16[4,1,192,768]{3,2,1,0:T(8,128)(2,1)}, bf16[4,1,192,768]{3,2,1,0:T(8,128)(2,1)}, u32[]{:S(2)}, u32[]{:S(2)}) collective-permute-start(bf16[4,1,192,768]{3,2,1,0:T(8,128)(2,1)} %bitcast.53.mine_ref), channel_id=1, source_target_pairs={{0,2},{1,5},{2,0},{3,7},{4,6},{5,1},{6,4},{7,3},{8,10},{9,13},{10,... | collective-permute-start | bytes 3538952 | tf_op jit(solution)/shard_map/ppermute | solution.py:79
  104.2 6.8 %collective-permute-start.16 = (bf16[8,24,768]{2,1,0:T(8,128)(2,1)S(1)}, bf16[8,24,768]{2,1,0:T(8,128)(2,1)S(1)}, u32[]{:S(2)}, u32[]{:S(2)}) collective-permute-start(bf16[8,24,768]{2,1,0:T(8,128)(2,1)S(1)} %dynamic-slice_bitcast_fusion.2), channel_id=1, source_target_pairs={{0,1},{1,0},{2,3},{3,2},{4,5},{5,4},{6,7},{7,6},{8,9},{9,8},{10,11... | collective-permute-start | bytes 884744 | tf_op jit(solution)/shard_map/ppermute | solution.py:47
  105.2 45.8 %copy-start.43 = (f32[8,768]{1,0:T(8,128)}, f32[8,768]{1,0:T(8,128)S(1)}, u32[]{:S(2)}) copy-start(f32[8,768]{1,0:T(8,128)S(1)} %slice.1041.vec_ref.refs_4_) | copy-start | bytes 73732
  107.2 34.0 %collective-permute-start.20 = (bf16[4,2,192,768]{3,2,1,0:T(8,128)(2,1)S(1)}, bf16[4,2,192,768]{3,2,1,0:T(8,128)(2,1)S(1)}, u32[]{:S(2)}, u32[]{:S(2)}) collective-permute-start(bf16[4,2,192,768]{3,2,1,0:T(8,128)(2,1)S(1)} %shard_map.181.mine_ref), channel_id=1, source_target_pairs={{0,4},{1,3},{2,6},{3,1},{4,0},{5,7},{6,2},{7,5},{8,12},{9,11},{10,... | collective-permute-start | bytes 7077896 | tf_op jit(solution)/shard_map/ppermute | solution.py:79
  111.2 11.0 %copy-start.18 = (bf16[4,4,48,768]{3,2,1,0:T(8,128)(2,1)S(1)}, bf16[4,4,48,768]{3,2,1,0:T(8,128)(2,1)}, u32[]{:S(2)}) copy-start(bf16[4,4,48,768]{3,2,1,0:T(8,128)(2,1)} %copy-done.17) | copy-start | bytes 3538948
  136.6 2.3 collective-permute-start.19
  137.1 29.1 %collective-permute-start.24 = (bf16[4,2,192,768]{3,2,1,0:T(8,128)(2,1)S(1)}, bf16[4,2,192,768]{3,2,1,0:T(8,128)(2,1)S(1)}, u32[]{:S(2)}, u32[]{:S(2)}) collective-permute-start(bf16[4,2,192,768]{3,2,1,0:T(8,128)(2,1)S(1)} %shard_map.182.mine_ref), channel_id=1, source_target_pairs={{0,4},{1,3},{2,6},{3,1},{4,0},{5,7},{6,2},{7,5},{8,12},{9,11},{10,... | collective-permute-start | bytes 7077896 | tf_op jit(solution)/shard_map/ppermute | solution.py:79
  148.7 2.3 collective-permute-start.21
  152.0 12.6 %copy-start.28 = (f32[512,768]{1,0:T(8,128)}, f32[512,768]{1,0:T(8,128)S(1)}, u32[]{:S(2)}) copy-start(f32[512,768]{1,0:T(8,128)S(1)} %get-tuple-element.232.refs_3_) | copy-start | bytes 4718596
  152.4 13.2 %copy-start.67 = (bf16[256,768]{1,0:T(8,128)(2,1)S(1)}, bf16[256,768]{1,0:T(8,128)(2,1)}, u32[]{:S(2)}) copy-start(bf16[256,768]{1,0:T(8,128)(2,1)} %param.19) | copy-start | bytes 1179652
  164.6 2.4 collective-permute-start.23
  165.7 8.0 %collective-permute-start.26 = (bf16[256,768]{1,0:T(8,128)(2,1)S(1)}, bf16[256,768]{1,0:T(8,128)(2,1)S(1)}, u32[]{:S(2)}, u32[]{:S(2)}) collective-permute-start(bf16[256,768]{1,0:T(8,128)(2,1)S(1)} %copy-done.67), channel_id=1, source_target_pairs={{0,1},{1,0},{2,3},{3,2},{4,5},{5,4},{6,7},{7,6},{8,9},{9,8},{10,11... | collective-permute-start | bytes 1179656 | tf_op jit(solution)/shard_map/ppermute | solution.py:47
  171.5 2.4 collective-permute-start.25
  184.5 2.9 collective-permute-start.27
  185.1 31.3 %copy-start.65 = (s32[16,768]{1,0:T(8,128)}, s32[16,768]{1,0:T(8,128)S(1)}, u32[]{:S(2)}) copy-start(s32[16,768]{1,0:T(8,128)S(1)} %fusion.64) | copy-start | bytes 147460
  185.1 20.9 %collective-permute-start.29 = (bf16[4,2,96,768]{3,2,1,0:T(8,128)(2,1)S(1)}, bf16[4,2,96,768]{3,2,1,0:T(8,128)(2,1)S(1)}, u32[]{:S(2)}, u32[]{:S(2)}) collective-permute-start(bf16[4,2,96,768]{3,2,1,0:T(8,128)(2,1)S(1)} %shard_map.192), channel_id=1, source_target_pairs={{0,4},{1,3},{2,6},{3,1},{4,0},{5,7},{6,2},{7,5},{8,12},{9,11},{10,... | collective-permute-start | bytes 3538952 | tf_op jit(solution)/shard_map/ppermute | solution.py:79
  187.0 26.1 %collective-permute-start.30 = (bf16[4,2,96,768]{3,2,1,0:T(8,128)(2,1)S(1)}, bf16[4,2,96,768]{3,2,1,0:T(8,128)(2,1)S(1)}, u32[]{:S(2)}, u32[]{:S(2)}) collective-permute-start(bf16[4,2,96,768]{3,2,1,0:T(8,128)(2,1)S(1)} %shard_map.194), channel_id=1, source_target_pairs={{0,4},{1,3},{2,6},{3,1},{4,0},{5,7},{6,2},{7,5},{8,12},{9,11},{10,... | collective-permute-start | bytes 3538952 | tf_op jit(solution)/shard_map/ppermute | solution.py:79
  205.2 10.1 %copy-start.30 = (f32[512,768]{1,0:T(8,128)}, f32[512,768]{1,0:T(8,128)S(1)}, u32[]{:S(2)}) copy-start(f32[512,768]{1,0:T(8,128)S(1)} %get-tuple-element.269.refs_0_) | copy-start | bytes 4718596
  205.2 12.7 %copy-start.22 = (bf16[768,768]{1,0:T(8,128)(2,1)}, bf16[768,768]{1,0:T(8,128)(2,1)S(1)}, u32[]{:S(2)}) copy-start(bf16[768,768]{1,0:T(8,128)(2,1)S(1)} %get-tuple-element.277) | copy-start | bytes 3538948
  205.2 15.7 %collective-permute-start.28 = (bf16[512,768]{1,0:T(8,128)(2,1)}, bf16[512,768]{1,0:T(8,128)(2,1)}, u32[]{:S(2)}, u32[]{:S(2)}) collective-permute-start(bf16[512,768]{1,0:T(8,128)(2,1)} %get-tuple-element.284.refs_1_), channel_id=1, source_target_pairs={{0,1},{1,0},{2,3},{3,2},{4,5},{5,4},{6,7},{7,6},{8,9},{9,8},{10,11... | collective-permute-start | bytes 2359304 | tf_op jit(solution)/shard_map/ppermute | solution.py:47
  215.2 2.4 collective-permute-start.31
  216.5 29.7 %collective-permute-start.33 = (bf16[4,1,192,768]{3,2,1,0:T(8,128)(2,1)}, bf16[4,1,192,768]{3,2,1,0:T(8,128)(2,1)}, u32[]{:S(2)}, u32[]{:S(2)}) collective-permute-start(bf16[4,1,192,768]{3,2,1,0:T(8,128)(2,1)} %get-tuple-element.276), channel_id=1, source_target_pairs={{0,2},{1,5},{2,0},{3,7},{4,6},{5,1},{6,4},{7,3},{8,10},{9,13},{10,... | collective-permute-start | bytes 3538952 | tf_op jit(solution)/shard_map/ppermute | solution.py:79
  219.6 53.2 %collective-permute-start.35 = (bf16[4,2,112,768]{3,2,1,0:T(8,128)(2,1)}, bf16[4,2,112,768]{3,2,1,0:T(8,128)(2,1)}, u32[]{:S(2)}, u32[]{:S(2)}) collective-permute-start(bf16[4,2,112,768]{3,2,1,0:T(8,128)(2,1)} %shard_map.197), channel_id=1, source_target_pairs={{0,4},{1,3},{2,6},{3,1},{4,0},{5,7},{6,2},{7,5},{8,12},{9,11},{10,... | collective-permute-start | bytes 4128776 | tf_op jit(solution)/shard_map/ppermute | solution.py:79
  242.7 7.7 %collective-permute-start.32 = (bf16[512,768]{1,0:T(8,128)(2,1)}, bf16[512,768]{1,0:T(8,128)(2,1)}, u32[]{:S(2)}, u32[]{:S(2)}) collective-permute-start(bf16[512,768]{1,0:T(8,128)(2,1)} %get-tuple-element.300.mine_ref), channel_id=1, source_target_pairs={{0,1},{1,0},{2,3},{3,2},{4,5},{5,4},{6,7},{7,6},{8,9},{9,8},{10,11... | collective-permute-start | bytes 2359304 | tf_op jit(solution)/shard_map/ppermute | solution.py:47
  248.8 23.4 %collective-permute-start.36 = (bf16[2,1,192,768]{3,2,0,1:T(8,128)(2,1)S(1)}, bf16[2,1,192,768]{3,2,0,1:T(8,128)(2,1)S(1)}, u32[]{:S(2)}, u32[]{:S(2)}) collective-permute-start(bf16[2,1,192,768]{3,2,0,1:T(8,128)(2,1)S(1)} %bitcast.372), channel_id=1, source_target_pairs={{0,8},{1,9},{2,10},{3,11},{4,12},{5,13},{6,14},{7,15},{8,0},{9,1},... | collective-permute-start | bytes 1769480 | tf_op jit(solution)/shard_map/ppermute | solution.py:47
  249.0 26.4 %collective-permute-start.38 = (bf16[4,2,96,768]{3,2,1,0:T(8,128)(2,1)}, bf16[4,2,96,768]{3,2,1,0:T(8,128)(2,1)S(1)}, u32[]{:S(2)}, u32[]{:S(2)}) collective-permute-start(bf16[4,2,96,768]{3,2,1,0:T(8,128)(2,1)} %copy-done.40), channel_id=1, source_target_pairs={{0,4},{1,3},{2,6},{3,1},{4,0},{5,7},{6,2},{7,5},{8,12},{9,11},{10,... | collective-permute-start | bytes 3538952 | tf_op jit(solution)/shard_map/ppermute | solution.py:79
  249.9 27.3 %collective-permute-start.39 = (bf16[4,2,96,768]{3,2,1,0:T(8,128)(2,1)S(1)}, bf16[4,2,96,768]{3,2,1,0:T(8,128)(2,1)S(1)}, u32[]{:S(2)}, u32[]{:S(2)}) collective-permute-start(bf16[4,2,96,768]{3,2,1,0:T(8,128)(2,1)S(1)} %shard_map.201), channel_id=1, source_target_pairs={{0,4},{1,3},{2,6},{3,1},{4,0},{5,7},{6,2},{7,5},{8,12},{9,11},{10,... | collective-permute-start | bytes 3538952 | tf_op jit(solution)/shard_map/ppermute | solution.py:79
  271.1 86.4 %collective-permute-start.34 = (bf16[256,768]{1,0:T(8,128)(2,1)S(1)}, bf16[256,768]{1,0:T(8,128)(2,1)S(1)}, u32[]{:S(2)}, u32[]{:S(2)}) collective-permute-start(bf16[256,768]{1,0:T(8,128)(2,1)S(1)} %get-tuple-element.472), channel_id=1, source_target_pairs={{0,1},{1,0},{2,3},{3,2},{4,5},{5,4},{6,7},{7,6},{8,9},{9,8},{10,11... | collective-permute-start | bytes 1179656 | tf_op jit(solution)/shard_map/ppermute | solution.py:47
  274.7 10.8 %collective-permute-start.37 = (bf16[4,1,112,768]{3,2,1,0:T(8,128)(2,1)S(1)}, bf16[4,1,112,768]{3,2,1,0:T(8,128)(2,1)S(1)}, u32[]{:S(2)}, u32[]{:S(2)}) collective-permute-start(bf16[4,1,112,768]{3,2,1,0:T(8,128)(2,1)S(1)} %get-tuple-element.316), channel_id=1, source_target_pairs={{0,2},{1,5},{2,0},{3,7},{4,6},{5,1},{6,4},{7,3},{8,10},{9,13},{10,... | collective-permute-start | bytes 2064392 | tf_op jit(solution)/shard_map/ppermute | solution.py:79
  278.2 8.7 %copy-start.66 = (s32[16,768]{1,0:T(8,128)S(1)}, s32[16,768]{1,0:T(8,128)}, u32[]{:S(2)}) copy-start(s32[16,768]{1,0:T(8,128)} %copy-done.65) | copy-start | bytes 147460
  278.2 28.2 %collective-permute-start.45 = (bf16[4,1,192,768]{3,2,1,0:T(8,128)(2,1)S(1)}, bf16[4,1,192,768]{3,2,1,0:T(8,128)(2,1)S(1)}, u32[]{:S(2)}, u32[]{:S(2)}) collective-permute-start(bf16[4,1,192,768]{3,2,1,0:T(8,128)(2,1)S(1)} %get-tuple-element.319), channel_id=1, source_target_pairs={{0,2},{1,5},{2,0},{3,7},{4,6},{5,1},{6,4},{7,3},{8,10},{9,13},{10,... | collective-permute-start | bytes 3538952 | tf_op jit(solution)/shard_map/ppermute | solution.py:79
  286.2 4.2 %collective-permute-start.40 = (bf16[8,24,768]{2,1,0:T(8,128)(2,1)S(1)}, bf16[8,24,768]{2,1,0:T(8,128)(2,1)S(1)}, u32[]{:S(2)}, u32[]{:S(2)}) collective-permute-start(bf16[8,24,768]{2,1,0:T(8,128)(2,1)S(1)} %dynamic-slice_bitcast_fusion), channel_id=1, source_target_pairs={{0,1},{1,0},{2,3},{3,2},{4,5},{5,4},{6,7},{7,6},{8,9},{9,8},{10,11... | collective-permute-start | bytes 884744 | tf_op jit(solution)/shard_map/ppermute | solution.py:47
  287.0 21.8 %collective-permute-start.52 = (bf16[1,1,192,768]{3,2,1,0:T(8,128)(2,1)S(1)}, bf16[1,1,192,768]{3,2,1,0:T(8,128)(2,1)S(1)}, u32[]{:S(2)}, u32[]{:S(2)}) collective-permute-start(bf16[1,1,192,768]{3,2,1,0:T(8,128)(2,1)S(1)} %get-tuple-element.313), channel_id=1, source_target_pairs={{0,16},{1,17},{2,18},{3,19},{4,20},{5,21},{6,22},{7,23},{8,24},{9,... | collective-permute-start | bytes 884744 | tf_op jit(solution)/shard_map/ppermute | solution.py:47
  290.3 15.0 %collective-permute-start.42 = (bf16[2,1,112,768]{3,2,0,1:T(8,128)(2,1)S(1)}, bf16[2,1,112,768]{3,2,0,1:T(8,128)(2,1)S(1)}, u32[]{:S(2)}, u32[]{:S(2)}) collective-permute-start(bf16[2,1,112,768]{3,2,0,1:T(8,128)(2,1)S(1)} %bitcast.373), channel_id=1, source_target_pairs={{0,8},{1,9},{2,10},{3,11},{4,12},{5,13},{6,14},{7,15},{8,0},{9,1},... | collective-permute-start | bytes 1032200 | tf_op jit(solution)/shard_map/ppermute | solution.py:47
  291.4 21.8 %collective-permute-start.41 = (bf16[4,2,112,768]{3,2,1,0:T(8,128)(2,1)S(1)}, bf16[4,2,112,768]{3,2,1,0:T(8,128)(2,1)S(1)}, u32[]{:S(2)}, u32[]{:S(2)}) collective-permute-start(bf16[4,2,112,768]{3,2,1,0:T(8,128)(2,1)S(1)} %shard_map.208), channel_id=1, source_target_pairs={{0,4},{1,3},{2,6},{3,1},{4,0},{5,7},{6,2},{7,5},{8,12},{9,11},{10,... | collective-permute-start | bytes 4128776 | tf_op jit(solution)/shard_map/ppermute | solution.py:79
  306.0 19.6 %collective-permute-start.44 = (bf16[1,1,112,768]{3,2,1,0:T(8,128)(2,1)S(1)}, bf16[1,1,112,768]{3,2,1,0:T(8,128)(2,1)S(1)}, u32[]{:S(2)}, u32[]{:S(2)}) collective-permute-start(bf16[1,1,112,768]{3,2,1,0:T(8,128)(2,1)S(1)} %get-tuple-element.330), channel_id=1, source_target_pairs={{0,16},{1,17},{2,18},{3,19},{4,20},{5,21},{6,22},{7,23},{8,24},{9,... | collective-permute-start | bytes 516104 | tf_op jit(solution)/shard_map/ppermute | solution.py:47
  307.2 17.8 %collective-permute-start.46 = (bf16[2,1,192,768]{3,2,0,1:T(8,128)(2,1)S(1)}, bf16[2,1,192,768]{3,2,0,1:T(8,128)(2,1)S(1)}, u32[]{:S(2)}, u32[]{:S(2)}) collective-permute-start(bf16[2,1,192,768]{3,2,0,1:T(8,128)(2,1)S(1)} %bitcast.371), channel_id=1, source_target_pairs={{0,8},{1,9},{2,10},{3,11},{4,12},{5,13},{6,14},{7,15},{8,0},{9,1},... | collective-permute-start | bytes 1769480 | tf_op jit(solution)/shard_map/ppermute | solution.py:47
  308.9 2.1 collective-permute-start.53
  314.0 15.9 %collective-permute-start.43 = (bf16[4,1,112,768]{3,2,1,0:T(8,128)(2,1)S(1)}, bf16[4,1,112,768]{3,2,1,0:T(8,128)(2,1)S(1)}, u32[]{:S(2)}, u32[]{:S(2)}) collective-permute-start(bf16[4,1,112,768]{3,2,1,0:T(8,128)(2,1)S(1)} %get-tuple-element.333), channel_id=1, source_target_pairs={{0,2},{1,5},{2,0},{3,7},{4,6},{5,1},{6,4},{7,3},{8,10},{9,13},{10,... | collective-permute-start | bytes 2064392 | tf_op jit(solution)/shard_map/ppermute | solution.py:79
  325.7 21.8 %collective-permute-start.50 = (bf16[1,1,192,768]{3,2,1,0:T(8,128)(2,1)S(1)}, bf16[1,1,192,768]{3,2,1,0:T(8,128)(2,1)S(1)}, u32[]{:S(2)}, u32[]{:S(2)}) collective-permute-start(bf16[1,1,192,768]{3,2,1,0:T(8,128)(2,1)S(1)} %get-tuple-element.340), channel_id=1, source_target_pairs={{0,16},{1,17},{2,18},{3,19},{4,20},{5,21},{6,22},{7,23},{8,24},{9,... | collective-permute-start | bytes 884744 | tf_op jit(solution)/shard_map/ppermute | solution.py:47
  326.6 3.0 collective-permute-start.49
  330.6 16.2 %collective-permute-start.47 = (bf16[2,1,112,768]{3,2,0,1:T(8,128)(2,1)S(1)}, bf16[2,1,112,768]{3,2,0,1:T(8,128)(2,1)S(1)}, u32[]{:S(2)}, u32[]{:S(2)}) collective-permute-start(bf16[2,1,112,768]{3,2,0,1:T(8,128)(2,1)S(1)} %bitcast.374), channel_id=1, source_target_pairs={{0,8},{1,9},{2,10},{3,11},{4,12},{5,13},{6,14},{7,15},{8,0},{9,1},... | collective-permute-start | bytes 1032200 | tf_op jit(solution)/shard_map/ppermute | solution.py:47
  347.4 9.9 %collective-permute-start.48 = (bf16[1,1,112,768]{3,2,1,0:T(8,128)(2,1)S(1)}, bf16[1,1,112,768]{3,2,1,0:T(8,128)(2,1)S(1)}, u32[]{:S(2)}, u32[]{:S(2)}) collective-permute-start(bf16[1,1,112,768]{3,2,1,0:T(8,128)(2,1)S(1)} %get-tuple-element.347), channel_id=1, source_target_pairs={{0,16},{1,17},{2,18},{3,19},{4,20},{5,21},{6,22},{7,23},{8,24},{9,... | collective-permute-start | bytes 516104 | tf_op jit(solution)/shard_map/ppermute | solution.py:47
  347.6 2.0 collective-permute-start.51
  357.5 2.3 collective-permute-start.54
  (67 other events, 178.8 us)
where the time goes:
time: 368 us; the launch traced here: 363 us
  Pallas kernels  125 us (34%)
  waiting for transfers between devices  111 us (30%)
  starting transfers between devices  57.4 us (16%)
  local copies, waits for them, and re-layouts  45.2 us (12%)
  other arithmetic  15.3 us (4%)
  between operations  5.06 us (1%)
    pallas_call x46, Pallas kernels, kernel_call(): pl.pallas_call(body, out_shape=shapes, in_specs=[in_smem if value.dtype =...  125 us
    ppermute x37, waiting for transfers between devices, swap(): return lax.ppermute(value, AXIS, pairs)  83 us
    ppermute x37, starting transfers between devices, swap(): return lax.ppermute(value, AXIS, pairs)  39.9 us
    unnamed x204, local copies, waits for them, and re-layouts  28.6 us
    ppermute x18, waiting for transfers between devices, plane_swap(): return lax.ppermute(value, AXIS, pairs)  28.1 us
    ppermute x18, starting transfers between devices, plane_swap(): return lax.ppermute(value, AXIS, pairs)  17.6 us
  transfers between devices with their start and end apart: 55, of which 25 were waited for; matrix products, arithmetic and copies ran while one was open for 9% of the time, Pallas kernels for 32%

commit v1 on v0

--- a/solution.py
+++ b/solution.py
@@ -20,13 +20,14 @@
 LATENCY = 2.5
 UNIT = 1.48
 ATTN, FFN = 0, 1
-OPEN_SENDS = 4
-VMEM_LIMIT = 24 * 2**20
-DIRECT = (False, False, False, False)
+OPEN_SENDS = 5
+VMEM_LIMIT = 8 * 2**20
+EARLY = (False, False, True, True)
+LATE = (False, True, False, True)
 ORDER = (
-    0, 16, 6, 1, 11, 17, 7, 18, 2, 21, 8, 12, 19, 9, 13, 3, 22, 20, 23, 10, 14, 24, 26,
-    15, 27, 4, 28, 29, 25, 30, 5, 31, 33, 34, 35, 37, 36, 47, 32, 48, 38, 49, 39, 42, 51,
-    43, 50, 52, 40, 44, 56, 53, 45, 57, 58, 54, 41, 55, 46, 59, 61, 60,
+    0, 6, 16, 7, 1, 11, 2, 12, 21, 8, 17, 22, 9, 18, 13, 19, 23, 14, 3, 10, 15, 20, 26,
+    24, 25, 27, 28, 29, 4, 5, 30, 31, 33, 34, 35, 36, 37, 32, 47, 48, 42, 49, 38, 51, 50,
+    52, 43, 56, 53, 39, 57, 44, 40, 58, 45, 54, 41, 61, 46, 59, 55, 60,
 )
 
 
@@ -159,55 +160,46 @@
 
 
 class Gather:
-    def __init__(self, chips, sequence, direct, piece):
+    def __init__(self, chips, sequence, early, piece):
         self.chips, self.sequence = chips, sequence
-        self.direct = direct
-        self.piece = piece
-        self.steps_done = 0
-        self.held = None
+        low = [("low", step) for step in range(len(chips.low))]
+        top = [("top", 2), ("top", 1)]
+        self.steps = low[:1] + top + low[1:] if early else top + low
+        self.held = piece[None, None]
 
     def start(self):
-        self.piece = self.sequence.gate(self.piece)
-        self.sequence.mark(self.piece)
-        if self.direct:
-            self.coming = [swap(self.piece, 2 * self.chips.step * k) for k in (1, 2, 3)]
-            self.steps_done = 1
+        self.held = self.sequence.gate(self.held)
+        self.sequence.mark(self.held)
+        self.send()
+
+    def send(self):
+        kind, step = self.steps[0]
+        if kind == "low":
+            self.coming = self.chips.plane_swap(self.held, step)
         else:
-            self.coming = swap(self.piece, 2 * 2 * self.chips.step)
-
-    def advance(self):
+            self.coming = swap(self.held, 2 * step * self.chips.step)
+
+    def merged(self, ranges=None):
         chips = self.chips
         coming = self.sequence.gate(self.coming)
-        step = self.steps_done
-        self.steps_done += 1
-        if step == 0:
-            self.held = merge_rows(self.piece[None, None], coming[None, None], chips.top // 2, 0)
-            self.held = self.held.reshape((2,) + self.piece.shape)
-            self.sequence.mark(self.held)
-            self.coming = swap(self.held, 2 * chips.step)
-            return
-        if step == 1:
-            if self.direct:
-                parts = [self.piece] + coming
-                parts = [merge(parts[i], parts[i + 1], chips.top % 2, 0) for i in (0, 2)]
-                held = merge(parts[0], parts[1], chips.top // 2, 0)
-            else:
-                held = merge_rows(self.held[:, None], coming[:, None], chips.top % 2, 0)
-            self.held = held.reshape((4, 1) + self.piece.shape)
-        else:
-            bit = chips.plane_bit(step - 2)
-            self.held = merge_rows(self.held, coming, bit, chips.core)
+        kind, step = self.steps.pop(0)
+        if kind == "low":
+            return merge_rows(self.held, coming, chips.plane_bit(step), chips.core, ranges)
+        lead, half, height, width = self.held.shape
+        flat = [value.reshape(lead, 1, half * height, width) for value in (self.held, coming)]
+        bit = chips.top // 2 if step == 2 else chips.top % 2
+        return merge_rows(*flat, bit, 0).reshape(2 * lead, half, height, width)
+
+    def advance(self):
+        self.held = self.merged()
         self.sequence.mark(self.held)
-        self.coming = chips.plane_swap(self.held, step - 1)
+        self.send()
 
     def finish(self, ranges):
-        chips = self.chips
-        while self.steps_done <= len(chips.low):
+        while len(self.steps) > 1:
             self.advance()
-        coming = self.sequence.gate(self.coming)
-        bit = chips.plane_bit(self.steps_done - 2)
-        results = merge_rows(self.held, coming, bit, chips.core, ranges)
-        results = [whole.reshape((chips.count,) + whole.shape[2:]) for whole in results]
+        results = self.merged(ranges)
+        results = [whole.reshape((self.chips.count,) + whole.shape[2:]) for whole in results]
         self.sequence.mark(results)
         return results
 
@@ -251,11 +243,14 @@
 
 
 class Scatter:
-    def __init__(self, chips, sequence, count):
+    def __init__(self, chips, sequence, count, late):
         self.chips, self.sequence = chips, sequence
-        self.steps_done = 0
+        low = [("low", step) for step in range(len(chips.low) - 1)][::-1]
+        top = [("top", 1), ("top", 2)]
+        self.steps = low[:-1] + top + low[-1:] if late else low + top
         self.arrays = [None] * count
         self.coming = [None] * count
+        self.heights = None
 
     def start(self, part, arrays):
         chips = self.chips
@@ -270,32 +265,32 @@
     def advance(self):
         chips = self.chips
         coming = self.sequence.gate(self.coming)
-        self.steps_done += 1
-        step = len(chips.low) - 1 - self.steps_done
-        if self.steps_done == 1:
+        if self.heights is None:
             self.heights = [value.shape[2] for part in self.arrays for value in part]
-            kept = chips.half_places(step + 1, True)
+            kept = chips.half_places(len(chips.low) - 1, True)
         else:
             self.arrays, coming = [[self.kept]], [coming]
             kept = jnp.arange(self.kept.shape[1])
-        if step >= 0:
+        kind, step = self.steps.pop(0)
+        if kind == "low":
             sides = [chips.half_places(step, own) for own in (False, True)]
         else:
-            bit = chips.top % 2 if step == -1 else chips.top // 2
-            sides = [jnp.reshape(1 - bit, (1,)), jnp.reshape(bit, (1,))]
-            lead = 2 if step == -1 else 1
+            bit = chips.top // 2 if step == 2 else chips.top % 2
+            lead, places = self.arrays[0][0].shape[:2]
+            half = coming[0].shape[1]
             self.arrays = [
-                [value.reshape((lead, 2) + value.shape[-2:]) for value in part]
+                [value.reshape((lead // 2, 2 * places) + value.shape[2:]) for value in part]
                 for part in self.arrays
             ]
-            coming = [got.reshape((lead, 2) + got.shape[-2:]) for got in coming]
-            kept = jnp.arange(2)
+            coming = [got.reshape((lead // 2, 2 * half) + got.shape[2:]) for got in coming]
+            kept = jnp.concatenate([kept, places + kept])
+            sides = [half * which + jnp.arange(half) for which in (1 - bit, bit)]
         sent, self.kept = fold_rows(self.arrays, coming, kept, sides)
         self.sequence.mark(sent)
-        if step >= 0:
+        if kind == "low":
             self.coming = chips.plane_swap(sent, step)
         else:
-            self.coming = swap(sent, 2 * chips.step if step == -1 else 4 * chips.step)
+            self.coming = swap(sent, 2 * step * chips.step)
 
     def finish(self):
         coming = self.sequence.gate(self.coming)
@@ -774,7 +769,7 @@
             vectors += [units[layer : layer + 1, i * width :][:, :width] for i in range(panels)]
             vectors.append(jnp.zeros((8 - panels, width), BF))
             state.gathers[ATTN, layer] = Gather(
-                chips, sequence, DIRECT[layer],
+                chips, sequence, EARLY[layer],
                 jnp.concatenate(
                     [
                         cols[layer, :, :, :width].reshape(2 * rows, width),
@@ -785,7 +780,7 @@
                     axis=0,
                 ),
             )
-        sequence.mark([state.gathers[ATTN, layer].piece for layer in range(LAYERS)])
+        sequence.mark([state.gathers[ATTN, layer].held for layer in range(LAYERS)])
 
     groups = hidden // width
 
@@ -806,10 +801,10 @@
                     ]
                     parts.append(jnp.concatenate(cut, axis=1))
             state.gathers[FFN, layer] = Gather(
-                chips, sequence, DIRECT[LAYERS + layer],
+                chips, sequence, EARLY[LAYERS + layer],
                 jnp.concatenate(parts + [w_down[layer]], axis=0),
             )
-        sequence.mark([state.gathers[FFN, layer].piece for layer in range(LAYERS)])
+        sequence.mark([state.gathers[FFN, layer].held for layer in range(LAYERS)])
 
     def read_vectors(layer, table):
         table = jnp.sum(table.astype(F32), axis=0)
@@ -1083,27 +1078,30 @@
             state.gathers[kind, layer].advance()
 
         units = 7.0 / 3 if kind == ATTN else 4.0
-        z = UNIT * 2 * units
-        if DIRECT[LAYERS * kind + layer]:
-            need = ("z", kind, layer)
-            links = (("z", 1.5 * z), ("w", 2 * z))
-            add(("g", kind, layer), 1 + rank, 5.0, needs, start, [(need, links, 3)])
-        else:
-            need = ("y", kind, layer)
-            links = (("z", 0.5 * z), ("w", z + 1.5))
-            add(("g", kind, layer), 1 + rank, 3.5, needs, start, [(need, links, 1)])
-            sent = ("z", kind, layer)
-            add(("h", kind, layer), 1 + rank, 2.2, [need], advance, [(sent, (("z", z),), 1)])
+        tops = [("top", 2), ("top", 1)]
+        lows = [("low", step) for step in range(low)]
+        early = EARLY[LAYERS * kind + layer]
+        steps = lows[:1] + tops + lows[1:] if early else tops + lows
+        need = None
+        held = 1
+        for number, (bits, step) in enumerate(steps):
+            length = UNIT / 2 * units * held
+            held *= 2
+            if bits == "low":
+                links = plane(length)
+            elif step == 2:
+                links = (("z", 2 * length), ("w", 4 * length + 1.5))
+            else:
+                links = (("z", 2 * length),)
+            sent = ("gx", kind, layer, number)
+            if number == 0:
+                add(("g", kind, layer), 1 + rank, 3.5, needs, start, [(sent, links, 1)])
+            else:
+                add(
+                    ("gs", kind, layer, number), 1 + rank, 1.0 + 0.1 * held + (2.8 if len(links) > 1 and links[1][0] == "w" else 1.4),
+                    [need], advance, [(sent, links, 1)],
+                )
             need = sent
-        length = UNIT * 2 * units
-        for step in range(low):
-            sent = ("xy", kind, layer, step)
-            add(
-                ("gs", kind, layer, step), 1 + rank, 2.5 + 0.3 * kind, [need], advance,
-                [(sent, plane(length), 1)],
-            )
-            need = sent
-            length *= 2
         if kind == ATTN:
             add(
                 ("go", layer), 1 + rank, 4.5, [need], call(out_exchange, layer),
@@ -1127,8 +1125,8 @@
 
     needs = [need, "ce"]
     for layer in reversed(range(LAYERS)):
-        state.scatters[FFN, layer] = Scatter(chips, sequence, 2)
-        state.scatters[ATTN, layer] = Scatter(chips, sequence, 1)
+        state.scatters[FFN, layer] = Scatter(chips, sequence, 2, LATE[LAYERS + layer])
+        state.scatters[ATTN, layer] = Scatter(chips, sequence, 1, LATE[layer])
         add(
             ("b", 0, layer), 10, 5.0, needs, call(run_back_second, layer),
             [(("r", FFN, layer, 0), plane(UNIT * 8), 1)],
@@ -1154,25 +1152,27 @@
                 state.scatters[kind, layer].advance()
 
             units = 7.0 / 3 if kind == ATTN else 4.0
-            length = UNIT * 2 * units
-            for step in range(low - 1):
-                sent = ("r", kind, layer, 2 + step)
-                add(
-                    ("rs", kind, layer, step), rank, 2.8 + 0.4 * kind, need, reduce,
-                    [(sent, plane(length), 1)],
-                )
+            tops = [("top", 1), ("top", 2)]
+            lows = [("low", step) for step in range(low - 1)][::-1]
+            late = LATE[LAYERS * kind + layer]
+            steps = lows[:-1] + tops + lows[-1:] if late else lows + tops
+            held = 2 * count // 4
+            for number, (bits, step) in enumerate(steps):
+                held //= 2
+                length = UNIT / 2 * units * held
+                cost = 1.0 + 0.1 * held
+                if bits == "low":
+                    cost, links = cost + 1.4, plane(length)
+                elif step == 2:
+                    cost, links = cost + 2.8, (("z", 2 * length), ("w", 4 * length + 1.5))
+                else:
+                    cost, links = cost + 1.4, (("z", 2 * length),)
+                sent = ("rx", kind, layer, number)
+                add(("rs", kind, layer, number), rank, cost, need, reduce, [(sent, links, 1)])
                 need = [sent]
-                length /= 2
-            z = UNIT * 2 * units
-            sent = ("rz", kind, layer)
-            add(("rs", kind, layer, low), rank, 2.2, need, reduce, [(sent, (("z", z),), 1)])
-            need = sent
-            links = (("z", 0.5 * z), ("w", z + 1.5))
-            sent = ("ry", kind, layer)
-            add(("rs", kind, layer, low + 1), rank, 3.5, [need], reduce, [(sent, links, 1)])
             last = finish_hidden if kind == FFN else finish_attention
             add(
-                ("rf", kind, layer), 19, 2.0, [sent], call(last, layer),
+                ("rf", kind, layer), 19, 2.0, need, call(last, layer),
                 pair_send(("re", kind, layer)),
             )
             last = end_hidden if kind == FFN else end_attention

time: 368 us -> 438 us (1.19)
  local copies, waits for them, and re-layouts: 45.2 us -> 77.8 us
  waiting for transfers between devices: 111 us -> 128 us
  other arithmetic: 15.3 us -> 26.1 us
  Pallas kernels: 125 us -> 135 us
    unnamed x204 -> x298, local copies, waits for them, and re-layouts: 28.6 us -> 55.8 us
    ppermute x18, waiting for transfers between devices: 28.1 us -> 40.1 us  [plane_swap(): return lax.ppermute(value, AXIS, pairs)]
    pallas_call x46, Pallas kernels: 125 us -> 135 us  [kernel_call(): pl.pallas_call(body, out_shape=shapes, in_specs=[in_smem if value.dtype =...]
    ppermute x37, waiting for transfers between devices: 83 us -> 87.8 us  [swap(): return lax.ppermute(value, AXIS, pairs)]
  transfers between devices with their start and end apart: 55 -> 55, of which waited for: 25 -> 19; matrix products, arithmetic and copies ran while one was open for 9% -> 11% of each run, Pallas kernels for 32% -> 27%
where the time goes in v1:
time: 438 us; the launch traced here: 432 us
  Pallas kernels  135 us (31%)
  waiting for transfers between devices  128 us (29%)
  local copies, waits for them, and re-layouts  77.8 us (18%)
  starting transfers between devices  56.3 us (13%)
  other arithmetic  26.1 us (6%)
  between operations  5.23 us (1%)
    pallas_call x46, Pallas kernels, kernel_call(): pl.pallas_call(body, out_shape=shapes, in_specs=[in_smem if value.dtype =...  135 us
    ppermute x37, waiting for transfers between devices, swap(): return lax.ppermute(value, AXIS, pairs)  87.8 us
    unnamed x298, local copies, waits for them, and re-layouts  55.8 us
    ppermute x37, starting transfers between devices, swap(): return lax.ppermute(value, AXIS, pairs)  40.7 us
    ppermute x18, waiting for transfers between devices, plane_swap(): return lax.ppermute(value, AXIS, pairs)  40.1 us
    ppermute x18, starting transfers between devices, plane_swap(): return lax.ppermute(value, AXIS, pairs)  15.6 us
  transfers between devices with their start and end apart: 55, of which 19 were waited for; matrix products, arithmetic and copies ran while one was open for 11% of the time, Pallas kernels for 27%

profile of v1, /device:TPU:1, one launch (start us, length us, event | category | flops | bytes accessed | tf_op | source)
XLA Modules:
  0.0 431.9 jit_solution(15856540227971280283)
XLA Ops:
  3.9 3.7 collective-permute-start.2
  8.3 7.6 %collective-permute-done.2.theirs_ref = bf16[1,1,112,768]{3,2,1,0:T(8,128)(2,1)S(1)} collective-permute-done((bf16[1,1,112,768]{3,2,1,0:T(8,128)(2,1)S(1)}, bf16[1,1,112,768]{3,2,1,0:T(8,128)(2,1)S(1)}, u32[]{:S(2)}, u32[]{:S(2)}) %collective-permute-start.2) | collective-permute-done | bytes 172064 | tf_op jit(solution)/shard_map/ppermute | solution.py:48
  23.7 4.5 %collective-permute-done.5.theirs_ref = bf16[1,1,192,768]{3,2,1,0:T(8,128)(2,1)S(1)} collective-permute-done((bf16[1,1,192,768]{3,2,1,0:T(8,128)(2,1)S(1)}, bf16[1,1,192,768]{3,2,1,0:T(8,128)(2,1)S(1)}, u32[]{:S(2)}, u32[]{:S(2)}) %collective-permute-start.5) | collective-permute-done | bytes 294944 | tf_op jit(solution)/shard_map/ppermute | solution.py:80
  29.4 1.4 collective-permute-start.10
  30.8 2.5 collective-permute-start.6
  33.3 33.0 %collective-permute-done.7.theirs_ref = bf16[1,1,112,768]{3,2,1,0:T(8,128)(2,1)S(1)} collective-permute-done((bf16[1,1,112,768]{3,2,1,0:T(8,128)(2,1)S(1)}, bf16[1,1,112,768]{3,2,1,0:T(8,128)(2,1)S(1)}, u32[]{:S(2)}, u32[]{:S(2)}) %collective-permute-start.7) | collective-permute-done | bytes 172064 | tf_op jit(solution)/shard_map/ppermute | solution.py:48
  68.5 5.4 %collective-permute-done.11.theirs_ref = bf16[1,1,192,768]{3,2,1,0:T(8,128)(2,1)S(1)} collective-permute-done((bf16[1,1,192,768]{3,2,1,0:T(8,128)(2,1)}, bf16[1,1,192,768]{3,2,1,0:T(8,128)(2,1)S(1)}, u32[]{:S(2)}, u32[]{:S(2)}) %collective-permute-start.11) | collective-permute-done | bytes 294944 | tf_op jit(solution)/shard_map/ppermute | solution.py:80
  76.7 1.8 shard_map.174.mine_ref
  82.8 1.4 collective-permute-start.15
  86.1 2.5 collective-permute-start.13
  88.6 2.6 collective-permute-start.4
  93.8 8.6 %collective-permute-done.14.theirs_ref = bf16[4,1,112,768]{3,2,1,0:T(8,128)(2,1)S(1)} collective-permute-done((bf16[4,1,112,768]{3,2,1,0:T(8,128)(2,1)S(1)}, bf16[4,1,112,768]{3,2,1,0:T(8,128)(2,1)S(1)}, u32[]{:S(2)}, u32[]{:S(2)}) %collective-permute-start.14) | collective-permute-done | bytes 688160 | tf_op jit(solution)/shard_map/ppermute | solution.py:80
  102.4 1.7 shard_map.177.mine_ref
  104.1 14.3 %collective-permute-done.13 = bf16[1,2,192,768]{3,2,1,0:T(8,128)(2,1)} collective-permute-done((bf16[1,2,192,768]{3,2,1,0:T(8,128)(2,1)S(1)}, bf16[1,2,192,768]{3,2,1,0:T(8,128)(2,1)}, u32[]{:S(2)}, u32[]{:S(2)}) %collective-permute-start.13) | collective-permute-done | bytes 589856 | tf_op jit(solution)/shard_map/ppermute | solution.py:48
  118.4 2.2 shard_map.178
  120.5 5.3 %collective-permute-start.24 = (bf16[2,2,192,768]{3,2,1,0:T(8,128)(2,1)}, bf16[2,2,192,768]{3,2,1,0:T(8,128)(2,1)}, u32[]{:S(2)}, u32[]{:S(2)}) collective-permute-start(bf16[2,2,192,768]{3,2,1,0:T(8,128)(2,1)} %bitcast.39), channel_id=1, source_target_pairs={{0,8},{1,9},{2,10},{3,11},{4,12},{5,13},{6,14},{7,15},{8,0},{9,1},... | collective-permute-start | bytes 3538952 | tf_op jit(solution)/shard_map/ppermute | solution.py:48
  125.9 1.5 shard_map.179
  131.0 1.9 shard_map.180
  136.6 2.2 collective-permute-start.16
  138.8 2.9 reshape.469
  141.8 2.0 copy.56
  145.8 1.9 shard_map.181
  150.7 2.5 reshape.475
  158.1 12.0 %shard_map.182 = (bf16[512,768]{1,0:T(8,128)(2,1)S(1)}, bf16[512,1152]{1,0:T(8,128)(2,1)S(1)}, bf16[512,384]{1,0:T(8,128)(2,1)S(1)}, f32[512,128]{1,0:T(8,128)S(1)}) custom-call(s32[1]{0:T(128)S(6)} %copy.135.kind_ref, bf16[512,768]{1,0:T(8,128)(2,1)S(1)} %get-tuple-element.210.x_ref, bf16[768,768]{1,0:T(8,128)(2,1)S(1)} %bitcast.337, ...), custom_call_target="tpu_custom_call" | custom-call | tf_op jit(solution)/shard_map/pallas_call | solution.py:623
  170.7 1.8 shard_map.187
  173.9 2.1 shard_map.183
  176.0 4.5 %shard_map.184 = (f32[512,768]{1,0:T(8,128)S(1)}, f32[512,768]{1,0:T(8,128)S(1)}, bf16[512,768]{1,0:T(8,128)(2,1)S(1)}, bf16[512,1536]{1,0:T(8,128)(2,1)S(1)}, b...) custom-call(f32[512,768]{1,0:T(8,128)S(1)} %copy-done.8, bf16[512,768]{1,0:T(8,128)(2,1)S(1)} %get-tuple-element.216.mine_ref, ...), custom_call_target="tpu_custom_call" | custom-call | tf_op jit(solution)/shard_map/pallas_call | solution.py:623
  186.6 12.2 %shard_map.186 = (bf16[512,768]{1,0:T(8,128)(2,1)S(1)}, bf16[512,1152]{1,0:T(8,128)(2,1)S(1)}, bf16[512,384]{1,0:T(8,128)(2,1)S(1)}, f32[512,128]{1,0:T(8,128)S(1)}) custom-call(s32[1]{0:T(128)S(6)} %copy.135.kind_ref, bf16[512,768]{1,0:T(8,128)(2,1)S(1)} %get-tuple-element.230.x_ref, bf16[768,768]{1,0:T(8,128)(2,1)S(1)} %bitcast.339, ...), custom_call_target="tpu_custom_call" | custom-call | tf_op jit(solution)/shard_map/pallas_call | solution.py:623
  203.1 5.3 %shard_map.189 = (f32[512,768]{1,0:T(8,128)S(1)}, f32[512,768]{1,0:T(8,128)S(1)}, bf16[512,768]{1,0:T(8,128)(2,1)S(1)}, bf16[512,1536]{1,0:T(8,128)(2,1)S(1)}, b...) custom-call(f32[512,768]{1,0:T(8,128)S(1)} %get-tuple-element.226.x_ref, ...), custom_call_target="tpu_custom_call" | custom-call | tf_op jit(solution)/shard_map/pallas_call | solution.py:623
  217.5 1.4 copy-done.51
  219.0 3.7 shard_map.190
  223.6 2.9 shard_map.191
  230.8 4.8 %shard_map.193 = (bf16[768,768]{1,0:T(8,128)(2,1)S(1)}, bf16[768,768]{1,0:T(8,128)(2,1)S(1)}, bf16[512,768]{1,0:T(8,128)(2,1)}, f32[1,1536]{1,0:T(1,128)S(1)}) custom-call(bf16[512,768]{1,0:T(8,128)(2,1)S(1)} %get-tuple-element.255.d_ffn_ref, bf16[512,1536]{1,0:T(8,128)(2,1)S(1)} %copy-done.71, bf16[512,768]{1,0:T(8,128)(2,1)S(1)} %copy-done.83, ...), custom_call_target="tpu_custom_call" | custom-call | tf_op jit(solution)/shard_map/pallas_call | solution.py:623
  245.9 1.4 copy-done.65
  247.3 1.4 copy-done.69
  251.0 17.9 %shard_map.195 = (bf16[768,768]{1,0:T(8,128)(2,1)S(1)}, bf16[768,384]{1,0:T(8,128)(2,1)S(1)}, bf16[384,768]{1,0:T(8,128)(2,1)S(1)}, bf16[512,768]{1,0:T(8,128)(2...) custom-call(s32[1]{0:T(128)S(6)} %copy.135.kind_ref, f32[512,768]{1,0:T(8,128)S(1)} %copy-done.69, ...), custom_call_target="tpu_custom_call" | custom-call | tf_op jit(solution)/shard_map/pallas_call | solution.py:623
  269.8 2.0 collective-permute-done.30
  272.1 1.7 shard_map.196
  275.1 2.1 shard_map.197
  277.2 1.5 copy-done.48
  279.4 1.8 constant_dynamic-slice_fusion
  281.1 1.4 copy-done.53
  282.5 1.4 copy-done.55
  284.0 1.4 copy-done.57
  285.4 4.4 %shard_map.198 = (f32[512,768]{1,0:T(8,128)S(1)}, bf16[512,768]{1,0:T(8,128)(2,1)S(1)}, bf16[1536,768]{1,0:T(8,128)(2,1)S(1)}, f32[8,768]{1,0:T(8,128)S(1)}) custom-call(f32[512,768]{1,0:T(8,128)S(1)} %copy-done.57, bf16[512,768]{1,0:T(8,128)(2,1)S(1)} %get-tuple-element.284.refs_1_, bf16[512,768]{1,0:T(8,128)(2,1)} %collective-permute-done.31.refs_2_, ...), custom_call_target="tpu_custom_call" | custom-call | tf_op jit(solution)/shard_map/pallas_call | solution.py:623
  292.4 1.4 copy-done.7
  294.2 4.8 %shard_map.200 = (bf16[768,768]{1,0:T(8,128)(2,1)S(1)}, bf16[768,768]{1,0:T(8,128)(2,1)S(1)}, bf16[512,768]{1,0:T(8,128)(2,1)}, f32[1,1536]{1,0:T(1,128)S(1)}) custom-call(bf16[512,768]{1,0:T(8,128)(2,1)S(1)} %get-tuple-element.290.d_ffn_ref, bf16[512,1536]{1,0:T(8,128)(2,1)S(1)} %copy-done.63, bf16[512,768]{1,0:T(8,128)(2,1)S(1)} %copy-done.81, ...), custom_call_target="tpu_custom_call" | custom-call | tf_op jit(solution)/shard_map/pallas_call | solution.py:623
  308.7 1.8 shard_map.202
  312.6 18.3 %shard_map.203 = (bf16[768,768]{1,0:T(8,128)(2,1)S(1)}, bf16[768,384]{1,0:T(8,128)(2,1)S(1)}, bf16[384,768]{1,0:T(8,128)(2,1)S(1)}, bf16[512,768]{1,0:T(8,128)(2...) custom-call(s32[1]{0:T(128)S(6)} %copy.135.kind_ref, f32[512,768]{1,0:T(8,128)S(1)} %copy-done.67, ...), custom_call_target="tpu_custom_call" | custom-call | tf_op jit(solution)/shard_map/pallas_call | solution.py:623
  332.0 2.5 shard_map.204
  339.4 1.7 collective-permute-start.43
  341.2 20.4 %collective-permute-done.39 = bf16[4,1,192,768]{3,2,1,0:T(8,128)(2,1)S(1)} collective-permute-done((bf16[4,1,192,768]{3,2,1,0:T(8,128)(2,1)S(1)}, bf16[4,1,192,768]{3,2,1,0:T(8,128)(2,1)S(1)}, u32[]{:S(2)}, u32[]{:S(2)}) %collective-permute-start.39) | collective-permute-done | bytes 1179680 | tf_op jit(solution)/shard_map/ppermute | solution.py:80
  361.6 1.5 shard_map.207
  364.2 1.6 collective-permute-start.41
  366.7 2.4 collective-permute-start.34
  369.8 1.6 shard_map.209
  372.6 14.8 %collective-permute-done.41 = bf16[2,1,192,768]{3,2,0,1:T(8,128)(2,1)} collective-permute-done((bf16[2,1,192,768]{3,2,0,1:T(8,128)(2,1)}, bf16[2,1,192,768]{3,2,0,1:T(8,128)(2,1)}, u32[]{:S(2)}, u32[]{:S(2)}) %collective-permute-start.41) | collective-permute-done | bytes 589856 | tf_op jit(solution)/shard_map/ppermute | solution.py:48
  390.7 1.9 shard_map.211
  394.7 2.4 add_add_fusion
  398.4 1.8 collective-permute-start.48
  402.9 2.5 collective-permute-start.47
  407.9 5.4 %collective-permute-done.48 = bf16[2,1,112,768]{3,2,0,1:T(8,128)(2,1)S(1)} collective-permute-done((bf16[2,1,112,768]{3,2,0,1:T(8,128)(2,1)S(1)}, bf16[2,1,112,768]{3,2,0,1:T(8,128)(2,1)S(1)}, u32[]{:S(2)}, u32[]{:S(2)}) %collective-permute-start.48) | collective-permute-done | bytes 344096 | tf_op jit(solution)/shard_map/ppermute | solution.py:48
  414.6 1.9 collective-permute-start.51
  418.0 6.8 %collective-permute-done.49 = bf16[1,1,112,768]{3,2,1,0:T(8,128)(2,1)S(1)} collective-permute-done((bf16[1,1,112,768]{3,2,1,0:T(8,128)(2,1)S(1)}, bf16[1,1,112,768]{3,2,1,0:T(8,128)(2,1)S(1)}, u32[]{:S(2)}, u32[]{:S(2)}) %collective-permute-start.49) | collective-permute-done | bytes 172064 | tf_op jit(solution)/shard_map/ppermute | solution.py:48
  (596 shorter events, 128.5 us)
Async XLA Ops:
  2.1 1.6 collective-permute-start
  2.4 1.3 collective-permute-start.1
  3.2 13.4 %copy-start.107 = (bf16[2,24,3072]{2,1,0:T(8,128)(2,1)S(1)}, bf16[2,24,3072]{2,1,0:T(8,128)(2,1)}, u32[]{:S(2)}) copy-start(bf16[2,24,3072]{2,1,0:T(8,128)(2,1)} %param.16) | copy-start | bytes 884740
  3.9 12.0 %collective-permute-start.2 = (bf16[1,1,112,768]{3,2,1,0:T(8,128)(2,1)S(1)}, bf16[1,1,112,768]{3,2,1,0:T(8,128)(2,1)S(1)}, u32[]{:S(2)}, u32[]{:S(2)}) collective-permute-start(bf16[1,1,112,768]{3,2,1,0:T(8,128)(2,1)S(1)} %bitcast.369), channel_id=1, source_target_pairs={{0,16},{1,17},{2,18},{3,19},{4,20},{5,21},{6,22},{7,23},{8,24},{9,... | collective-permute-start | bytes 516104 | tf_op jit(solution)/shard_map/ppermute | solution.py:48
  17.2 1.8 collective-permute-start.3
  18.0 10.8 %collective-permute-start.8 = (bf16[2,1,112,768]{3,2,1,0:T(8,128)(2,1)S(1)}, bf16[2,1,112,768]{3,2,1,0:T(8,128)(2,1)S(1)}, u32[]{:S(2)}, u32[]{:S(2)}) collective-permute-start(bf16[2,1,112,768]{3,2,1,0:T(8,128)(2,1)S(1)} %bitcast.355), channel_id=1, source_target_pairs={{0,8},{1,9},{2,10},{3,11},{4,12},{5,13},{6,14},{7,15},{8,0},{9,1},... | collective-permute-start | bytes 1032200 | tf_op jit(solution)/shard_map/ppermute | solution.py:48
  22.3 5.9 %collective-permute-start.5 = (bf16[1,1,192,768]{3,2,1,0:T(8,128)(2,1)S(1)}, bf16[1,1,192,768]{3,2,1,0:T(8,128)(2,1)S(1)}, u32[]{:S(2)}, u32[]{:S(2)}) collective-permute-start(bf16[1,1,192,768]{3,2,1,0:T(8,128)(2,1)S(1)} %bitcast.378), channel_id=1, source_target_pairs={{0,2},{1,5},{2,0},{3,7},{4,6},{5,1},{6,4},{7,3},{8,10},{9,13},{10,... | collective-permute-start | bytes 884744 | tf_op jit(solution)/shard_map/ppermute | solution.py:80
  29.4 47.2 %collective-permute-start.10 = (bf16[4,1,112,768]{3,2,1,0:T(8,128)(2,1)S(1)}, bf16[4,1,112,768]{3,2,1,0:T(8,128)(2,1)S(1)}, u32[]{:S(2)}, u32[]{:S(2)}) collective-permute-start(bf16[4,1,112,768]{3,2,1,0:T(8,128)(2,1)S(1)} %bitcast.347), channel_id=1, source_target_pairs={{0,2},{1,5},{2,0},{3,7},{4,6},{5,1},{6,4},{7,3},{8,10},{9,13},{10,... | collective-permute-start | bytes 2064392 | tf_op jit(solution)/shard_map/ppermute | solution.py:80
  30.8 48.8 %collective-permute-start.6 = (bf16[1,2,192,768]{3,2,1,0:T(8,128)(2,1)S(1)}, bf16[1,2,192,768]{3,2,1,0:T(8,128)(2,1)S(1)}, u32[]{:S(2)}, u32[]{:S(2)}) collective-permute-start(bf16[1,2,192,768]{3,2,1,0:T(8,128)(2,1)S(1)} %shard_map.170), channel_id=1, source_target_pairs={{0,16},{1,17},{2,18},{3,19},{4,20},{5,21},{6,22},{7,23},{8,24},{9,... | collective-permute-start | bytes 1769480 | tf_op jit(solution)/shard_map/ppermute | solution.py:48
  33.3 33.0 %collective-permute-start.7 = (bf16[1,1,112,768]{3,2,1,0:T(8,128)(2,1)S(1)}, bf16[1,1,112,768]{3,2,1,0:T(8,128)(2,1)S(1)}, u32[]{:S(2)}, u32[]{:S(2)}) collective-permute-start(bf16[1,1,112,768]{3,2,1,0:T(8,128)(2,1)S(1)} %bitcast.367), channel_id=1, source_target_pairs={{0,16},{1,17},{2,18},{3,19},{4,20},{5,21},{6,22},{7,23},{8,24},{9,... | collective-permute-start | bytes 516104 | tf_op jit(solution)/shard_map/ppermute | solution.py:48
  66.9 11.6 %collective-permute-start.9 = (bf16[2,1,112,768]{3,2,1,0:T(8,128)(2,1)S(1)}, bf16[2,1,112,768]{3,2,1,0:T(8,128)(2,1)}, u32[]{:S(2)}, u32[]{:S(2)}) collective-permute-start(bf16[2,1,112,768]{3,2,1,0:T(8,128)(2,1)S(1)} %bitcast.357), channel_id=1, source_target_pairs={{0,8},{1,9},{2,10},{3,11},{4,12},{5,13},{6,14},{7,15},{8,0},{9,1},... | collective-permute-start | bytes 1032200 | tf_op jit(solution)/shard_map/ppermute | solution.py:48
  67.8 6.2 %collective-permute-start.11 = (bf16[1,1,192,768]{3,2,1,0:T(8,128)(2,1)}, bf16[1,1,192,768]{3,2,1,0:T(8,128)(2,1)S(1)}, u32[]{:S(2)}, u32[]{:S(2)}) collective-permute-start(bf16[1,1,192,768]{3,2,1,0:T(8,128)(2,1)} %bitcast.25.mine_ref), channel_id=1, source_target_pairs={{0,2},{1,5},{2,0},{3,7},{4,6},{5,1},{6,4},{7,3},{8,10},{9,13},{10,... | collective-permute-start | bytes 884744 | tf_op jit(solution)/shard_map/ppermute | solution.py:80
  68.0 16.2 %copy-start.111 = (s32[2]{0:T(128)}, s32[2]{0:T(128)S(1)}, u32[]{:S(2)}) copy-start(s32[2]{0:T(128)S(1)} %get-tuple-element.482) | copy-start | bytes 28
  82.0 43.8 %collective-permute-start.12 = (bf16[2,2,192,768]{3,2,1,0:T(8,128)(2,1)S(1)}, bf16[2,2,192,768]{3,2,1,0:T(8,128)(2,1)}, u32[]{:S(2)}, u32[]{:S(2)}) collective-permute-start(bf16[2,2,192,768]{3,2,1,0:T(8,128)(2,1)S(1)} %bitcast.327), channel_id=1, source_target_pairs={{0,8},{1,9},{2,10},{3,11},{4,12},{5,13},{6,14},{7,15},{8,0},{9,1},... | collective-permute-start | bytes 3538952 | tf_op jit(solution)/shard_map/ppermute | solution.py:48
  82.8 48.3 %collective-permute-start.15 = (bf16[4,2,112,768]{3,2,1,0:T(8,128)(2,1)}, bf16[4,2,112,768]{3,2,1,0:T(8,128)(2,1)}, u32[]{:S(2)}, u32[]{:S(2)}) collective-permute-start(bf16[4,2,112,768]{3,2,1,0:T(8,128)(2,1)} %shard_map.174.mine_ref), channel_id=1, source_target_pairs={{0,4},{1,3},{2,6},{3,1},{4,0},{5,7},{6,2},{7,5},{8,12},{9,11},{10,... | collective-permute-start | bytes 4128776 | tf_op jit(solution)/shard_map/ppermute | solution.py:80
  85.4 16.9 %collective-permute-start.14 = (bf16[4,1,112,768]{3,2,1,0:T(8,128)(2,1)S(1)}, bf16[4,1,112,768]{3,2,1,0:T(8,128)(2,1)S(1)}, u32[]{:S(2)}, u32[]{:S(2)}) collective-permute-start(bf16[4,1,112,768]{3,2,1,0:T(8,128)(2,1)S(1)} %bitcast.345), channel_id=1, source_target_pairs={{0,2},{1,5},{2,0},{3,7},{4,6},{5,1},{6,4},{7,3},{8,10},{9,13},{10,... | collective-permute-start | bytes 2064392 | tf_op jit(solution)/shard_map/ppermute | solution.py:80
  86.1 32.3 %collective-permute-start.13 = (bf16[1,2,192,768]{3,2,1,0:T(8,128)(2,1)S(1)}, bf16[1,2,192,768]{3,2,1,0:T(8,128)(2,1)}, u32[]{:S(2)}, u32[]{:S(2)}) collective-permute-start(bf16[1,2,192,768]{3,2,1,0:T(8,128)(2,1)S(1)} %shard_map.173), channel_id=1, source_target_pairs={{0,16},{1,17},{2,18},{3,19},{4,20},{5,21},{6,22},{7,23},{8,24},{9,... | collective-permute-start | bytes 1769480 | tf_op jit(solution)/shard_map/ppermute | solution.py:48
  88.6 40.1 %collective-permute-start.4 = (bf16[256,768]{1,0:T(8,128)(2,1)}, bf16[256,768]{1,0:T(8,128)(2,1)}, u32[]{:S(2)}, u32[]{:S(2)}) collective-permute-start(bf16[256,768]{1,0:T(8,128)(2,1)} %param.12), channel_id=1, source_target_pairs={{0,1},{1,0},{2,3},{3,2},{4,5},{5,4},{6,7},{7,6},{8,9},{9,8},{10,11... | collective-permute-start | bytes 1179656 | tf_op jit(solution)/shard_map/ppermute | solution.py:48
  104.1 41.7 %collective-permute-start.17 = (bf16[4,2,112,768]{3,2,1,0:T(8,128)(2,1)}, bf16[4,2,112,768]{3,2,1,0:T(8,128)(2,1)}, u32[]{:S(2)}, u32[]{:S(2)}) collective-permute-start(bf16[4,2,112,768]{3,2,1,0:T(8,128)(2,1)} %shard_map.177.mine_ref), channel_id=1, source_target_pairs={{0,4},{1,3},{2,6},{3,1},{4,0},{5,7},{6,2},{7,5},{8,12},{9,11},{10,... | collective-permute-start | bytes 4128776 | tf_op jit(solution)/shard_map/ppermute | solution.py:80
  120.5 50.2 %collective-permute-start.24 = (bf16[2,2,192,768]{3,2,1,0:T(8,128)(2,1)}, bf16[2,2,192,768]{3,2,1,0:T(8,128)(2,1)}, u32[]{:S(2)}, u32[]{:S(2)}) collective-permute-start(bf16[2,2,192,768]{3,2,1,0:T(8,128)(2,1)} %bitcast.39), channel_id=1, source_target_pairs={{0,8},{1,9},{2,10},{3,11},{4,12},{5,13},{6,14},{7,15},{8,0},{9,1},... | collective-permute-start | bytes 3538952 | tf_op jit(solution)/shard_map/ppermute | solution.py:48
  127.4 46.5 %collective-permute-start.19 = (bf16[4,2,192,768]{3,2,1,0:T(8,128)(2,1)S(1)}, bf16[4,2,192,768]{3,2,1,0:T(8,128)(2,1)}, u32[]{:S(2)}, u32[]{:S(2)}) collective-permute-start(bf16[4,2,192,768]{3,2,1,0:T(8,128)(2,1)S(1)} %bitcast.305), channel_id=1, source_target_pairs={{0,4},{1,3},{2,6},{3,1},{4,0},{5,7},{6,2},{7,5},{8,12},{9,11},{10,... | collective-permute-start | bytes 7077896 | tf_op jit(solution)/shard_map/ppermute | solution.py:80
  136.6 7.2 %collective-permute-start.16 = (bf16[8,24,768]{2,1,0:T(8,128)(2,1)}, bf16[8,24,768]{2,1,0:T(8,128)(2,1)}, u32[]{:S(2)}, u32[]{:S(2)}) collective-permute-start(bf16[8,24,768]{2,1,0:T(8,128)(2,1)} %dynamic-slice_bitcast_fusion.3), channel_id=1, source_target_pairs={{0,1},{1,0},{2,3},{3,2},{4,5},{5,4},{6,7},{7,6},{8,9},{9,8},{10,11... | collective-permute-start | bytes 884744 | tf_op jit(solution)/shard_map/ppermute | solution.py:48
  154.5 31.9 %copy-start.13 = (bf16[16,2,24,384]{3,2,1,0:T(8,128)(2,1)}, bf16[16,2,24,384]{3,2,1,0:T(8,128)(2,1)S(1)}, u32[]{:S(2)}) copy-start(bf16[16,2,24,384]{3,2,1,0:T(8,128)(2,1)S(1)} %copy.58) | copy-start | bytes 1769476
  156.8 26.7 %collective-permute-start.21 = (bf16[8,24,768]{2,1,0:T(8,128)(2,1)S(1)}, bf16[8,24,768]{2,1,0:T(8,128)(2,1)S(1)}, u32[]{:S(2)}, u32[]{:S(2)}) collective-permute-start(bf16[8,24,768]{2,1,0:T(8,128)(2,1)S(1)} %dynamic-slice_bitcast_fusion.2), channel_id=1, source_target_pairs={{0,1},{1,0},{2,3},{3,2},{4,5},{5,4},{6,7},{7,6},{8,9},{9,8},{10,11... | collective-permute-start | bytes 884744 | tf_op jit(solution)/shard_map/ppermute | solution.py:48
  170.1 3.7 collective-permute-start.18
  172.5 28.1 %collective-permute-start.25 = (bf16[4,2,192,768]{3,2,1,0:T(8,128)(2,1)S(1)}, bf16[4,2,192,768]{3,2,1,0:T(8,128)(2,1)S(1)}, u32[]{:S(2)}, u32[]{:S(2)}) collective-permute-start(bf16[4,2,192,768]{3,2,1,0:T(8,128)(2,1)S(1)} %bitcast.307), channel_id=1, source_target_pairs={{0,4},{1,3},{2,6},{3,1},{4,0},{5,7},{6,2},{7,5},{8,12},{9,11},{10,... | collective-permute-start | bytes 7077896 | tf_op jit(solution)/shard_map/ppermute | solution.py:80
  182.6 2.7 collective-permute-start.20
  186.4 12.4 %copy-start.45 = (bf16[512,768]{1,0:T(8,128)(2,1)}, bf16[512,768]{1,0:T(8,128)(2,1)S(1)}, u32[]{:S(2)}) copy-start(bf16[512,768]{1,0:T(8,128)(2,1)S(1)} %get-tuple-element.230.x_ref) | copy-start | bytes 2359300
  186.4 12.4 %copy-start.54 = (f32[512,768]{1,0:T(8,128)}, f32[512,768]{1,0:T(8,128)S(1)}, u32[]{:S(2)}) copy-start(f32[512,768]{1,0:T(8,128)S(1)} %get-tuple-element.229.refs_3_) | copy-start | bytes 4718596
  186.6 12.7 %copy-start.106 = (bf16[256,768]{1,0:T(8,128)(2,1)S(1)}, bf16[256,768]{1,0:T(8,128)(2,1)}, u32[]{:S(2)}) copy-start(bf16[256,768]{1,0:T(8,128)(2,1)} %param.21) | copy-start | bytes 1179652
  198.8 4.2 collective-permute-start.22
  199.3 2.5 collective-permute-start.23
  203.1 12.9 %copy-start.119 = (s32[2,1]{0,1:T(1,128)S(1)}, s32[2,1]{0,1:T(1,128)}, u32[]{:S(2)}) copy-start(s32[2,1]{0,1:T(1,128)} %fusion.118) | copy-start | bytes 28
  214.0 3.6 collective-permute-start.26
  237.8 7.2 %collective-permute-start.29 = (bf16[512,768]{1,0:T(8,128)(2,1)}, bf16[512,768]{1,0:T(8,128)(2,1)S(1)}, u32[]{:S(2)}, u32[]{:S(2)}) collective-permute-start(bf16[512,768]{1,0:T(8,128)(2,1)} %get-tuple-element.262.mine_ref), channel_id=1, source_target_pairs={{0,1},{1,0},{2,3},{3,2},{4,5},{5,4},{6,7},{7,6},{8,9},{9,8},{10,11... | collective-permute-start | bytes 2359304 | tf_op jit(solution)/shard_map/ppermute | solution.py:48
  240.2 34.9 %collective-permute-start.27 = (bf16[4,2,96,768]{3,2,1,0:T(8,128)(2,1)}, bf16[4,2,96,768]{3,2,1,0:T(8,128)(2,1)S(1)}, u32[]{:S(2)}, u32[]{:S(2)}) collective-permute-start(bf16[4,2,96,768]{3,2,1,0:T(8,128)(2,1)} %copy-done.79), channel_id=1, source_target_pairs={{0,4},{1,3},{2,6},{3,1},{4,0},{5,7},{6,2},{7,5},{8,12},{9,11},{10,... | collective-permute-start | bytes 3538952 | tf_op jit(solution)/shard_map/ppermute | solution.py:80
  244.6 30.5 %collective-permute-start.28 = (bf16[4,2,96,768]{3,2,1,0:T(8,128)(2,1)S(1)}, bf16[4,2,96,768]{3,2,1,0:T(8,128)(2,1)S(1)}, u32[]{:S(2)}, u32[]{:S(2)}) collective-permute-start(bf16[4,2,96,768]{3,2,1,0:T(8,128)(2,1)S(1)} %shard_map.194), channel_id=1, source_target_pairs={{0,4},{1,3},{2,6},{3,1},{4,0},{5,7},{6,2},{7,5},{8,12},{9,11},{10,... | collective-permute-start | bytes 3538952 | tf_op jit(solution)/shard_map/ppermute | solution.py:80
  268.9 12.3 %collective-permute-start.31 = (bf16[512,768]{1,0:T(8,128)(2,1)S(1)}, bf16[512,768]{1,0:T(8,128)(2,1)}, u32[]{:S(2)}, u32[]{:S(2)}) collective-permute-start(bf16[512,768]{1,0:T(8,128)(2,1)S(1)} %get-tuple-element.284.refs_1_), channel_id=1, source_target_pairs={{0,1},{1,0},{2,3},{3,2},{4,5},{5,4},{6,7},{7,6},{8,9},{9,8},{10,11... | collective-permute-start | bytes 2359304 | tf_op jit(solution)/shard_map/ppermute | solution.py:48
  269.4 2.3 collective-permute-start.30
  273.8 34.8 %collective-permute-start.33 = (bf16[4,2,112,768]{3,2,1,0:T(8,128)(2,1)}, bf16[4,2,112,768]{3,2,1,0:T(8,128)(2,1)}, u32[]{:S(2)}, u32[]{:S(2)}) collective-permute-start(bf16[4,2,112,768]{3,2,1,0:T(8,128)(2,1)} %shard_map.196), channel_id=1, source_target_pairs={{0,4},{1,3},{2,6},{3,1},{4,0},{5,7},{6,2},{7,5},{8,12},{9,11},{10,... | collective-permute-start | bytes 4128776 | tf_op jit(solution)/shard_map/ppermute | solution.py:80
  278.7 52.2 %collective-permute-start.35 = (bf16[2,2,192,768]{3,2,1,0:T(8,128)(2,1)}, bf16[2,2,192,768]{3,2,1,0:T(8,128)(2,1)}, u32[]{:S(2)}, u32[]{:S(2)}) collective-permute-start(bf16[2,2,192,768]{3,2,1,0:T(8,128)(2,1)} %get-tuple-element.281), channel_id=1, source_target_pairs={{0,8},{1,9},{2,10},{3,11},{4,12},{5,13},{6,14},{7,15},{8,0},{9,1},... | collective-permute-start | bytes 3538952 | tf_op jit(solution)/shard_map/ppermute | solution.py:48
  301.1 9.4 %collective-permute-start.32 = (bf16[512,768]{1,0:T(8,128)(2,1)}, bf16[512,768]{1,0:T(8,128)(2,1)}, u32[]{:S(2)}, u32[]{:S(2)}) collective-permute-start(bf16[512,768]{1,0:T(8,128)(2,1)} %get-tuple-element.298.mine_ref), channel_id=1, source_target_pairs={{0,1},{1,0},{2,3},{3,2},{4,5},{5,4},{6,7},{7,6},{8,9},{9,8},{10,11... | collective-permute-start | bytes 2359304 | tf_op jit(solution)/shard_map/ppermute | solution.py:48
  303.8 30.8 %collective-permute-start.37 = (bf16[4,2,96,768]{3,2,1,0:T(8,128)(2,1)}, bf16[4,2,96,768]{3,2,1,0:T(8,128)(2,1)S(1)}, u32[]{:S(2)}, u32[]{:S(2)}) collective-permute-start(bf16[4,2,96,768]{3,2,1,0:T(8,128)(2,1)} %copy-done.78), channel_id=1, source_target_pairs={{0,4},{1,3},{2,6},{3,1},{4,0},{5,7},{6,2},{7,5},{8,12},{9,11},{10,... | collective-permute-start | bytes 3538952 | tf_op jit(solution)/shard_map/ppermute | solution.py:80
  307.9 26.7 %collective-permute-start.38 = (bf16[4,2,96,768]{3,2,1,0:T(8,128)(2,1)S(1)}, bf16[4,2,96,768]{3,2,1,0:T(8,128)(2,1)S(1)}, u32[]{:S(2)}, u32[]{:S(2)}) collective-permute-start(bf16[4,2,96,768]{3,2,1,0:T(8,128)(2,1)S(1)} %shard_map.201), channel_id=1, source_target_pairs={{0,4},{1,3},{2,6},{3,1},{4,0},{5,7},{6,2},{7,5},{8,12},{9,11},{10,... | collective-permute-start | bytes 3538952 | tf_op jit(solution)/shard_map/ppermute | solution.py:80
  312.6 19.5 %copy-start.49 = (f32[2,2,192,768]{3,2,1,0:T(8,128)S(1)}, f32[2,2,192,768]{3,2,1,0:T(8,128)}, u32[]{:S(2)}) copy-start(f32[2,2,192,768]{3,2,1,0:T(8,128)} %copy-done.48) | copy-start | bytes 7077892
  312.6 22.0 %copy-start.30 = (bf16[768,768]{1,0:T(8,128)(2,1)S(1)}, bf16[768,768]{1,0:T(8,128)(2,1)}, u32[]{:S(2)}) copy-start(bf16[768,768]{1,0:T(8,128)(2,1)} %copy-done.28) | copy-start | bytes 3538948
  335.7 1.9 collective-permute-start.40
  336.4 25.2 %collective-permute-start.39 = (bf16[4,1,192,768]{3,2,1,0:T(8,128)(2,1)S(1)}, bf16[4,1,192,768]{3,2,1,0:T(8,128)(2,1)S(1)}, u32[]{:S(2)}, u32[]{:S(2)}) collective-permute-start(bf16[4,1,192,768]{3,2,1,0:T(8,128)(2,1)S(1)} %get-tuple-element.313), channel_id=1, source_target_pairs={{0,2},{1,5},{2,0},{3,7},{4,6},{5,1},{6,4},{7,3},{8,10},{9,13},{10,... | collective-permute-start | bytes 3538952 | tf_op jit(solution)/shard_map/ppermute | solution.py:80
  338.5 31.3 %collective-permute-start.42 = (bf16[4,2,112,768]{3,2,1,0:T(8,128)(2,1)S(1)}, bf16[4,2,112,768]{3,2,1,0:T(8,128)(2,1)S(1)}, u32[]{:S(2)}, u32[]{:S(2)}) collective-permute-start(bf16[4,2,112,768]{3,2,1,0:T(8,128)(2,1)S(1)} %shard_map.206), channel_id=1, source_target_pairs={{0,4},{1,3},{2,6},{3,1},{4,0},{5,7},{6,2},{7,5},{8,12},{9,11},{10,... | collective-permute-start | bytes 4128776 | tf_op jit(solution)/shard_map/ppermute | solution.py:80
  339.4 29.7 %collective-permute-start.43 = (bf16[2,2,112,768]{3,2,1,0:T(8,128)(2,1)S(1)}, bf16[2,2,112,768]{3,2,1,0:T(8,128)(2,1)S(1)}, u32[]{:S(2)}, u32[]{:S(2)}) collective-permute-start(bf16[2,2,112,768]{3,2,1,0:T(8,128)(2,1)S(1)} %get-tuple-element.297), channel_id=1, source_target_pairs={{0,8},{1,9},{2,10},{3,11},{4,12},{5,13},{6,14},{7,15},{8,0},{9,1},... | collective-permute-start | bytes 2064392 | tf_op jit(solution)/shard_map/ppermute | solution.py:48
  341.2 49.5 %collective-permute-start.36 = (bf16[1,2,192,768]{3,2,1,0:T(8,128)(2,1)}, bf16[1,2,192,768]{3,2,1,0:T(8,128)(2,1)}, u32[]{:S(2)}, u32[]{:S(2)}) collective-permute-start(bf16[1,2,192,768]{3,2,1,0:T(8,128)(2,1)} %get-tuple-element.309), channel_id=1, source_target_pairs={{0,16},{1,17},{2,18},{3,19},{4,20},{5,21},{6,22},{7,23},{8,24},{9,... | collective-permute-start | bytes 1769480 | tf_op jit(solution)/shard_map/ppermute | solution.py:48
  364.2 23.3 %collective-permute-start.41 = (bf16[2,1,192,768]{3,2,0,1:T(8,128)(2,1)}, bf16[2,1,192,768]{3,2,0,1:T(8,128)(2,1)}, u32[]{:S(2)}, u32[]{:S(2)}) collective-permute-start(bf16[2,1,192,768]{3,2,0,1:T(8,128)(2,1)} %bitcast.143), channel_id=1, source_target_pairs={{0,8},{1,9},{2,10},{3,11},{4,12},{5,13},{6,14},{7,15},{8,0},{9,1},... | collective-permute-start | bytes 1769480 | tf_op jit(solution)/shard_map/ppermute | solution.py:48
  366.7 28.0 %collective-permute-start.34 = (bf16[256,768]{1,0:T(8,128)(2,1)}, bf16[256,768]{1,0:T(8,128)(2,1)}, u32[]{:S(2)}, u32[]{:S(2)}) collective-permute-start(bf16[256,768]{1,0:T(8,128)(2,1)} %get-tuple-element.495), channel_id=1, source_target_pairs={{0,1},{1,0},{2,3},{3,2},{4,5},{5,4},{6,7},{7,6},{8,9},{9,8},{10,11... | collective-permute-start | bytes 1179656 | tf_op jit(solution)/shard_map/ppermute | solution.py:48
  371.5 25.6 %collective-permute-start.46 = (bf16[4,1,112,768]{3,2,1,0:T(8,128)(2,1)}, bf16[4,1,112,768]{3,2,1,0:T(8,128)(2,1)}, u32[]{:S(2)}, u32[]{:S(2)}) collective-permute-start(bf16[4,1,112,768]{3,2,1,0:T(8,128)(2,1)} %get-tuple-element.331), channel_id=1, source_target_pairs={{0,2},{1,5},{2,0},{3,7},{4,6},{5,1},{6,4},{7,3},{8,10},{9,13},{10,... | collective-permute-start | bytes 2064392 | tf_op jit(solution)/shard_map/ppermute | solution.py:80
  372.5 27.6 %collective-permute-start.45 = (bf16[1,2,112,768]{3,2,1,0:T(8,128)(2,1)}, bf16[1,2,112,768]{3,2,1,0:T(8,128)(2,1)}, u32[]{:S(2)}, u32[]{:S(2)}) collective-permute-start(bf16[1,2,112,768]{3,2,1,0:T(8,128)(2,1)} %copy-done.101), channel_id=1, source_target_pairs={{0,16},{1,17},{2,18},{3,19},{4,20},{5,21},{6,22},{7,23},{8,24},{9,... | collective-permute-start | bytes 1032200 | tf_op jit(solution)/shard_map/ppermute | solution.py:48
  393.5 8.4 %collective-permute-start.44 = (bf16[1,1,192,768]{3,2,1,0:T(8,128)(2,1)}, bf16[1,1,192,768]{3,2,1,0:T(8,128)(2,1)}, u32[]{:S(2)}, u32[]{:S(2)}) collective-permute-start(bf16[1,1,192,768]{3,2,1,0:T(8,128)(2,1)} %get-tuple-element.336), channel_id=1, source_target_pairs={{0,2},{1,5},{2,0},{3,7},{4,6},{5,1},{6,4},{7,3},{8,10},{9,13},{10,... | collective-permute-start | bytes 884744 | tf_op jit(solution)/shard_map/ppermute | solution.py:80
  397.1 17.4 %collective-permute-start.53 = (bf16[1,1,192,768]{3,2,1,0:T(8,128)(2,1)S(1)}, bf16[1,1,192,768]{3,2,1,0:T(8,128)(2,1)S(1)}, u32[]{:S(2)}, u32[]{:S(2)}) collective-permute-start(bf16[1,1,192,768]{3,2,1,0:T(8,128)(2,1)S(1)} %get-tuple-element.333), channel_id=1, source_target_pairs={{0,16},{1,17},{2,18},{3,19},{4,20},{5,21},{6,22},{7,23},{8,24},{9,... | collective-permute-start | bytes 884744 | tf_op jit(solution)/shard_map/ppermute | solution.py:48
  398.4 15.0 %collective-permute-start.48 = (bf16[2,1,112,768]{3,2,0,1:T(8,128)(2,1)S(1)}, bf16[2,1,112,768]{3,2,0,1:T(8,128)(2,1)S(1)}, u32[]{:S(2)}, u32[]{:S(2)}) collective-permute-start(bf16[2,1,112,768]{3,2,0,1:T(8,128)(2,1)S(1)} %bitcast.381), channel_id=1, source_target_pairs={{0,8},{1,9},{2,10},{3,11},{4,12},{5,13},{6,14},{7,15},{8,0},{9,1},... | collective-permute-start | bytes 1032200 | tf_op jit(solution)/shard_map/ppermute | solution.py:48
  401.2 13.1 %collective-permute-start.50 = (bf16[1,1,112,768]{3,2,1,0:T(8,128)(2,1)S(1)}, bf16[1,1,112,768]{3,2,1,0:T(8,128)(2,1)S(1)}, u32[]{:S(2)}, u32[]{:S(2)}) collective-permute-start(bf16[1,1,112,768]{3,2,1,0:T(8,128)(2,1)S(1)} %get-tuple-element.342), channel_id=1, source_target_pairs={{0,2},{1,5},{2,0},{3,7},{4,6},{5,1},{6,4},{7,3},{8,10},{9,13},{10,... | collective-permute-start | bytes 516104 | tf_op jit(solution)/shard_map/ppermute | solution.py:80
  402.9 3.5 collective-permute-start.47
  414.0 10.8 %collective-permute-start.49 = (bf16[1,1,112,768]{3,2,1,0:T(8,128)(2,1)S(1)}, bf16[1,1,112,768]{3,2,1,0:T(8,128)(2,1)S(1)}, u32[]{:S(2)}, u32[]{:S(2)}) collective-permute-start(bf16[1,1,112,768]{3,2,1,0:T(8,128)(2,1)S(1)} %get-tuple-element.350), channel_id=1, source_target_pairs={{0,16},{1,17},{2,18},{3,19},{4,20},{5,21},{6,22},{7,23},{8,24},{9,... | collective-permute-start | bytes 516104 | tf_op jit(solution)/shard_map/ppermute | solution.py:48
  414.6 2.9 collective-permute-start.51
  416.6 8.9 %collective-permute-start.54 = (f32[24,1536]{1,0:T(8,128)S(1)}, f32[24,1536]{1,0:T(8,128)S(1)}, u32[]{:S(2)}, u32[]{:S(2)}) collective-permute-start(f32[24,1536]{1,0:T(8,128)S(1)} %get-tuple-element.533), channel_id=1, source_target_pairs={{0,1},{1,0},{2,3},{3,2},{4,5},{5,4},{6,7},{7,6},{8,9},{9,8},{10,11... | collective-permute-start | bytes 442376 | tf_op jit(solution)/shard_map/ppermute | solution.py:48
  424.9 3.6 collective-permute-start.52
  (114 other events, 318.9 us)

commit v2 on v1

--- a/solution.py
+++ b/solution.py
@@ -21,13 +21,13 @@
 UNIT = 1.48
 ATTN, FFN = 0, 1
 OPEN_SENDS = 5
-VMEM_LIMIT = 8 * 2**20
-EARLY = (False, False, True, True)
-LATE = (False, True, False, True)
+VMEM_LIMIT = 16 * 2**20
+EARLY = (False, False, False, False)
+LATE = (False, False, False, False)
 ORDER = (
-    0, 6, 16, 7, 1, 11, 2, 12, 21, 8, 17, 22, 9, 18, 13, 19, 23, 14, 3, 10, 15, 20, 26,
-    24, 25, 27, 28, 29, 4, 5, 30, 31, 33, 34, 35, 36, 37, 32, 47, 48, 42, 49, 38, 51, 50,
-    52, 43, 56, 53, 39, 57, 44, 40, 58, 45, 54, 41, 61, 46, 59, 55, 60,
+    0, 6, 1, 2, 11, 7, 16, 8, 3, 12, 21, 9, 13, 17, 14, 10, 22, 23, 18, 26, 15, 19, 27,
+    28, 24, 20, 4, 29, 25, 30, 5, 31, 33, 34, 35, 36, 37, 47, 48, 49, 38, 42, 51, 39, 43,
+    50, 52, 44, 61, 40, 56, 53, 45, 57, 58, 54, 59, 32, 55, 60, 41, 46,
 )
 
 
@@ -67,6 +67,7 @@
         self.step = self.count // 4
         self.top = self.chip // self.step
         self.low = list(range(self.count.bit_length() - 3))
+        self.info = self.table()
 
     def bit(self, place):
         return (self.chip // 2**place) % 2
@@ -79,11 +80,23 @@
         pairs = [(source, source ^ masks[source % 2]) for source in range(2 * self.count)]
         return lax.ppermute(value, AXIS, pairs)
 
-    def half_places(self, step, own):
-        bit = self.plane_bit(step)
-        bit = bit if own else 1 - bit
-        index = jnp.arange(2**step)
-        return jnp.where(self.core == 0, 2**step * bit + index, 2 * index + bit)
+    def table(self):
+        bits = [self.plane_bit(step) for step in range(len(self.low))]
+        entries = [self.core] + bits + [self.top % 2, self.top // 2]
+        return jnp.stack(entries).astype(jnp.int32)
+
+
+def half_place(table, step, index, own):
+    bit = table[1 + step]
+    bit = bit if own else 1 - bit
+    return jnp.where(table[0] == 0, 2**step * bit + index, 2 * index + bit)
+
+
+def merge_place(table, kind, step, low, half, index, own):
+    if kind == "low":
+        return half_place(table, step, index, own)
+    bit = table[low + step]
+    return half * (bit if own else 1 - bit) + index
 
 
 class Sequence:
@@ -184,11 +197,10 @@
         coming = self.sequence.gate(self.coming)
         kind, step = self.steps.pop(0)
         if kind == "low":
-            return merge_rows(self.held, coming, chips.plane_bit(step), chips.core, ranges)
+            return merge_rows(chips, kind, step, self.held, coming, ranges)
         lead, half, height, width = self.held.shape
         flat = [value.reshape(lead, 1, half * height, width) for value in (self.held, coming)]
-        bit = chips.top // 2 if step == 2 else chips.top % 2
-        return merge_rows(*flat, bit, 0).reshape(2 * lead, half, height, width)
+        return merge_rows(chips, kind, step, *flat).reshape(2 * lead, half, height, width)
 
     def advance(self):
         self.held = self.merged()
@@ -204,41 +216,38 @@
         return results
 
 
-def merge_kernel(ranges, place_ref, mine_ref, theirs_ref, *out_refs):
-    half = mine_ref.shape[1]
-    for lead in range(mine_ref.shape[0]):
-        for index in range(half):
+def merge_kernel(ranges, place, table_ref, mine_ref, theirs_ref, *out_refs):
+    for index in range(mine_ref.shape[1]):
+        own, other = place(table_ref, index, True), place(table_ref, index, False)
+        for lead in range(mine_ref.shape[0]):
             for (start, stop), out_ref in zip(ranges, out_refs):
-                out_ref[lead, place_ref[index]] = mine_ref[lead, index, start:stop]
-                out_ref[lead, place_ref[half + index]] = theirs_ref[lead, index, start:stop]
-
-
-def merge_rows(mine, theirs, bit, inner, ranges=None):
+                out_ref[lead, own] = mine_ref[lead, index, start:stop]
+                out_ref[lead, other] = theirs_ref[lead, index, start:stop]
+
+
+def merge_rows(chips, kind, step, mine, theirs, ranges=None):
     half = mine.shape[1]
     cuts = ranges or [(0, mine.shape[2])]
+
+    def place(table, index, own):
+        return merge_place(table, kind, step, len(chips.low), half, index, own)
+
+    shapes = [
+        jax.ShapeDtypeStruct((mine.shape[0], 2 * half, stop - start, mine.shape[3]), BF)
+        for start, stop in cuts
+    ]
     if all(edge % 16 == 0 for cut in cuts for edge in cut):
-        index = jnp.arange(half)
-
-        def place(own):
-            return jnp.where(inner == 1, 2 * index + own, half * own + index)
-
-        places = jnp.concatenate([place(bit), place(1 - bit)]).astype(jnp.int32)
-        shapes = [
-            jax.ShapeDtypeStruct((mine.shape[0], 2 * half, stop - start, mine.shape[3]), BF)
-            for start, stop in cuts
-        ]
         results = kernel_call(
-            functools.partial(merge_kernel, cuts), shapes, [], places, mine, theirs
+            functools.partial(merge_kernel, cuts, place), shapes, [], chips.info, mine, theirs
         )
     else:
+        sides = [place(chips.info, jnp.arange(half), own) for own in (True, False)]
         results = []
-        for start, stop in cuts:
-            cut = [value[:, :, start:stop] for value in (mine, theirs)]
-            outer = merge(*cut, bit, 1)
-            outer = outer.reshape((mine.shape[0], 2 * half) + outer.shape[3:])
-            results.append(
-                jnp.where(inner == 1, merge(*cut, bit, 2).reshape(outer.shape), outer)
-            )
+        for (start, stop), shape in zip(cuts, shapes):
+            whole = jnp.zeros(shape.shape, BF)
+            for side, value in zip(sides, (mine, theirs)):
+                whole = whole.at[:, side].set(value[:, :, start:stop])
+            results.append(whole)
     return results if ranges else results[0]
 
 
@@ -258,34 +267,26 @@
         shape = (4, 2 ** len(chips.low))
         arrays = [value.reshape(shape + value.shape[1:]) for value in arrays]
         self.arrays[part] = arrays
-        sent = send_rows(arrays, chips.half_places(step, False))
+        sent = send_rows(chips, step, arrays)
         self.coming[part] = chips.plane_swap(sent, step)
         self.sent = sent
 
     def advance(self):
         chips = self.chips
         coming = self.sequence.gate(self.coming)
-        if self.heights is None:
+        first = self.heights is None
+        if first:
             self.heights = [value.shape[2] for part in self.arrays for value in part]
-            kept = chips.half_places(len(chips.low) - 1, True)
         else:
             self.arrays, coming = [[self.kept]], [coming]
-            kept = jnp.arange(self.kept.shape[1])
         kind, step = self.steps.pop(0)
-        if kind == "low":
-            sides = [chips.half_places(step, own) for own in (False, True)]
-        else:
-            bit = chips.top // 2 if step == 2 else chips.top % 2
-            lead, places = self.arrays[0][0].shape[:2]
-            half = coming[0].shape[1]
+        if kind == "top":
             self.arrays = [
-                [value.reshape((lead // 2, 2 * places) + value.shape[2:]) for value in part]
+                [value.reshape((-1, 2 * value.shape[1]) + value.shape[2:]) for value in part]
                 for part in self.arrays
             ]
-            coming = [got.reshape((lead // 2, 2 * half) + got.shape[2:]) for got in coming]
-            kept = jnp.concatenate([kept, places + kept])
-            sides = [half * which + jnp.arange(half) for which in (1 - bit, bit)]
-        sent, self.kept = fold_rows(self.arrays, coming, kept, sides)
+            coming = [got.reshape((-1, 2 * got.shape[1]) + got.shape[2:]) for got in coming]
+        sent, self.kept = fold_rows(chips, kind, step, first, self.arrays, coming)
         self.sequence.mark(sent)
         if kind == "low":
             self.coming = chips.plane_swap(sent, step)
@@ -300,43 +301,44 @@
         return [total[start:stop] for start, stop in zip(ends[:-1], ends[1:])]
 
 
-def send_kernel(heights, place_ref, *refs):
+def send_kernel(step, heights, table_ref, *refs):
     *array_refs, sent_ref = refs
-    for lead in range(sent_ref.shape[0]):
-        for index in range(sent_ref.shape[1]):
+    for index in range(sent_ref.shape[1]):
+        place = half_place(table_ref, step, index, False)
+        for lead in range(sent_ref.shape[0]):
             row = 0
             for height, ref in zip(heights, array_refs):
-                sent_ref[lead, index, row : row + height] = ref[lead, place_ref[index]]
+                sent_ref[lead, index, row : row + height] = ref[lead, place]
                 row += height
 
 
-def send_rows(arrays, places):
+def send_rows(chips, step, arrays):
     heights = [value.shape[2] for value in arrays]
-    shape = (arrays[0].shape[0], places.shape[0], sum(heights), arrays[0].shape[3])
+    shape = (arrays[0].shape[0], 2**step, sum(heights), arrays[0].shape[3])
     if any(height % 16 for height in heights):
+        places = half_place(chips.info, step, jnp.arange(2**step), False)
         return jnp.concatenate([jnp.take(value, places, axis=1) for value in arrays], axis=2)
     (sent,) = kernel_call(
-        functools.partial(send_kernel, heights), [jax.ShapeDtypeStruct(shape, BF)], [],
-        places.astype(jnp.int32), *arrays,
+        functools.partial(send_kernel, step, heights), [jax.ShapeDtypeStruct(shape, BF)], [],
+        chips.info, *arrays,
     )
     return sent
 
 
-def fold_kernel(layout, place_ref, *refs):
+def fold_kernel(layout, place, table_ref, *refs):
     *refs, sent_ref, kept_ref = refs
-    count = sent_ref.shape[1]
-    for lead in range(sent_ref.shape[0]):
-        for index in range(count):
-            for array, got, start, height, row in layout:
-                for side, out_ref in enumerate((sent_ref, kept_ref)):
-                    place = 2 * (count * side + index)
-                    mine = refs[array][lead, place_ref[place]]
-                    theirs = refs[got][lead, place_ref[place + 1], start : start + height]
+    for index in range(sent_ref.shape[1]):
+        for own, out_ref in enumerate((sent_ref, kept_ref)):
+            source, came = place(table_ref, index, own == 1)
+            for lead in range(sent_ref.shape[0]):
+                for array, got, start, height, row in layout:
+                    mine = refs[array][lead, source]
+                    theirs = refs[got][lead, came, start : start + height]
                     total = mine.astype(F32) + theirs.astype(F32)
                     out_ref[lead, index, row : row + height] = total.astype(out_ref.dtype)
 
 
-def fold_rows(parts, coming, kept, sides):
+def fold_rows(chips, kind, step, first, parts, coming):
     arrays = [value for part in parts for value in part]
     layout = []
     row = 0
@@ -347,19 +349,36 @@
             layout.append((len(layout), got, start, height, row))
             start += height
             row += height
-    shape = (arrays[0].shape[0], sides[0].shape[0], row, arrays[0].shape[3])
+    half = coming[0].shape[1] // 2
+    low = len(chips.low)
+
+    def place(table, index, own):
+        if kind == "low":
+            came = half_place(table, step, index, own)
+            return (half_place(table, low - 1, came, True) if first else came), came
+        bit = table[low + step]
+        bit = bit if own else 1 - bit
+        came = half * bit + index
+        if not first:
+            return came, came
+        return 2**low * bit + half_place(table, low - 1, index, True), came
+
+    shape = (arrays[0].shape[0], half, row, arrays[0].shape[3])
     if any(value.shape[2] % 16 for value in arrays):
-        totals = []
-        for array, got, start, height, _ in layout:
-            theirs = coming[got - len(arrays)][:, :, start : start + height]
-            totals.append(jnp.take(arrays[array], kept, axis=1).astype(F32) + theirs.astype(F32))
-        total = jnp.concatenate(totals, axis=2)
-        return [jnp.take(total, side, axis=1).astype(kind) for side, kind in zip(sides, (BF, F32))]
-    places = [jnp.stack([jnp.take(kept, side), side], axis=1).reshape(-1) for side in sides]
+        results = []
+        for own, dtype in ((False, BF), (True, F32)):
+            source, came = place(chips.info, jnp.arange(half), own)
+            totals = []
+            for array, got, start, height, _ in layout:
+                theirs = jnp.take(coming[got - len(arrays)], came, axis=1)
+                theirs = theirs[:, :, start : start + height].astype(F32)
+                totals.append(jnp.take(arrays[array], source, axis=1).astype(F32) + theirs)
+            results.append(jnp.concatenate(totals, axis=2).astype(dtype))
+        return results
     return kernel_call(
-        functools.partial(fold_kernel, layout),
+        functools.partial(fold_kernel, layout, place),
         [jax.ShapeDtypeStruct(shape, kind) for kind in (BF, F32)], [],
-        jnp.concatenate(places).astype(jnp.int32), *arrays, *coming,
+        chips.info, *arrays, *coming,
     )
 
 
@@ -764,7 +783,8 @@
         table = table + swap(table, 1)
         cols = merge(side(core), got, core, 1)
         for layer in range(LAYERS):
-            last = cols[layer, :, :, width:]
+            last = cols[layer, :, :, width:].reshape(2 * rows, half)
+            outs = jnp.concatenate([w_out[layer, :, :half], w_out[layer, :, half:]], axis=0)
             vectors = [table[8 * layer : 8 * layer + 8]]
             vectors += [units[layer : layer + 1, i * width :][:, :width] for i in range(panels)]
             vectors.append(jnp.zeros((8 - panels, width), BF))
@@ -773,8 +793,7 @@
                 jnp.concatenate(
                     [
                         cols[layer, :, :, :width].reshape(2 * rows, width),
-                        jnp.concatenate([last[0], last[1]], axis=1),
-                        w_out[layer],
+                        jnp.concatenate([last, outs], axis=1),
                         *vectors,
                     ],
                     axis=0,
@@ -846,13 +865,14 @@
     def out_exchange(layer):
         ends = [0, 2 * rows, 4 * rows, 4 * rows + 16]
         first, second, table = state.gathers[ATTN, layer].finish(list(zip(ends[:-1], ends[1:])))
-        last, out_all = second[:, :rows], second[:, rows:]
-        w_b = jnp.swapaxes(last.reshape(count, rows, 2, half), 1, 2)
-        out_all = out_all.reshape(2, count // 2, rows, width)
-        sent, w_b = pick(out_all, 1 - core, 0), w_b.reshape(width, half)
+        w_b = second[:, :, :half].reshape(width, half)
+        out_all = second[:, :, half:].reshape(2, count // 2, 2 * rows, half)
+        sent = pick(out_all, 1 - core, 0)
         read_vectors(layer, table)
         sequence.mark((sent, w_b, state.vec[layer]))
-        full_out = merge(pick(out_all, core, 0), swap(sent, 1), core, 1).reshape(half, width)
+        parts = ordered(pick(out_all, core, 0), swap(sent, 1))
+        parts = [jnp.concatenate([part[:, :rows], part[:, rows:]], axis=2) for part in parts]
+        full_out = jnp.stack(parts, axis=1).reshape(half, width)
         state.w_attn[layer] = (first.reshape(width, width), w_b, full_out)
 
     def hidden_weights(layer):
@@ -958,9 +978,10 @@
         out_pair = g_out.reshape(count // 2, 2, rows, width)
         out_got = swap(pick(out_pair, 1 - core, 1), 1)
         out = merge(pick(out_pair, core, 1), out_got, core, 0).reshape(count, rows, width)
-        g_b = g_b.reshape(count, 2, rows, half)
-        last = jnp.concatenate([g_b[:, 0], g_b[:, 1]], axis=2)
-        rest = jnp.concatenate([last, out, sum_rows(layer)], axis=1)
+        g_b = g_b.reshape(count, 2 * rows, half)
+        out = jnp.concatenate([out[:, :, :half], out[:, :, half:]], axis=1)
+        rest = jnp.concatenate([g_b, out], axis=2)
+        rest = jnp.concatenate([rest, sum_rows(layer)], axis=1)
         rest = lax.optimization_barrier(rest)
         bundle.start(0, [g_a.reshape(count, 2 * rows, width), rest])
         sequence.mark(bundle.sent)
@@ -1008,11 +1029,10 @@
 
     def finish_attention(layer):
         first, rest = state.scatters[ATTN, layer].finish()
-        last, out, small = rest[:rows], rest[rows : 2 * rows], rest[2 * rows :]
+        last, out, small = rest[: 2 * rows, :half], rest[: 2 * rows, half:], rest[2 * rows :]
+        out = jnp.concatenate([out[:rows], out[rows:]], axis=1)
         sides = [
-            jnp.concatenate(
-                [first[side * rows :][:rows], last[:, side * half :][:, :half]], axis=1
-            )
+            jnp.concatenate([value[side * rows :][:rows] for value in (first, last)], axis=1)
             for side in range(2)
         ]
         mine, sent = ordered(*sides)
@@ -1090,7 +1110,7 @@
             if bits == "low":
                 links = plane(length)
             elif step == 2:
-                links = (("z", 2 * length), ("w", 4 * length + 1.5))
+                links = (("z", 2 * length), ("w", 5 * length + 1.5))
             else:
                 links = (("z", 2 * length),)
             sent = ("gx", kind, layer, number)
@@ -1164,7 +1184,7 @@
                 if bits == "low":
                     cost, links = cost + 1.4, plane(length)
                 elif step == 2:
-                    cost, links = cost + 2.8, (("z", 2 * length), ("w", 4 * length + 1.5))
+                    cost, links = cost + 2.8, (("z", 2 * length), ("w", 5 * length + 1.5))
                 else:
                     cost, links = cost + 1.4, (("z", 2 * length),)
                 sent = ("rx", kind, layer, number)

time: 438 us -> 375 us (0.86)
  local copies, waits for them, and re-layouts: 77.8 us -> 7.88 us
  waiting for transfers between devices: 128 us -> 156 us
  Pallas kernels: 135 us -> 114 us
  starting transfers between devices: 56.3 us -> 74.4 us
  other arithmetic: 26.1 us -> 11 us
    unnamed x298 -> x96, local copies, waits for them, and re-layouts: 55.8 us -> 4.34 us
    ppermute x18, waiting for transfers between devices: 40.1 us -> 78.2 us  [plane_swap(): return lax.ppermute(value, AXIS, pairs)]
    pallas_call x46, Pallas kernels: 135 us -> 114 us  [kernel_call(): pl.pallas_call(body, out_shape=shapes, in_specs=[in_smem if value.dtype =...]
    ppermute x37, starting transfers between devices: 40.7 us -> 58 us  [swap(): return lax.ppermute(value, AXIS, pairs)]
    ppermute x37, waiting for transfers between devices: 87.8 us -> 77.9 us  [swap(): return lax.ppermute(value, AXIS, pairs)]
    reshape x6 -> x0, local copies, waits for them, and re-layouts: 6.9 us -> none  [the longest x2 5.48 us: out_exchange(): w_b = jnp.swapaxes(last.reshape(count, rows, 2, half), 1, 2)]
  transfers between devices with their start and end apart: 55 -> 55, of which waited for: 19 -> 26; matrix products, arithmetic and copies ran while one was open for 11% -> 3% of each run, Pallas kernels for 27% -> 28%
where the time goes in v2:
time: 375 us; the launch traced here: 370 us
  waiting for transfers between devices  156 us (42%)
  Pallas kernels  114 us (30%)
  starting transfers between devices  74.4 us (20%)
  other arithmetic  11 us (3%)
  local copies, waits for them, and re-layouts  7.88 us (2%)
    pallas_call x46, Pallas kernels, kernel_call(): pl.pallas_call(body, out_shape=shapes, in_specs=[in_smem if value.dtype =...  114 us
    ppermute x18, waiting for transfers between devices, plane_swap(): return lax.ppermute(value, AXIS, pairs)  78.2 us
    ppermute x37, waiting for transfers between devices, swap(): return lax.ppermute(value, AXIS, pairs)  77.9 us
    ppermute x37, starting transfers between devices, swap(): return lax.ppermute(value, AXIS, pairs)  58 us
    ppermute x18, starting transfers between devices, plane_swap(): return lax.ppermute(value, AXIS, pairs)  16.4 us
  transfers between devices with their start and end apart: 55, of which 26 were waited for; matrix products, arithmetic and copies ran while one was open for 3% of the time, Pallas kernels for 28%

profile of v2, /device:TPU:1, one launch (start us, length us, event | category | flops | bytes accessed | tf_op | source)
XLA Modules:
  0.0 370.4 jit_solution(1423618175598771685)
XLA Ops:
  5.1 3.5 collective-permute-start.4
  9.6 7.1 %collective-permute-done.4.theirs_ref = bf16[1,1,112,768]{3,2,1,0:T(8,128)(2,1)S(1)} collective-permute-done((bf16[1,1,112,768]{3,2,1,0:T(8,128)(2,1)S(1)}, bf16[1,1,112,768]{3,2,1,0:T(8,128)(2,1)S(1)}, u32[]{:S(2)}, u32[]{:S(2)}) %collective-permute-start.4) | collective-permute-done | bytes 172064 | tf_op jit(solution)/shard_map/ppermute | solution.py:48
  18.2 3.1 collective-permute-start.7
  21.3 11.1 %collective-permute-done.5.theirs_ref = bf16[2,1,112,768]{3,2,1,0:T(8,128)(2,1)S(1)} collective-permute-done((bf16[2,1,112,768]{3,2,1,0:T(8,128)(2,1)S(1)}, bf16[2,1,112,768]{3,2,1,0:T(8,128)(2,1)S(1)}, u32[]{:S(2)}, u32[]{:S(2)}) %collective-permute-start.5) | collective-permute-done | bytes 344096 | tf_op jit(solution)/shard_map/ppermute | solution.py:48
  34.6 1.8 collective-permute-start.9
  36.3 6.9 %collective-permute-done.6.theirs_ref = bf16[4,1,112,768]{3,2,1,0:T(8,128)(2,1)S(1)} collective-permute-done((bf16[4,1,112,768]{3,2,1,0:T(8,128)(2,1)S(1)}, bf16[4,1,112,768]{3,2,1,0:T(8,128)(2,1)S(1)}, u32[]{:S(2)}, u32[]{:S(2)}) %collective-permute-start.6) | collective-permute-done | bytes 688160 | tf_op jit(solution)/shard_map/ppermute | solution.py:81
  44.5 3.5 collective-permute-done.9.theirs_ref
  48.6 1.3 collective-permute-start.10
  49.9 1.7 collective-permute-start.11
  53.0 2.1 collective-permute-done.11.theirs_ref
  55.6 11.9 %collective-permute-start.13 = (bf16[2,1,112,768]{3,2,1,0:T(8,128)(2,1)S(1)}, bf16[2,1,112,768]{3,2,1,0:T(8,128)(2,1)S(1)}, u32[]{:S(2)}, u32[]{:S(2)}) collective-permute-start(bf16[2,1,112,768]{3,2,1,0:T(8,128)(2,1)S(1)} %bitcast.274), channel_id=1, source_target_pairs={{0,8},{1,9},{2,10},{3,11},{4,12},{5,13},{6,14},{7,15},{8,0},{9,1},... | collective-permute-start | bytes 1032200 | tf_op jit(solution)/shard_map/ppermute | solution.py:48
  67.5 9.2 %collective-permute-done.10.theirs_ref = bf16[4,1,192,768]{3,2,1,0:T(8,128)(2,1)S(1)} collective-permute-done((bf16[4,1,192,768]{3,2,1,0:T(8,128)(2,1)S(1)}, bf16[4,1,192,768]{3,2,1,0:T(8,128)(2,1)S(1)}, u32[]{:S(2)}, u32[]{:S(2)}) %collective-permute-start.10) | collective-permute-done | bytes 1179680 | tf_op jit(solution)/shard_map/ppermute | solution.py:81
  77.4 1.4 collective-permute-start.18
  81.4 13.5 %collective-permute-done.15.theirs_ref = bf16[2,1,192,768]{3,2,1,0:T(8,128)(2,1)S(1)} collective-permute-done((bf16[2,1,192,768]{3,2,1,0:T(8,128)(2,1)S(1)}, bf16[2,1,192,768]{3,2,1,0:T(8,128)(2,1)S(1)}, u32[]{:S(2)}, u32[]{:S(2)}) %collective-permute-start.15) | collective-permute-done | bytes 589856 | tf_op jit(solution)/shard_map/ppermute | solution.py:48
  96.2 1.3 collective-permute-start.17
  97.6 12.4 %shard_map.180 = (bf16[512,768]{1,0:T(8,128)(2,1)S(1)}, bf16[512,1152]{1,0:T(8,128)(2,1)S(1)}, bf16[512,384]{1,0:T(8,128)(2,1)S(1)}, f32[512,128]{1,0:T(8,128)S(1)}) custom-call(s32[1]{0:T(128)S(6)} %copy.100.kind_ref, bf16[512,768]{1,0:T(8,128)(2,1)S(1)} %get-tuple-element.206.x_ref, bf16[768,768]{1,0:T(8,128)(2,1)S(1)} %bitcast.254, ...), custom_call_target="tpu_custom_call" | custom-call | tf_op jit(solution)/shard_map/pallas_call | solution.py:642
  112.7 1.2 collective-permute-start.21
  114.9 4.5 %shard_map.183 = (f32[512,768]{1,0:T(8,128)S(1)}, f32[512,768]{1,0:T(8,128)S(1)}, bf16[512,768]{1,0:T(8,128)(2,1)S(1)}, bf16[512,1536]{1,0:T(8,128)(2,1)S(1)}, b...) custom-call(f32[512,768]{1,0:T(8,128)S(1)} %get-tuple-element.398.x_ref, ...), custom_call_target="tpu_custom_call" | custom-call | tf_op jit(solution)/shard_map/pallas_call | solution.py:642
  119.4 3.1 collective-permute-start.19
  122.5 1.9 collective-permute-done.19.theirs_ref
  125.5 13.5 %collective-permute-done.21.theirs_ref = bf16[4,1,192,768]{3,2,1,0:T(8,128)(2,1)S(1)} collective-permute-done((bf16[4,1,192,768]{3,2,1,0:T(8,128)(2,1)S(1)}, bf16[4,1,192,768]{3,2,1,0:T(8,128)(2,1)S(1)}, u32[]{:S(2)}, u32[]{:S(2)}) %collective-permute-start.21) | collective-permute-done | bytes 1179680 | tf_op jit(solution)/shard_map/ppermute | solution.py:81
  141.4 4.4 %collective-permute-start.22 = (bf16[8,48,384]{2,1,0:T(8,128)(2,1)S(1)}, bf16[8,48,384]{2,1,0:T(8,128)(2,1)S(1)}, u32[]{:S(2)}, u32[]{:S(2)}) collective-permute-start(bf16[8,48,384]{2,1,0:T(8,128)(2,1)S(1)} %dynamic-slice_bitcast_fusion.2), channel_id=1, source_target_pairs={{0,1},{1,0},{2,3},{3,2},{4,5},{5,4},{6,7},{7,6},{8,9},{9,8},{10,11... | collective-permute-start | bytes 884744 | tf_op jit(solution)/shard_map/ppermute | solution.py:48
  147.4 12.0 %shard_map.187 = (bf16[512,768]{1,0:T(8,128)(2,1)S(1)}, bf16[512,1152]{1,0:T(8,128)(2,1)S(1)}, bf16[512,384]{1,0:T(8,128)(2,1)S(1)}, f32[512,128]{1,0:T(8,128)S(1)}) custom-call(s32[1]{0:T(128)S(6)} %copy.100.kind_ref, bf16[512,768]{1,0:T(8,128)(2,1)S(1)} %get-tuple-element.230.x_ref, bf16[768,768]{1,0:T(8,128)(2,1)S(1)} %bitcast.258, ...), custom_call_target="tpu_custom_call" | custom-call | tf_op jit(solution)/shard_map/pallas_call | solution.py:642
  160.0 1.8 collective-permute-done.23.theirs_ref
  161.8 6.8 %collective-permute-done.24.theirs_ref = bf16[4,2,192,768]{3,2,1,0:T(8,128)(2,1)S(1)} collective-permute-done((bf16[4,2,192,768]{3,2,1,0:T(8,128)(2,1)S(1)}, bf16[4,2,192,768]{3,2,1,0:T(8,128)(2,1)S(1)}, u32[]{:S(2)}, u32[]{:S(2)}) %collective-permute-start.24) | collective-permute-done | bytes 2359328 | tf_op jit(solution)/shard_map/ppermute | solution.py:81
  169.4 4.7 %shard_map.189 = (f32[512,768]{1,0:T(8,128)S(1)}, f32[512,768]{1,0:T(8,128)S(1)}, bf16[512,768]{1,0:T(8,128)(2,1)S(1)}, bf16[512,1536]{1,0:T(8,128)(2,1)S(1)}, b...) custom-call(f32[512,768]{1,0:T(8,128)S(1)} %get-tuple-element.221.x_ref, ...), custom_call_target="tpu_custom_call" | custom-call | tf_op jit(solution)/shard_map/pallas_call | solution.py:642
  174.1 4.4 %collective-permute-start.25 = (bf16[512,768]{1,0:T(8,128)(2,1)S(1)}, bf16[512,768]{1,0:T(8,128)(2,1)S(1)}, u32[]{:S(2)}, u32[]{:S(2)}) collective-permute-start(bf16[512,768]{1,0:T(8,128)(2,1)S(1)} %get-tuple-element.245.mine_ref), channel_id=1, source_target_pairs={{0,1},{1,0},{2,3},{3,2},{4,5},{5,4},{6,7},{7,6},{8,9},{9,8},{10,11... | collective-permute-start | bytes 2359304 | tf_op jit(solution)/shard_map/ppermute | solution.py:48
  178.7 1.8 collective-permute-done.25.theirs_ref
  180.5 2.2 shard_map.190
  182.6 2.9 shard_map.191
  186.2 3.9 %shard_map.193 = (bf16[768,768]{1,0:T(8,128)(2,1)S(1)}, bf16[768,768]{1,0:T(8,128)(2,1)S(1)}, bf16[512,768]{1,0:T(8,128)(2,1)S(1)}, f32[1,1536]{1,0:T(1,128)S(1)}) custom-call(bf16[512,768]{1,0:T(8,128)(2,1)S(1)} %get-tuple-element.254.d_ffn_ref, bf16[512,1536]{1,0:T(8,128)(2,1)S(1)} %get-tuple-element.255.slope_ref, ...), custom_call_target="tpu_custom_call" | custom-call | tf_op jit(solution)/shard_map/pallas_call | solution.py:642
  193.0 16.9 %shard_map.195 = (bf16[768,768]{1,0:T(8,128)(2,1)S(1)}, bf16[768,384]{1,0:T(8,128)(2,1)S(1)}, bf16[384,768]{1,0:T(8,128)(2,1)S(1)}, bf16[512,768]{1,0:T(8,128)(2...) custom-call(s32[1]{0:T(128)S(6)} %copy.100.kind_ref, ...), custom_call_target="tpu_custom_call" | custom-call | tf_op jit(solution)/shard_map/pallas_call | solution.py:642
  210.9 2.1 collective-permute-done.31
  214.0 4.8 %collective-permute-done.30.refs_4_ = bf16[4,2,96,768]{3,2,1,0:T(8,128)(2,1)S(1)} collective-permute-done((bf16[4,2,96,768]{3,2,1,0:T(8,128)(2,1)S(1)}, bf16[4,2,96,768]{3,2,1,0:T(8,128)(2,1)S(1)}, u32[]{:S(2)}, u32[]{:S(2)}) %collective-permute-start.30) | collective-permute-done | bytes 1179680 | tf_op jit(solution)/shard_map/ppermute | solution.py:81
  219.8 1.3 collective-permute-start.34
  221.9 3.1 shard_map.198
  226.2 4.0 %shard_map.200 = (bf16[768,768]{1,0:T(8,128)(2,1)S(1)}, bf16[768,768]{1,0:T(8,128)(2,1)S(1)}, bf16[512,768]{1,0:T(8,128)(2,1)S(1)}, f32[1,1536]{1,0:T(1,128)S(1)}) custom-call(bf16[512,768]{1,0:T(8,128)(2,1)S(1)} %get-tuple-element.287.d_ffn_ref, bf16[512,1536]{1,0:T(8,128)(2,1)S(1)} %get-tuple-element.288.slope_ref, bf16[512,768]{1,0:T(8,128)(2,1)S(1)} %copy-done.5, ...), custom_call_target="tpu_custom_call" | custom-call | tf_op jit(solution)/shard_map/pallas_call | solution.py:642
  230.1 1.6 collective-permute-start.32
  233.9 16.9 %shard_map.202 = (bf16[768,768]{1,0:T(8,128)(2,1)S(1)}, bf16[768,384]{1,0:T(8,128)(2,1)S(1)}, bf16[384,768]{1,0:T(8,128)(2,1)S(1)}, bf16[512,768]{1,0:T(8,128)(2...) custom-call(s32[1]{0:T(128)S(6)} %copy.100.kind_ref, ...), custom_call_target="tpu_custom_call" | custom-call | tf_op jit(solution)/shard_map/pallas_call | solution.py:642
  254.1 1.7 collective-permute-start.48
  255.9 13.9 %collective-permute-done.37.refs_3_ = bf16[4,2,96,768]{3,2,1,0:T(8,128)(2,1)S(1)} collective-permute-done((bf16[4,2,96,768]{3,2,1,0:T(8,128)(2,1)S(1)}, bf16[4,2,96,768]{3,2,1,0:T(8,128)(2,1)S(1)}, u32[]{:S(2)}, u32[]{:S(2)}) %collective-permute-start.37) | collective-permute-done | bytes 1179680 | tf_op jit(solution)/shard_map/ppermute | solution.py:81
  269.7 13.9 %collective-permute-done.38.refs_4_ = bf16[4,2,96,768]{3,2,1,0:T(8,128)(2,1)S(1)} collective-permute-done((bf16[4,2,96,768]{3,2,1,0:T(8,128)(2,1)S(1)}, bf16[4,2,96,768]{3,2,1,0:T(8,128)(2,1)S(1)}, u32[]{:S(2)}, u32[]{:S(2)}) %collective-permute-start.38) | collective-permute-done | bytes 1179680 | tf_op jit(solution)/shard_map/ppermute | solution.py:81
  283.6 2.0 shard_map.205
  285.9 1.4 shard_map.206
  288.1 1.4 shard_map.207
  291.5 1.7 shard_map.208
  294.1 2.4 collective-permute-start.53
  296.4 9.1 %collective-permute-done.43 = bf16[4,1,192,768]{3,2,1,0:T(8,128)(2,1)} collective-permute-done((bf16[4,1,192,768]{3,2,1,0:T(8,128)(2,1)}, bf16[4,1,192,768]{3,2,1,0:T(8,128)(2,1)}, u32[]{:S(2)}, u32[]{:S(2)}) %collective-permute-start.43) | collective-permute-done | bytes 1179680 | tf_op jit(solution)/shard_map/ppermute | solution.py:81
  305.5 1.7 copy-done.3
  307.2 1.7 shard_map.210
  310.9 2.8 collective-permute-start.45
  313.7 2.0 add_add_fusion
  316.8 1.6 collective-permute-start.54
  318.4 1.7 shard_map.209
  320.1 1.4 collective-permute-start.41
  321.5 7.3 %collective-permute-done.45 = bf16[2,1,192,768]{3,2,0,1:T(8,128)(2,1)S(1)} collective-permute-done((bf16[2,1,192,768]{3,2,0,1:T(8,128)(2,1)S(1)}, bf16[2,1,192,768]{3,2,0,1:T(8,128)(2,1)S(1)}, u32[]{:S(2)}, u32[]{:S(2)}) %collective-permute-start.45) | collective-permute-done | bytes 589856 | tf_op jit(solution)/shard_map/ppermute | solution.py:48
  329.4 1.6 collective-permute-start.50
  331.1 1.8 collective-permute-start.52
  334.9 1.5 collective-permute-start.46
  336.6 13.9 %collective-permute-done.46 = bf16[2,1,112,768]{3,2,0,1:T(8,128)(2,1)S(1)} collective-permute-done((bf16[2,1,112,768]{3,2,0,1:T(8,128)(2,1)S(1)}, bf16[2,1,112,768]{3,2,0,1:T(8,128)(2,1)S(1)}, u32[]{:S(2)}, u32[]{:S(2)}) %collective-permute-start.46) | collective-permute-done | bytes 344096 | tf_op jit(solution)/shard_map/ppermute | solution.py:48
  351.3 1.2 collective-permute-start.51
  353.4 7.6 %collective-permute-done.47 = bf16[1,1,112,768]{3,2,1,0:T(8,128)(2,1)S(1)} collective-permute-done((bf16[1,1,112,768]{3,2,1,0:T(8,128)(2,1)S(1)}, bf16[1,1,112,768]{3,2,1,0:T(8,128)(2,1)S(1)}, u32[]{:S(2)}, u32[]{:S(2)}) %collective-permute-start.47) | collective-permute-done | bytes 172064 | tf_op jit(solution)/shard_map/ppermute | solution.py:48
  362.6 1.3 fusion.1
  365.2 1.3 fusion
  (350 shorter events, 57.8 us)
Async XLA Ops:
  2.1 1.7 collective-permute-start
  2.4 1.4 collective-permute-start.1
  4.7 4.2 %copy-start.15 = (bf16[256,768]{1,0:T(8,128)(2,1)S(1)}, bf16[256,768]{1,0:T(8,128)(2,1)}, u32[]{:S(2)}) copy-start(bf16[256,768]{1,0:T(8,128)(2,1)} %param.10) | copy-start | bytes 1179652
  4.7 3.9 %collective-permute-start.2 = (bf16[192,384]{1,0:T(8,128)(2,1)S(1)}, bf16[192,384]{1,0:T(8,128)(2,1)S(1)}, u32[]{:S(2)}, u32[]{:S(2)}) collective-permute-start(bf16[192,384]{1,0:T(8,128)(2,1)S(1)} %broadcast_select_fusion.8), channel_id=1, source_target_pairs={{0,1},{1,0},{2,3},{3,2},{4,5},{5,4},{6,7},{7,6},{8,9},{9,8},{10,11... | collective-permute-start | bytes 442376 | tf_op jit(solution)/shard_map/ppermute | solution.py:48
  5.1 11.6 %collective-permute-start.4 = (bf16[1,1,112,768]{3,2,1,0:T(8,128)(2,1)S(1)}, bf16[1,1,112,768]{3,2,1,0:T(8,128)(2,1)S(1)}, u32[]{:S(2)}, u32[]{:S(2)}) collective-permute-start(bf16[1,1,112,768]{3,2,1,0:T(8,128)(2,1)S(1)} %bitcast.289), channel_id=1, source_target_pairs={{0,16},{1,17},{2,18},{3,19},{4,20},{5,21},{6,22},{7,23},{8,24},{9,... | collective-permute-start | bytes 516104 | tf_op jit(solution)/shard_map/ppermute | solution.py:48
  8.9 24.9 %collective-permute-start.3 = (bf16[256,768]{1,0:T(8,128)(2,1)S(1)}, bf16[256,768]{1,0:T(8,128)(2,1)S(1)}, u32[]{:S(2)}, u32[]{:S(2)}) collective-permute-start(bf16[256,768]{1,0:T(8,128)(2,1)S(1)} %copy-done.15), channel_id=1, source_target_pairs={{0,1},{1,0},{2,3},{3,2},{4,5},{5,4},{6,7},{7,6},{8,9},{9,8},{10,11... | collective-permute-start | bytes 1179656 | tf_op jit(solution)/shard_map/ppermute | solution.py:48
  17.3 15.1 %collective-permute-start.5 = (bf16[2,1,112,768]{3,2,1,0:T(8,128)(2,1)S(1)}, bf16[2,1,112,768]{3,2,1,0:T(8,128)(2,1)S(1)}, u32[]{:S(2)}, u32[]{:S(2)}) collective-permute-start(bf16[2,1,112,768]{3,2,1,0:T(8,128)(2,1)S(1)} %bitcast.276), channel_id=1, source_target_pairs={{0,8},{1,9},{2,10},{3,11},{4,12},{5,13},{6,14},{7,15},{8,0},{9,1},... | collective-permute-start | bytes 1032200 | tf_op jit(solution)/shard_map/ppermute | solution.py:48
  18.2 15.7 %collective-permute-start.7 = (bf16[1,1,192,768]{3,2,1,0:T(8,128)(2,1)S(1)}, bf16[1,1,192,768]{3,2,1,0:T(8,128)(2,1)S(1)}, u32[]{:S(2)}, u32[]{:S(2)}) collective-permute-start(bf16[1,1,192,768]{3,2,1,0:T(8,128)(2,1)S(1)} %bitcast.299), channel_id=1, source_target_pairs={{0,16},{1,17},{2,18},{3,19},{4,20},{5,21},{6,22},{7,23},{8,24},{9,... | collective-permute-start | bytes 884744 | tf_op jit(solution)/shard_map/ppermute | solution.py:48
  33.0 10.1 %collective-permute-start.6 = (bf16[4,1,112,768]{3,2,1,0:T(8,128)(2,1)S(1)}, bf16[4,1,112,768]{3,2,1,0:T(8,128)(2,1)S(1)}, u32[]{:S(2)}, u32[]{:S(2)}) collective-permute-start(bf16[4,1,112,768]{3,2,1,0:T(8,128)(2,1)S(1)} %bitcast.264), channel_id=1, source_target_pairs={{0,2},{1,5},{2,0},{3,7},{4,6},{5,1},{6,4},{7,3},{8,10},{9,13},{10,... | collective-permute-start | bytes 2064392 | tf_op jit(solution)/shard_map/ppermute | solution.py:81
  34.6 13.4 %collective-permute-start.9 = (bf16[2,1,192,768]{3,2,1,0:T(8,128)(2,1)S(1)}, bf16[2,1,192,768]{3,2,1,0:T(8,128)(2,1)S(1)}, u32[]{:S(2)}, u32[]{:S(2)}) collective-permute-start(bf16[2,1,192,768]{3,2,1,0:T(8,128)(2,1)S(1)} %bitcast.268), channel_id=1, source_target_pairs={{0,8},{1,9},{2,10},{3,11},{4,12},{5,13},{6,14},{7,15},{8,0},{9,1},... | collective-permute-start | bytes 1769480 | tf_op jit(solution)/shard_map/ppermute | solution.py:48
  43.8 35.0 %collective-permute-start.8 = (bf16[4,2,112,768]{3,2,1,0:T(8,128)(2,1)S(1)}, bf16[4,2,112,768]{3,2,1,0:T(8,128)(2,1)S(1)}, u32[]{:S(2)}, u32[]{:S(2)}) collective-permute-start(bf16[4,2,112,768]{3,2,1,0:T(8,128)(2,1)S(1)} %shard_map.172.mine_ref), channel_id=1, source_target_pairs={{0,4},{1,3},{2,6},{3,1},{4,0},{5,7},{6,2},{7,5},{8,12},{9,11},{10,... | collective-permute-start | bytes 4128776 | tf_op jit(solution)/shard_map/ppermute | solution.py:81
  48.6 28.1 %collective-permute-start.10 = (bf16[4,1,192,768]{3,2,1,0:T(8,128)(2,1)S(1)}, bf16[4,1,192,768]{3,2,1,0:T(8,128)(2,1)S(1)}, u32[]{:S(2)}, u32[]{:S(2)}) collective-permute-start(bf16[4,1,192,768]{3,2,1,0:T(8,128)(2,1)S(1)} %bitcast.244), channel_id=1, source_target_pairs={{0,2},{1,5},{2,0},{3,7},{4,6},{5,1},{6,4},{7,3},{8,10},{9,13},{10,... | collective-permute-start | bytes 3538952 | tf_op jit(solution)/shard_map/ppermute | solution.py:81
  49.9 5.2 %collective-permute-start.11 = (bf16[1,1,112,768]{3,2,1,0:T(8,128)(2,1)S(1)}, bf16[1,1,112,768]{3,2,1,0:T(8,128)(2,1)S(1)}, u32[]{:S(2)}, u32[]{:S(2)}) collective-permute-start(bf16[1,1,112,768]{3,2,1,0:T(8,128)(2,1)S(1)} %bitcast.287), channel_id=1, source_target_pairs={{0,16},{1,17},{2,18},{3,19},{4,20},{5,21},{6,22},{7,23},{8,24},{9,... | collective-permute-start | bytes 516104 | tf_op jit(solution)/shard_map/ppermute | solution.py:48
  52.2 27.6 %collective-permute-start.14 = (bf16[1,1,192,768]{3,2,1,0:T(8,128)(2,1)S(1)}, bf16[1,1,192,768]{3,2,1,0:T(8,128)(2,1)S(1)}, u32[]{:S(2)}, u32[]{:S(2)}) collective-permute-start(bf16[1,1,192,768]{3,2,1,0:T(8,128)(2,1)S(1)} %bitcast.301), channel_id=1, source_target_pairs={{0,16},{1,17},{2,18},{3,19},{4,20},{5,21},{6,22},{7,23},{8,24},{9,... | collective-permute-start | bytes 884744 | tf_op jit(solution)/shard_map/ppermute | solution.py:48
  55.6 39.9 %collective-permute-start.13 = (bf16[2,1,112,768]{3,2,1,0:T(8,128)(2,1)S(1)}, bf16[2,1,112,768]{3,2,1,0:T(8,128)(2,1)S(1)}, u32[]{:S(2)}, u32[]{:S(2)}) collective-permute-start(bf16[2,1,112,768]{3,2,1,0:T(8,128)(2,1)S(1)} %bitcast.274), channel_id=1, source_target_pairs={{0,8},{1,9},{2,10},{3,11},{4,12},{5,13},{6,14},{7,15},{8,0},{9,1},... | collective-permute-start | bytes 1032200 | tf_op jit(solution)/shard_map/ppermute | solution.py:48
  77.4 36.6 %collective-permute-start.18 = (bf16[4,2,192,768]{3,2,1,0:T(8,128)(2,1)S(1)}, bf16[4,2,192,768]{3,2,1,0:T(8,128)(2,1)S(1)}, u32[]{:S(2)}, u32[]{:S(2)}) collective-permute-start(bf16[4,2,192,768]{3,2,1,0:T(8,128)(2,1)S(1)} %shard_map.175.mine_ref), channel_id=1, source_target_pairs={{0,4},{1,3},{2,6},{3,1},{4,0},{5,7},{6,2},{7,5},{8,12},{9,11},{10,... | collective-permute-start | bytes 7077896 | tf_op jit(solution)/shard_map/ppermute | solution.py:81
  79.7 1.6 collective-permute-start.12
  80.5 14.5 %collective-permute-start.15 = (bf16[2,1,192,768]{3,2,1,0:T(8,128)(2,1)S(1)}, bf16[2,1,192,768]{3,2,1,0:T(8,128)(2,1)S(1)}, u32[]{:S(2)}, u32[]{:S(2)}) collective-permute-start(bf16[2,1,192,768]{3,2,1,0:T(8,128)(2,1)S(1)} %bitcast.266), channel_id=1, source_target_pairs={{0,8},{1,9},{2,10},{3,11},{4,12},{5,13},{6,14},{7,15},{8,0},{9,1},... | collective-permute-start | bytes 1769480 | tf_op jit(solution)/shard_map/ppermute | solution.py:48
  96.2 14.8 %collective-permute-start.17 = (bf16[4,1,112,768]{3,2,1,0:T(8,128)(2,1)S(1)}, bf16[4,1,112,768]{3,2,1,0:T(8,128)(2,1)S(1)}, u32[]{:S(2)}, u32[]{:S(2)}) collective-permute-start(bf16[4,1,112,768]{3,2,1,0:T(8,128)(2,1)S(1)} %bitcast.262), channel_id=1, source_target_pairs={{0,2},{1,5},{2,0},{3,7},{4,6},{5,1},{6,4},{7,3},{8,10},{9,13},{10,... | collective-permute-start | bytes 2064392 | tf_op jit(solution)/shard_map/ppermute | solution.py:81
  110.1 4.8 %copy-start.8 = (bf16[512,384]{1,0:T(8,128)(2,1)}, bf16[512,384]{1,0:T(8,128)(2,1)S(1)}, u32[]{:S(2)}) copy-start(bf16[512,384]{1,0:T(8,128)(2,1)S(1)} %get-tuple-element.297.context_ref) | copy-start | bytes 1179652
  110.1 3.9 %collective-permute-start.16 = (bf16[512,768]{1,0:T(8,128)(2,1)S(1)}, bf16[512,768]{1,0:T(8,128)(2,1)S(1)}, u32[]{:S(2)}, u32[]{:S(2)}) collective-permute-start(bf16[512,768]{1,0:T(8,128)(2,1)S(1)} %get-tuple-element.211.mine_ref), channel_id=1, source_target_pairs={{0,1},{1,0},{2,3},{3,2},{4,5},{5,4},{6,7},{7,6},{8,9},{9,8},{10,11... | collective-permute-start | bytes 2359304 | tf_op jit(solution)/shard_map/ppermute | solution.py:48
  111.6 28.1 %collective-permute-start.20 = (bf16[4,2,112,768]{3,2,1,0:T(8,128)(2,1)S(1)}, bf16[4,2,112,768]{3,2,1,0:T(8,128)(2,1)S(1)}, u32[]{:S(2)}, u32[]{:S(2)}) collective-permute-start(bf16[4,2,112,768]{3,2,1,0:T(8,128)(2,1)S(1)} %shard_map.181.mine_ref), channel_id=1, source_target_pairs={{0,4},{1,3},{2,6},{3,1},{4,0},{5,7},{6,2},{7,5},{8,12},{9,11},{10,... | collective-permute-start | bytes 4128776 | tf_op jit(solution)/shard_map/ppermute | solution.py:81
  112.7 26.2 %collective-permute-start.21 = (bf16[4,1,192,768]{3,2,1,0:T(8,128)(2,1)S(1)}, bf16[4,1,192,768]{3,2,1,0:T(8,128)(2,1)S(1)}, u32[]{:S(2)}, u32[]{:S(2)}) collective-permute-start(bf16[4,1,192,768]{3,2,1,0:T(8,128)(2,1)S(1)} %bitcast.242), channel_id=1, source_target_pairs={{0,2},{1,5},{2,0},{3,7},{4,6},{5,1},{6,4},{7,3},{8,10},{9,13},{10,... | collective-permute-start | bytes 3538952 | tf_op jit(solution)/shard_map/ppermute | solution.py:81
  119.4 6.1 %copy-start.4 = (bf16[512,768]{1,0:T(8,128)(2,1)}, bf16[512,768]{1,0:T(8,128)(2,1)S(1)}, u32[]{:S(2)}) copy-start(bf16[512,768]{1,0:T(8,128)(2,1)S(1)} %get-tuple-element.289.normed_b_ref) | copy-start | bytes 2359300
  119.4 5.1 %collective-permute-start.19 = (bf16[512,768]{1,0:T(8,128)(2,1)S(1)}, bf16[512,768]{1,0:T(8,128)(2,1)S(1)}, u32[]{:S(2)}, u32[]{:S(2)}) collective-permute-start(bf16[512,768]{1,0:T(8,128)(2,1)S(1)} %get-tuple-element.219.mine_ref), channel_id=1, source_target_pairs={{0,1},{1,0},{2,3},{3,2},{4,5},{5,4},{6,7},{7,6},{8,9},{9,8},{10,11... | collective-permute-start | bytes 2359304 | tf_op jit(solution)/shard_map/ppermute | solution.py:48
  140.5 28.1 %collective-permute-start.24 = (bf16[4,2,192,768]{3,2,1,0:T(8,128)(2,1)S(1)}, bf16[4,2,192,768]{3,2,1,0:T(8,128)(2,1)S(1)}, u32[]{:S(2)}, u32[]{:S(2)}) collective-permute-start(bf16[4,2,192,768]{3,2,1,0:T(8,128)(2,1)S(1)} %shard_map.185.mine_ref), channel_id=1, source_target_pairs={{0,4},{1,3},{2,6},{3,1},{4,0},{5,7},{6,2},{7,5},{8,12},{9,11},{10,... | collective-permute-start | bytes 7077896 | tf_op jit(solution)/shard_map/ppermute | solution.py:81
  141.4 5.7 %collective-permute-start.22 = (bf16[8,48,384]{2,1,0:T(8,128)(2,1)S(1)}, bf16[8,48,384]{2,1,0:T(8,128)(2,1)S(1)}, u32[]{:S(2)}, u32[]{:S(2)}) collective-permute-start(bf16[8,48,384]{2,1,0:T(8,128)(2,1)S(1)} %dynamic-slice_bitcast_fusion.2), channel_id=1, source_target_pairs={{0,1},{1,0},{2,3},{3,2},{4,5},{5,4},{6,7},{7,6},{8,9},{9,8},{10,11... | collective-permute-start | bytes 884744 | tf_op jit(solution)/shard_map/ppermute | solution.py:48
  147.4 12.5 %copy-start.16 = (bf16[256,768]{1,0:T(8,128)(2,1)S(1)}, bf16[256,768]{1,0:T(8,128)(2,1)}, u32[]{:S(2)}) copy-start(bf16[256,768]{1,0:T(8,128)(2,1)} %param.19) | copy-start | bytes 1179652
  159.4 2.4 collective-permute-start.23
  159.9 18.7 %collective-permute-start.26 = (bf16[256,768]{1,0:T(8,128)(2,1)S(1)}, bf16[256,768]{1,0:T(8,128)(2,1)S(1)}, u32[]{:S(2)}, u32[]{:S(2)}) collective-permute-start(bf16[256,768]{1,0:T(8,128)(2,1)S(1)} %copy-done.16), channel_id=1, source_target_pairs={{0,1},{1,0},{2,3},{3,2},{4,5},{5,4},{6,7},{7,6},{8,9},{9,8},{10,11... | collective-permute-start | bytes 1179656 | tf_op jit(solution)/shard_map/ppermute | solution.py:48
  174.1 6.4 %collective-permute-start.25 = (bf16[512,768]{1,0:T(8,128)(2,1)S(1)}, bf16[512,768]{1,0:T(8,128)(2,1)S(1)}, u32[]{:S(2)}, u32[]{:S(2)}) collective-permute-start(bf16[512,768]{1,0:T(8,128)(2,1)S(1)} %get-tuple-element.245.mine_ref), channel_id=1, source_target_pairs={{0,1},{1,0},{2,3},{3,2},{4,5},{5,4},{6,7},{7,6},{8,9},{9,8},{10,11... | collective-permute-start | bytes 2359304 | tf_op jit(solution)/shard_map/ppermute | solution.py:48
  190.2 2.8 collective-permute-start.27
  190.7 23.2 %collective-permute-start.29 = (bf16[4,2,96,768]{3,2,1,0:T(8,128)(2,1)S(1)}, bf16[4,2,96,768]{3,2,1,0:T(8,128)(2,1)S(1)}, u32[]{:S(2)}, u32[]{:S(2)}) collective-permute-start(bf16[4,2,96,768]{3,2,1,0:T(8,128)(2,1)S(1)} %shard_map.192), channel_id=1, source_target_pairs={{0,4},{1,3},{2,6},{3,1},{4,0},{5,7},{6,2},{7,5},{8,12},{9,11},{10,... | collective-permute-start | bytes 3538952 | tf_op jit(solution)/shard_map/ppermute | solution.py:81
  192.2 26.6 %collective-permute-start.30 = (bf16[4,2,96,768]{3,2,1,0:T(8,128)(2,1)S(1)}, bf16[4,2,96,768]{3,2,1,0:T(8,128)(2,1)S(1)}, u32[]{:S(2)}, u32[]{:S(2)}) collective-permute-start(bf16[4,2,96,768]{3,2,1,0:T(8,128)(2,1)S(1)} %shard_map.194), channel_id=1, source_target_pairs={{0,4},{1,3},{2,6},{3,1},{4,0},{5,7},{6,2},{7,5},{8,12},{9,11},{10,... | collective-permute-start | bytes 3538952 | tf_op jit(solution)/shard_map/ppermute | solution.py:81
  209.9 12.0 %collective-permute-start.28 = (bf16[512,768]{1,0:T(8,128)(2,1)S(1)}, bf16[512,768]{1,0:T(8,128)(2,1)S(1)}, u32[]{:S(2)}, u32[]{:S(2)}) collective-permute-start(bf16[512,768]{1,0:T(8,128)(2,1)S(1)} %get-tuple-element.281.refs_1_), channel_id=1, source_target_pairs={{0,1},{1,0},{2,3},{3,2},{4,5},{5,4},{6,7},{7,6},{8,9},{9,8},{10,11... | collective-permute-start | bytes 2359304 | tf_op jit(solution)/shard_map/ppermute | solution.py:48
  210.7 2.3 collective-permute-start.31
  219.8 31.0 %collective-permute-start.34 = (bf16[4,1,192,768]{3,2,1,0:T(8,128)(2,1)S(1)}, bf16[4,1,192,768]{3,2,1,0:T(8,128)(2,1)S(1)}, u32[]{:S(2)}, u32[]{:S(2)}) collective-permute-start(bf16[4,1,192,768]{3,2,1,0:T(8,128)(2,1)S(1)} %get-tuple-element.280), channel_id=1, source_target_pairs={{0,2},{1,5},{2,0},{3,7},{4,6},{5,1},{6,4},{7,3},{8,10},{9,13},{10,... | collective-permute-start | bytes 3538952 | tf_op jit(solution)/shard_map/ppermute | solution.py:81
  221.1 31.8 %collective-permute-start.33 = (bf16[4,2,112,768]{3,2,1,0:T(8,128)(2,1)S(1)}, bf16[4,2,112,768]{3,2,1,0:T(8,128)(2,1)S(1)}, u32[]{:S(2)}, u32[]{:S(2)}) collective-permute-start(bf16[4,2,112,768]{3,2,1,0:T(8,128)(2,1)S(1)} %shard_map.196), channel_id=1, source_target_pairs={{0,4},{1,3},{2,6},{3,1},{4,0},{5,7},{6,2},{7,5},{8,12},{9,11},{10,... | collective-permute-start | bytes 4128776 | tf_op jit(solution)/shard_map/ppermute | solution.py:81
  230.1 3.8 %collective-permute-start.32 = (bf16[512,768]{1,0:T(8,128)(2,1)S(1)}, bf16[512,768]{1,0:T(8,128)(2,1)S(1)}, u32[]{:S(2)}, u32[]{:S(2)}) collective-permute-start(bf16[512,768]{1,0:T(8,128)(2,1)S(1)} %get-tuple-element.293.mine_ref), channel_id=1, source_target_pairs={{0,1},{1,0},{2,3},{3,2},{4,5},{5,4},{6,7},{7,6},{8,9},{9,8},{10,11... | collective-permute-start | bytes 2359304 | tf_op jit(solution)/shard_map/ppermute | solution.py:48
  231.7 38.0 %collective-permute-start.37 = (bf16[4,2,96,768]{3,2,1,0:T(8,128)(2,1)S(1)}, bf16[4,2,96,768]{3,2,1,0:T(8,128)(2,1)S(1)}, u32[]{:S(2)}, u32[]{:S(2)}) collective-permute-start(bf16[4,2,96,768]{3,2,1,0:T(8,128)(2,1)S(1)} %shard_map.199), channel_id=1, source_target_pairs={{0,4},{1,3},{2,6},{3,1},{4,0},{5,7},{6,2},{7,5},{8,12},{9,11},{10,... | collective-permute-start | bytes 3538952 | tf_op jit(solution)/shard_map/ppermute | solution.py:81
  233.1 50.5 %collective-permute-start.38 = (bf16[4,2,96,768]{3,2,1,0:T(8,128)(2,1)S(1)}, bf16[4,2,96,768]{3,2,1,0:T(8,128)(2,1)S(1)}, u32[]{:S(2)}, u32[]{:S(2)}) collective-permute-start(bf16[4,2,96,768]{3,2,1,0:T(8,128)(2,1)S(1)} %shard_map.201), channel_id=1, source_target_pairs={{0,4},{1,3},{2,6},{3,1},{4,0},{5,7},{6,2},{7,5},{8,12},{9,11},{10,... | collective-permute-start | bytes 3538952 | tf_op jit(solution)/shard_map/ppermute | solution.py:81
  252.0 33.9 %collective-permute-start.36 = (bf16[2,1,192,768]{3,2,0,1:T(8,128)(2,1)S(1)}, bf16[2,1,192,768]{3,2,0,1:T(8,128)(2,1)S(1)}, u32[]{:S(2)}, u32[]{:S(2)}) collective-permute-start(bf16[2,1,192,768]{3,2,0,1:T(8,128)(2,1)S(1)} %bitcast.304), channel_id=1, source_target_pairs={{0,8},{1,9},{2,10},{3,11},{4,12},{5,13},{6,14},{7,15},{8,0},{9,1},... | collective-permute-start | bytes 1769480 | tf_op jit(solution)/shard_map/ppermute | solution.py:48
  253.8 34.3 %collective-permute-start.35 = (bf16[4,1,112,768]{3,2,1,0:T(8,128)(2,1)S(1)}, bf16[4,1,112,768]{3,2,1,0:T(8,128)(2,1)S(1)}, u32[]{:S(2)}, u32[]{:S(2)}) collective-permute-start(bf16[4,1,112,768]{3,2,1,0:T(8,128)(2,1)S(1)} %get-tuple-element.308), channel_id=1, source_target_pairs={{0,2},{1,5},{2,0},{3,7},{4,6},{5,1},{6,4},{7,3},{8,10},{9,13},{10,... | collective-permute-start | bytes 2064392 | tf_op jit(solution)/shard_map/ppermute | solution.py:81
  254.1 59.6 %collective-permute-start.48 = (bf16[256,768]{1,0:T(8,128)(2,1)}, bf16[256,768]{1,0:T(8,128)(2,1)}, u32[]{:S(2)}, u32[]{:S(2)}) collective-permute-start(bf16[256,768]{1,0:T(8,128)(2,1)} %get-tuple-element.393), channel_id=1, source_target_pairs={{0,1},{1,0},{2,3},{3,2},{4,5},{5,4},{6,7},{7,6},{8,9},{9,8},{10,11... | collective-permute-start | bytes 1179656 | tf_op jit(solution)/shard_map/ppermute | solution.py:48
  285.6 19.9 %collective-permute-start.43 = (bf16[4,1,192,768]{3,2,1,0:T(8,128)(2,1)}, bf16[4,1,192,768]{3,2,1,0:T(8,128)(2,1)}, u32[]{:S(2)}, u32[]{:S(2)}) collective-permute-start(bf16[4,1,192,768]{3,2,1,0:T(8,128)(2,1)} %get-tuple-element.312), channel_id=1, source_target_pairs={{0,2},{1,5},{2,0},{3,7},{4,6},{5,1},{6,4},{7,3},{8,10},{9,13},{10,... | collective-permute-start | bytes 3538952 | tf_op jit(solution)/shard_map/ppermute | solution.py:81
  289.5 1.6 collective-permute-start.39
  289.9 18.9 %collective-permute-start.42 = (bf16[2,1,112,768]{3,2,0,1:T(8,128)(2,1)}, bf16[2,1,112,768]{3,2,0,1:T(8,128)(2,1)}, u32[]{:S(2)}, u32[]{:S(2)}) collective-permute-start(bf16[2,1,112,768]{3,2,0,1:T(8,128)(2,1)} %bitcast.94), channel_id=1, source_target_pairs={{0,8},{1,9},{2,10},{3,11},{4,12},{5,13},{6,14},{7,15},{8,0},{9,1},... | collective-permute-start | bytes 1032200 | tf_op jit(solution)/shard_map/ppermute | solution.py:48
  293.3 25.2 %collective-permute-start.40 = (bf16[4,2,112,768]{3,2,1,0:T(8,128)(2,1)}, bf16[4,2,112,768]{3,2,1,0:T(8,128)(2,1)}, u32[]{:S(2)}, u32[]{:S(2)}) collective-permute-start(bf16[4,2,112,768]{3,2,1,0:T(8,128)(2,1)} %shard_map.208), channel_id=1, source_target_pairs={{0,4},{1,3},{2,6},{3,1},{4,0},{5,7},{6,2},{7,5},{8,12},{9,11},{10,... | collective-permute-start | bytes 4128776 | tf_op jit(solution)/shard_map/ppermute | solution.py:81
  294.1 21.7 %collective-permute-start.53 = (bf16[1,1,192,768]{3,2,1,0:T(8,128)(2,1)}, bf16[1,1,192,768]{3,2,1,0:T(8,128)(2,1)}, u32[]{:S(2)}, u32[]{:S(2)}) collective-permute-start(bf16[1,1,192,768]{3,2,1,0:T(8,128)(2,1)} %get-tuple-element.314), channel_id=1, source_target_pairs={{0,16},{1,17},{2,18},{3,19},{4,20},{5,21},{6,22},{7,23},{8,24},{9,... | collective-permute-start | bytes 884744 | tf_op jit(solution)/shard_map/ppermute | solution.py:48
  307.2 6.6 %copy-start.11 = (f32[512,768]{1,0:T(8,128)S(1)}, f32[512,768]{1,0:T(8,128)}, u32[]{:S(2)}) copy-start(f32[512,768]{1,0:T(8,128)} %copy-done.10) | copy-start | bytes 4718596
  307.2 6.6 %copy-start.14 = (bf16[256,768]{1,0:T(8,128)(2,1)S(1)}, bf16[256,768]{1,0:T(8,128)(2,1)}, u32[]{:S(2)}) copy-start(bf16[256,768]{1,0:T(8,128)(2,1)} %get-tuple-element.345) | copy-start | bytes 1179652
  308.8 6.9 %copy-start.7 = (f32[1,1,192,768]{3,2,1,0:T(8,128)S(1)}, f32[1,1,192,768]{3,2,1,0:T(8,128)}, u32[]{:S(2)}) copy-start(f32[1,1,192,768]{3,2,1,0:T(8,128)} %copy-done.6) | copy-start | bytes 1769476
  310.0 19.4 %collective-permute-start.44 = (bf16[1,1,112,768]{3,2,1,0:T(8,128)(2,1)S(1)}, bf16[1,1,112,768]{3,2,1,0:T(8,128)(2,1)S(1)}, u32[]{:S(2)}, u32[]{:S(2)}) collective-permute-start(bf16[1,1,112,768]{3,2,1,0:T(8,128)(2,1)S(1)} %get-tuple-element.332), channel_id=1, source_target_pairs={{0,16},{1,17},{2,18},{3,19},{4,20},{5,21},{6,22},{7,23},{8,24},{9,... | collective-permute-start | bytes 516104 | tf_op jit(solution)/shard_map/ppermute | solution.py:48
  310.9 17.8 %collective-permute-start.45 = (bf16[2,1,192,768]{3,2,0,1:T(8,128)(2,1)S(1)}, bf16[2,1,192,768]{3,2,0,1:T(8,128)(2,1)S(1)}, u32[]{:S(2)}, u32[]{:S(2)}) collective-permute-start(bf16[2,1,192,768]{3,2,0,1:T(8,128)(2,1)S(1)} %bitcast.305), channel_id=1, source_target_pairs={{0,8},{1,9},{2,10},{3,11},{4,12},{5,13},{6,14},{7,15},{8,0},{9,1},... | collective-permute-start | bytes 1769480 | tf_op jit(solution)/shard_map/ppermute | solution.py:48
  316.8 48.2 %collective-permute-start.54 = (f32[24,1536]{1,0:T(8,128)S(1)}, f32[24,1536]{1,0:T(8,128)S(1)}, u32[]{:S(2)}, u32[]{:S(2)}) collective-permute-start(f32[24,1536]{1,0:T(8,128)S(1)} %get-tuple-element.441), channel_id=1, source_target_pairs={{0,1},{1,0},{2,3},{3,2},{4,5},{5,4},{6,7},{7,6},{8,9},{9,8},{10,11... | collective-permute-start | bytes 442376 | tf_op jit(solution)/shard_map/ppermute | solution.py:48
  320.1 14.1 %collective-permute-start.41 = (bf16[4,1,112,768]{3,2,1,0:T(8,128)(2,1)S(1)}, bf16[4,1,112,768]{3,2,1,0:T(8,128)(2,1)S(1)}, u32[]{:S(2)}, u32[]{:S(2)}) collective-permute-start(bf16[4,1,112,768]{3,2,1,0:T(8,128)(2,1)S(1)} %get-tuple-element.325), channel_id=1, source_target_pairs={{0,2},{1,5},{2,0},{3,7},{4,6},{5,1},{6,4},{7,3},{8,10},{9,13},{10,... | collective-permute-start | bytes 2064392 | tf_op jit(solution)/shard_map/ppermute | solution.py:81
  329.4 21.7 %collective-permute-start.50 = (bf16[1,1,192,768]{3,2,1,0:T(8,128)(2,1)S(1)}, bf16[1,1,192,768]{3,2,1,0:T(8,128)(2,1)S(1)}, u32[]{:S(2)}, u32[]{:S(2)}) collective-permute-start(bf16[1,1,192,768]{3,2,1,0:T(8,128)(2,1)S(1)} %get-tuple-element.335), channel_id=1, source_target_pairs={{0,16},{1,17},{2,18},{3,19},{4,20},{5,21},{6,22},{7,23},{8,24},{9,... | collective-permute-start | bytes 884744 | tf_op jit(solution)/shard_map/ppermute | solution.py:48
  331.1 2.8 collective-permute-start.52
  334.9 15.5 %collective-permute-start.46 = (bf16[2,1,112,768]{3,2,0,1:T(8,128)(2,1)S(1)}, bf16[2,1,112,768]{3,2,0,1:T(8,128)(2,1)S(1)}, u32[]{:S(2)}, u32[]{:S(2)}) collective-permute-start(bf16[2,1,112,768]{3,2,0,1:T(8,128)(2,1)S(1)} %bitcast.306), channel_id=1, source_target_pairs={{0,8},{1,9},{2,10},{3,11},{4,12},{5,13},{6,14},{7,15},{8,0},{9,1},... | collective-permute-start | bytes 1032200 | tf_op jit(solution)/shard_map/ppermute | solution.py:48
  351.1 9.9 %collective-permute-start.47 = (bf16[1,1,112,768]{3,2,1,0:T(8,128)(2,1)S(1)}, bf16[1,1,112,768]{3,2,1,0:T(8,128)(2,1)S(1)}, u32[]{:S(2)}, u32[]{:S(2)}) collective-permute-start(bf16[1,1,112,768]{3,2,1,0:T(8,128)(2,1)S(1)} %get-tuple-element.342), channel_id=1, source_target_pairs={{0,16},{1,17},{2,18},{3,19},{4,20},{5,21},{6,22},{7,23},{8,24},{9,... | collective-permute-start | bytes 516104 | tf_op jit(solution)/shard_map/ppermute | solution.py:48
  351.3 10.4 %copy-start.13 = (bf16[512,768]{1,0:T(8,128)(2,1)S(1)}, bf16[512,768]{1,0:T(8,128)(2,1)}, u32[]{:S(2)}) copy-start(bf16[512,768]{1,0:T(8,128)(2,1)} %copy-done.12) | copy-start | bytes 2359300
  351.3 11.1 %collective-permute-start.51 = (f32[24,1536]{1,0:T(8,128)S(1)}, f32[24,1536]{1,0:T(8,128)S(1)}, u32[]{:S(2)}, u32[]{:S(2)}) collective-permute-start(f32[24,1536]{1,0:T(8,128)S(1)} %get-tuple-element.433), channel_id=1, source_target_pairs={{0,1},{1,0},{2,3},{3,2},{4,5},{5,4},{6,7},{7,6},{8,9},{9,8},{10,11... | collective-permute-start | bytes 442376 | tf_op jit(solution)/shard_map/ppermute | solution.py:48
  361.2 3.5 collective-permute-start.49
  365.1 4.9 %copy-start.1 = (bf16[2,96]{1,0:T(2,128)(2,1)S(1)}, bf16[2,96]{1,0:T(2,128)(2,1)}, u32[]{:S(2)}) copy-start(bf16[2,96]{1,0:T(2,128)(2,1)} %param.18) | copy-start | bytes 1156
  (13 other events, 26.6 us)

commit v3 on v2

--- a/solution.py
+++ b/solution.py
@@ -25,8 +25,8 @@
 EARLY = (False, False, False, False)
 LATE = (False, False, False, False)
 ORDER = (
-    0, 6, 1, 2, 11, 7, 16, 8, 3, 12, 21, 9, 13, 17, 14, 10, 22, 23, 18, 26, 15, 19, 27,
-    28, 24, 20, 4, 29, 25, 30, 5, 31, 33, 34, 35, 36, 37, 47, 48, 49, 38, 42, 51, 39, 43,
+    0, 6, 1, 2, 7, 11, 16, 8, 3, 12, 21, 9, 13, 17, 14, 10, 22, 15, 23, 18, 26, 19, 24,
+    27, 28, 20, 4, 29, 25, 5, 30, 31, 33, 34, 35, 36, 37, 47, 48, 49, 38, 42, 51, 43, 39,
     50, 52, 44, 61, 40, 56, 53, 45, 57, 58, 54, 59, 32, 55, 60, 41, 46,
 )
 

time: 375 us -> 373 us (level)
  transfers between devices with their start and end apart: 55 -> 55, of which waited for: 26 -> 26; matrix products, arithmetic and copies ran while one was open for 3% -> 3% of each run, Pallas kernels for 28% -> 27%
where the time goes in v3:
time: 373 us; the launch traced here: 368 us
  waiting for transfers between devices  156 us (42%)
  Pallas kernels  114 us (31%)
  starting transfers between devices  72.3 us (19%)
  other arithmetic  11 us (3%)
  local copies, waits for them, and re-layouts  7.94 us (2%)
    pallas_call x46, Pallas kernels, kernel_call(): pl.pallas_call(body, out_shape=shapes, in_specs=[in_smem if value.dtype =...  114 us
    ppermute x18, waiting for transfers between devices, plane_swap(): return lax.ppermute(value, AXIS, pairs)  79.1 us
    ppermute x37, waiting for transfers between devices, swap(): return lax.ppermute(value, AXIS, pairs)  76.5 us
    ppermute x37, starting transfers between devices, swap(): return lax.ppermute(value, AXIS, pairs)  56.5 us
    ppermute x18, starting transfers between devices, plane_swap(): return lax.ppermute(value, AXIS, pairs)  15.8 us
  transfers between devices with their start and end apart: 55, of which 26 were waited for; matrix products, arithmetic and copies ran while one was open for 3% of the time, Pallas kernels for 27%

profile of v3, /device:TPU:1, one launch (start us, length us, event | category | flops | bytes accessed | tf_op | source)
XLA Modules:
  0.0 367.8 jit_solution(15132403255596470252)
XLA Ops:
  5.1 3.5 collective-permute-start.4
  9.6 7.1 %collective-permute-done.4.theirs_ref = bf16[1,1,112,768]{3,2,1,0:T(8,128)(2,1)S(1)} collective-permute-done((bf16[1,1,112,768]{3,2,1,0:T(8,128)(2,1)S(1)}, bf16[1,1,112,768]{3,2,1,0:T(8,128)(2,1)S(1)}, u32[]{:S(2)}, u32[]{:S(2)}) %collective-permute-start.4) | collective-permute-done | bytes 172064 | tf_op jit(solution)/shard_map/ppermute | solution.py:48
  18.2 3.1 collective-permute-start.7
  21.3 11.1 %collective-permute-done.5.theirs_ref = bf16[2,1,112,768]{3,2,1,0:T(8,128)(2,1)S(1)} collective-permute-done((bf16[2,1,112,768]{3,2,1,0:T(8,128)(2,1)S(1)}, bf16[2,1,112,768]{3,2,1,0:T(8,128)(2,1)S(1)}, u32[]{:S(2)}, u32[]{:S(2)}) %collective-permute-start.5) | collective-permute-done | bytes 344096 | tf_op jit(solution)/shard_map/ppermute | solution.py:48
  34.6 1.8 collective-permute-start.9
  36.3 6.9 %collective-permute-done.6.theirs_ref = bf16[4,1,112,768]{3,2,1,0:T(8,128)(2,1)S(1)} collective-permute-done((bf16[4,1,112,768]{3,2,1,0:T(8,128)(2,1)S(1)}, bf16[4,1,112,768]{3,2,1,0:T(8,128)(2,1)S(1)}, u32[]{:S(2)}, u32[]{:S(2)}) %collective-permute-start.6) | collective-permute-done | bytes 688160 | tf_op jit(solution)/shard_map/ppermute | solution.py:81
  44.5 3.5 collective-permute-done.9.theirs_ref
  48.6 1.3 collective-permute-start.10
  49.9 1.7 collective-permute-start.11
  53.0 2.1 collective-permute-done.11.theirs_ref
  55.6 11.9 %collective-permute-start.13 = (bf16[2,1,112,768]{3,2,1,0:T(8,128)(2,1)S(1)}, bf16[2,1,112,768]{3,2,1,0:T(8,128)(2,1)S(1)}, u32[]{:S(2)}, u32[]{:S(2)}) collective-permute-start(bf16[2,1,112,768]{3,2,1,0:T(8,128)(2,1)S(1)} %bitcast.274), channel_id=1, source_target_pairs={{0,8},{1,9},{2,10},{3,11},{4,12},{5,13},{6,14},{7,15},{8,0},{9,1},... | collective-permute-start | bytes 1032200 | tf_op jit(solution)/shard_map/ppermute | solution.py:48
  67.5 9.2 %collective-permute-done.10.theirs_ref = bf16[4,1,192,768]{3,2,1,0:T(8,128)(2,1)S(1)} collective-permute-done((bf16[4,1,192,768]{3,2,1,0:T(8,128)(2,1)S(1)}, bf16[4,1,192,768]{3,2,1,0:T(8,128)(2,1)S(1)}, u32[]{:S(2)}, u32[]{:S(2)}) %collective-permute-start.10) | collective-permute-done | bytes 1179680 | tf_op jit(solution)/shard_map/ppermute | solution.py:81
  77.4 1.4 collective-permute-start.19
  81.4 13.5 %collective-permute-done.15.theirs_ref = bf16[2,1,192,768]{3,2,1,0:T(8,128)(2,1)S(1)} collective-permute-done((bf16[2,1,192,768]{3,2,1,0:T(8,128)(2,1)S(1)}, bf16[2,1,192,768]{3,2,1,0:T(8,128)(2,1)S(1)}, u32[]{:S(2)}, u32[]{:S(2)}) %collective-permute-start.15) | collective-permute-done | bytes 589856 | tf_op jit(solution)/shard_map/ppermute | solution.py:48
  95.6 1.3 collective-permute-start.17
  97.9 12.5 %shard_map.180 = (bf16[512,768]{1,0:T(8,128)(2,1)S(1)}, bf16[512,1152]{1,0:T(8,128)(2,1)S(1)}, bf16[512,384]{1,0:T(8,128)(2,1)S(1)}, f32[512,128]{1,0:T(8,128)S(1)}) custom-call(s32[1]{0:T(128)S(6)} %copy.100.kind_ref, bf16[512,768]{1,0:T(8,128)(2,1)S(1)} %get-tuple-element.205.x_ref, bf16[768,768]{1,0:T(8,128)(2,1)S(1)} %bitcast.254, ...), custom_call_target="tpu_custom_call" | custom-call | tf_op jit(solution)/shard_map/pallas_call | solution.py:642
  110.4 1.9 collective-permute-start.16
  112.4 11.2 %collective-permute-done.18.theirs_ref = bf16[4,1,112,768]{3,2,1,0:T(8,128)(2,1)S(1)} collective-permute-done((bf16[4,1,112,768]{3,2,1,0:T(8,128)(2,1)S(1)}, bf16[4,1,112,768]{3,2,1,0:T(8,128)(2,1)S(1)}, u32[]{:S(2)}, u32[]{:S(2)}) %collective-permute-start.18) | collective-permute-done | bytes 688160 | tf_op jit(solution)/shard_map/ppermute | solution.py:81
  126.6 4.5 %shard_map.184 = (f32[512,768]{1,0:T(8,128)S(1)}, f32[512,768]{1,0:T(8,128)S(1)}, bf16[512,768]{1,0:T(8,128)(2,1)S(1)}, bf16[512,1536]{1,0:T(8,128)(2,1)S(1)}, b...) custom-call(f32[512,768]{1,0:T(8,128)S(1)} %get-tuple-element.398.x_ref, ...), custom_call_target="tpu_custom_call" | custom-call | tf_op jit(solution)/shard_map/pallas_call | solution.py:642
  132.0 3.2 collective-permute-start.20
  135.1 1.3 collective-permute-start.25
  138.1 3.7 %collective-permute-done.21.theirs_ref = bf16[4,2,112,768]{3,2,1,0:T(8,128)(2,1)S(1)} collective-permute-done((bf16[4,2,112,768]{3,2,1,0:T(8,128)(2,1)S(1)}, bf16[4,2,112,768]{3,2,1,0:T(8,128)(2,1)S(1)}, u32[]{:S(2)}, u32[]{:S(2)}) %collective-permute-start.21) | collective-permute-done | bytes 1376288 | tf_op jit(solution)/shard_map/ppermute | solution.py:81
  142.7 3.2 collective-permute-start.22
  147.4 12.0 %shard_map.187 = (bf16[512,768]{1,0:T(8,128)(2,1)S(1)}, bf16[512,1152]{1,0:T(8,128)(2,1)S(1)}, bf16[512,384]{1,0:T(8,128)(2,1)S(1)}, f32[512,128]{1,0:T(8,128)S(1)}) custom-call(s32[1]{0:T(128)S(6)} %copy.100.kind_ref, bf16[512,768]{1,0:T(8,128)(2,1)S(1)} %get-tuple-element.230.x_ref, bf16[768,768]{1,0:T(8,128)(2,1)S(1)} %bitcast.258, ...), custom_call_target="tpu_custom_call" | custom-call | tf_op jit(solution)/shard_map/pallas_call | solution.py:642
  160.0 1.8 collective-permute-done.23.theirs_ref
  161.8 5.3 %collective-permute-done.25.theirs_ref = bf16[4,2,192,768]{3,2,1,0:T(8,128)(2,1)S(1)} collective-permute-done((bf16[4,2,192,768]{3,2,1,0:T(8,128)(2,1)S(1)}, bf16[4,2,192,768]{3,2,1,0:T(8,128)(2,1)S(1)}, u32[]{:S(2)}, u32[]{:S(2)}) %collective-permute-start.25) | collective-permute-done | bytes 2359328 | tf_op jit(solution)/shard_map/ppermute | solution.py:81
  167.9 4.7 %shard_map.189 = (f32[512,768]{1,0:T(8,128)S(1)}, f32[512,768]{1,0:T(8,128)S(1)}, bf16[512,768]{1,0:T(8,128)(2,1)S(1)}, bf16[512,1536]{1,0:T(8,128)(2,1)S(1)}, b...) custom-call(f32[512,768]{1,0:T(8,128)S(1)} %get-tuple-element.222.x_ref, ...), custom_call_target="tpu_custom_call" | custom-call | tf_op jit(solution)/shard_map/pallas_call | solution.py:642
  172.6 3.2 collective-permute-start.26
  175.8 1.9 collective-permute-done.26.theirs_ref
  177.7 2.2 shard_map.190
  179.9 2.9 shard_map.191
  183.5 4.0 %shard_map.193 = (bf16[768,768]{1,0:T(8,128)(2,1)S(1)}, bf16[768,768]{1,0:T(8,128)(2,1)S(1)}, bf16[512,768]{1,0:T(8,128)(2,1)S(1)}, f32[1,1536]{1,0:T(1,128)S(1)}) custom-call(bf16[512,768]{1,0:T(8,128)(2,1)S(1)} %get-tuple-element.254.d_ffn_ref, bf16[512,1536]{1,0:T(8,128)(2,1)S(1)} %get-tuple-element.255.slope_ref, ...), custom_call_target="tpu_custom_call" | custom-call | tf_op jit(solution)/shard_map/pallas_call | solution.py:642
  188.0 1.4 collective-permute-start.29
  190.2 16.9 %shard_map.195 = (bf16[768,768]{1,0:T(8,128)(2,1)S(1)}, bf16[768,384]{1,0:T(8,128)(2,1)S(1)}, bf16[384,768]{1,0:T(8,128)(2,1)S(1)}, bf16[512,768]{1,0:T(8,128)(2...) custom-call(s32[1]{0:T(128)S(6)} %copy.100.kind_ref, ...), custom_call_target="tpu_custom_call" | custom-call | tf_op jit(solution)/shard_map/pallas_call | solution.py:642
  208.1 2.1 collective-permute-done.31
  211.2 4.8 %collective-permute-done.30.refs_4_ = bf16[4,2,96,768]{3,2,1,0:T(8,128)(2,1)S(1)} collective-permute-done((bf16[4,2,96,768]{3,2,1,0:T(8,128)(2,1)S(1)}, bf16[4,2,96,768]{3,2,1,0:T(8,128)(2,1)S(1)}, u32[]{:S(2)}, u32[]{:S(2)}) %collective-permute-start.30) | collective-permute-done | bytes 1179680 | tf_op jit(solution)/shard_map/ppermute | solution.py:81
  217.1 1.3 collective-permute-start.33
  218.4 1.4 collective-permute-start.35
  219.7 3.1 shard_map.198
  224.0 4.0 %shard_map.200 = (bf16[768,768]{1,0:T(8,128)(2,1)S(1)}, bf16[768,768]{1,0:T(8,128)(2,1)S(1)}, bf16[512,768]{1,0:T(8,128)(2,1)S(1)}, f32[1,1536]{1,0:T(1,128)S(1)}) custom-call(bf16[512,768]{1,0:T(8,128)(2,1)S(1)} %get-tuple-element.287.d_ffn_ref, bf16[512,1536]{1,0:T(8,128)(2,1)S(1)} %get-tuple-element.288.slope_ref, bf16[512,768]{1,0:T(8,128)(2,1)S(1)} %copy-done.5, ...), custom_call_target="tpu_custom_call" | custom-call | tf_op jit(solution)/shard_map/pallas_call | solution.py:642
  228.0 1.6 collective-permute-start.32
  230.4 1.4 collective-permute-start.38
  231.8 16.9 %shard_map.202 = (bf16[768,768]{1,0:T(8,128)(2,1)S(1)}, bf16[768,384]{1,0:T(8,128)(2,1)S(1)}, bf16[384,768]{1,0:T(8,128)(2,1)S(1)}, bf16[512,768]{1,0:T(8,128)(2...) custom-call(s32[1]{0:T(128)S(6)} %copy.100.kind_ref, ...), custom_call_target="tpu_custom_call" | custom-call | tf_op jit(solution)/shard_map/pallas_call | solution.py:642
  252.8 14.2 %collective-permute-done.37.refs_3_ = bf16[4,2,96,768]{3,2,1,0:T(8,128)(2,1)S(1)} collective-permute-done((bf16[4,2,96,768]{3,2,1,0:T(8,128)(2,1)S(1)}, bf16[4,2,96,768]{3,2,1,0:T(8,128)(2,1)S(1)}, u32[]{:S(2)}, u32[]{:S(2)}) %collective-permute-start.37) | collective-permute-done | bytes 1179680 | tf_op jit(solution)/shard_map/ppermute | solution.py:81
  267.0 13.8 %collective-permute-done.38.refs_4_ = bf16[4,2,96,768]{3,2,1,0:T(8,128)(2,1)S(1)} collective-permute-done((bf16[4,2,96,768]{3,2,1,0:T(8,128)(2,1)S(1)}, bf16[4,2,96,768]{3,2,1,0:T(8,128)(2,1)S(1)}, u32[]{:S(2)}, u32[]{:S(2)}) %collective-permute-start.38) | collective-permute-done | bytes 1179680 | tf_op jit(solution)/shard_map/ppermute | solution.py:81
  280.8 2.0 shard_map.205
  283.1 1.4 shard_map.206
  284.5 1.4 shard_map.207
  288.4 1.7 shard_map.208
  291.1 1.9 collective-permute-start.53
  293.0 9.9 %collective-permute-done.43 = bf16[4,1,192,768]{3,2,1,0:T(8,128)(2,1)} collective-permute-done((bf16[4,1,192,768]{3,2,1,0:T(8,128)(2,1)}, bf16[4,1,192,768]{3,2,1,0:T(8,128)(2,1)}, u32[]{:S(2)}, u32[]{:S(2)}) %collective-permute-start.43) | collective-permute-done | bytes 1179680 | tf_op jit(solution)/shard_map/ppermute | solution.py:81
  302.9 1.7 copy-done.3
  304.6 1.7 shard_map.210
  307.7 2.9 collective-permute-start.45
  310.6 2.0 add_add_fusion
  313.7 2.2 collective-permute-start.54
  315.9 1.7 shard_map.209
  318.3 7.3 %collective-permute-done.45 = bf16[2,1,192,768]{3,2,0,1:T(8,128)(2,1)S(1)} collective-permute-done((bf16[2,1,192,768]{3,2,0,1:T(8,128)(2,1)S(1)}, bf16[2,1,192,768]{3,2,0,1:T(8,128)(2,1)S(1)}, u32[]{:S(2)}, u32[]{:S(2)}) %collective-permute-start.45) | collective-permute-done | bytes 589856 | tf_op jit(solution)/shard_map/ppermute | solution.py:48
  327.3 2.5 collective-permute-start.52
  331.8 1.5 collective-permute-start.46
  333.4 14.0 %collective-permute-done.46 = bf16[2,1,112,768]{3,2,0,1:T(8,128)(2,1)S(1)} collective-permute-done((bf16[2,1,112,768]{3,2,0,1:T(8,128)(2,1)S(1)}, bf16[2,1,112,768]{3,2,0,1:T(8,128)(2,1)S(1)}, u32[]{:S(2)}, u32[]{:S(2)}) %collective-permute-start.46) | collective-permute-done | bytes 344096 | tf_op jit(solution)/shard_map/ppermute | solution.py:48
  350.4 8.0 %collective-permute-done.47 = bf16[1,1,112,768]{3,2,1,0:T(8,128)(2,1)S(1)} collective-permute-done((bf16[1,1,112,768]{3,2,1,0:T(8,128)(2,1)S(1)}, bf16[1,1,112,768]{3,2,1,0:T(8,128)(2,1)S(1)}, u32[]{:S(2)}, u32[]{:S(2)}) %collective-permute-start.47) | collective-permute-done | bytes 172064 | tf_op jit(solution)/shard_map/ppermute | solution.py:48
  359.9 1.3 fusion.1
  362.5 1.3 fusion
  (350 shorter events, 56.6 us)
Async XLA Ops:
  2.1 1.7 collective-permute-start
  2.4 1.4 collective-permute-start.1
  4.7 4.1 %copy-start.18 = (bf16[2,96,768]{2,1,0:T(8,128)(2,1)S(1)}, bf16[2,96,768]{2,1,0:T(8,128)(2,1)}, u32[]{:S(2)}) copy-start(bf16[2,96,768]{2,1,0:T(8,128)(2,1)} %param.15) | copy-start | bytes 884740
  4.7 4.2 %copy-start.15 = (bf16[256,768]{1,0:T(8,128)(2,1)S(1)}, bf16[256,768]{1,0:T(8,128)(2,1)}, u32[]{:S(2)}) copy-start(bf16[256,768]{1,0:T(8,128)(2,1)} %param.10) | copy-start | bytes 1179652
  4.7 3.9 %collective-permute-start.2 = (bf16[192,384]{1,0:T(8,128)(2,1)S(1)}, bf16[192,384]{1,0:T(8,128)(2,1)S(1)}, u32[]{:S(2)}, u32[]{:S(2)}) collective-permute-start(bf16[192,384]{1,0:T(8,128)(2,1)S(1)} %broadcast_select_fusion.8), channel_id=1, source_target_pairs={{0,1},{1,0},{2,3},{3,2},{4,5},{5,4},{6,7},{7,6},{8,9},{9,8},{10,11... | collective-permute-start | bytes 442376 | tf_op jit(solution)/shard_map/ppermute | solution.py:48
  5.1 11.6 %collective-permute-start.4 = (bf16[1,1,112,768]{3,2,1,0:T(8,128)(2,1)S(1)}, bf16[1,1,112,768]{3,2,1,0:T(8,128)(2,1)S(1)}, u32[]{:S(2)}, u32[]{:S(2)}) collective-permute-start(bf16[1,1,112,768]{3,2,1,0:T(8,128)(2,1)S(1)} %bitcast.289), channel_id=1, source_target_pairs={{0,16},{1,17},{2,18},{3,19},{4,20},{5,21},{6,22},{7,23},{8,24},{9,... | collective-permute-start | bytes 516104 | tf_op jit(solution)/shard_map/ppermute | solution.py:48
  8.9 24.9 %collective-permute-start.3 = (bf16[256,768]{1,0:T(8,128)(2,1)S(1)}, bf16[256,768]{1,0:T(8,128)(2,1)S(1)}, u32[]{:S(2)}, u32[]{:S(2)}) collective-permute-start(bf16[256,768]{1,0:T(8,128)(2,1)S(1)} %copy-done.15), channel_id=1, source_target_pairs={{0,1},{1,0},{2,3},{3,2},{4,5},{5,4},{6,7},{7,6},{8,9},{9,8},{10,11... | collective-permute-start | bytes 1179656 | tf_op jit(solution)/shard_map/ppermute | solution.py:48
  17.3 15.1 %collective-permute-start.5 = (bf16[2,1,112,768]{3,2,1,0:T(8,128)(2,1)S(1)}, bf16[2,1,112,768]{3,2,1,0:T(8,128)(2,1)S(1)}, u32[]{:S(2)}, u32[]{:S(2)}) collective-permute-start(bf16[2,1,112,768]{3,2,1,0:T(8,128)(2,1)S(1)} %bitcast.276), channel_id=1, source_target_pairs={{0,8},{1,9},{2,10},{3,11},{4,12},{5,13},{6,14},{7,15},{8,0},{9,1},... | collective-permute-start | bytes 1032200 | tf_op jit(solution)/shard_map/ppermute | solution.py:48
  18.2 15.7 %collective-permute-start.7 = (bf16[1,1,192,768]{3,2,1,0:T(8,128)(2,1)S(1)}, bf16[1,1,192,768]{3,2,1,0:T(8,128)(2,1)S(1)}, u32[]{:S(2)}, u32[]{:S(2)}) collective-permute-start(bf16[1,1,192,768]{3,2,1,0:T(8,128)(2,1)S(1)} %bitcast.299), channel_id=1, source_target_pairs={{0,16},{1,17},{2,18},{3,19},{4,20},{5,21},{6,22},{7,23},{8,24},{9,... | collective-permute-start | bytes 884744 | tf_op jit(solution)/shard_map/ppermute | solution.py:48
  33.0 10.1 %collective-permute-start.6 = (bf16[4,1,112,768]{3,2,1,0:T(8,128)(2,1)S(1)}, bf16[4,1,112,768]{3,2,1,0:T(8,128)(2,1)S(1)}, u32[]{:S(2)}, u32[]{:S(2)}) collective-permute-start(bf16[4,1,112,768]{3,2,1,0:T(8,128)(2,1)S(1)} %bitcast.264), channel_id=1, source_target_pairs={{0,2},{1,5},{2,0},{3,7},{4,6},{5,1},{6,4},{7,3},{8,10},{9,13},{10,... | collective-permute-start | bytes 2064392 | tf_op jit(solution)/shard_map/ppermute | solution.py:81
  34.6 13.4 %collective-permute-start.9 = (bf16[2,1,192,768]{3,2,1,0:T(8,128)(2,1)S(1)}, bf16[2,1,192,768]{3,2,1,0:T(8,128)(2,1)S(1)}, u32[]{:S(2)}, u32[]{:S(2)}) collective-permute-start(bf16[2,1,192,768]{3,2,1,0:T(8,128)(2,1)S(1)} %bitcast.268), channel_id=1, source_target_pairs={{0,8},{1,9},{2,10},{3,11},{4,12},{5,13},{6,14},{7,15},{8,0},{9,1},... | collective-permute-start | bytes 1769480 | tf_op jit(solution)/shard_map/ppermute | solution.py:48
  43.8 35.0 %collective-permute-start.8 = (bf16[4,2,112,768]{3,2,1,0:T(8,128)(2,1)S(1)}, bf16[4,2,112,768]{3,2,1,0:T(8,128)(2,1)S(1)}, u32[]{:S(2)}, u32[]{:S(2)}) collective-permute-start(bf16[4,2,112,768]{3,2,1,0:T(8,128)(2,1)S(1)} %shard_map.172.mine_ref), channel_id=1, source_target_pairs={{0,4},{1,3},{2,6},{3,1},{4,0},{5,7},{6,2},{7,5},{8,12},{9,11},{10,... | collective-permute-start | bytes 4128776 | tf_op jit(solution)/shard_map/ppermute | solution.py:81
  48.6 28.1 %collective-permute-start.10 = (bf16[4,1,192,768]{3,2,1,0:T(8,128)(2,1)S(1)}, bf16[4,1,192,768]{3,2,1,0:T(8,128)(2,1)S(1)}, u32[]{:S(2)}, u32[]{:S(2)}) collective-permute-start(bf16[4,1,192,768]{3,2,1,0:T(8,128)(2,1)S(1)} %bitcast.244), channel_id=1, source_target_pairs={{0,2},{1,5},{2,0},{3,7},{4,6},{5,1},{6,4},{7,3},{8,10},{9,13},{10,... | collective-permute-start | bytes 3538952 | tf_op jit(solution)/shard_map/ppermute | solution.py:81
  49.9 5.2 %collective-permute-start.11 = (bf16[1,1,112,768]{3,2,1,0:T(8,128)(2,1)S(1)}, bf16[1,1,112,768]{3,2,1,0:T(8,128)(2,1)S(1)}, u32[]{:S(2)}, u32[]{:S(2)}) collective-permute-start(bf16[1,1,112,768]{3,2,1,0:T(8,128)(2,1)S(1)} %bitcast.287), channel_id=1, source_target_pairs={{0,16},{1,17},{2,18},{3,19},{4,20},{5,21},{6,22},{7,23},{8,24},{9,... | collective-permute-start | bytes 516104 | tf_op jit(solution)/shard_map/ppermute | solution.py:48
  52.2 27.6 %collective-permute-start.14 = (bf16[1,1,192,768]{3,2,1,0:T(8,128)(2,1)S(1)}, bf16[1,1,192,768]{3,2,1,0:T(8,128)(2,1)S(1)}, u32[]{:S(2)}, u32[]{:S(2)}) collective-permute-start(bf16[1,1,192,768]{3,2,1,0:T(8,128)(2,1)S(1)} %bitcast.301), channel_id=1, source_target_pairs={{0,16},{1,17},{2,18},{3,19},{4,20},{5,21},{6,22},{7,23},{8,24},{9,... | collective-permute-start | bytes 884744 | tf_op jit(solution)/shard_map/ppermute | solution.py:48
  55.6 41.2 %collective-permute-start.13 = (bf16[2,1,112,768]{3,2,1,0:T(8,128)(2,1)S(1)}, bf16[2,1,112,768]{3,2,1,0:T(8,128)(2,1)S(1)}, u32[]{:S(2)}, u32[]{:S(2)}) collective-permute-start(bf16[2,1,112,768]{3,2,1,0:T(8,128)(2,1)S(1)} %bitcast.274), channel_id=1, source_target_pairs={{0,8},{1,9},{2,10},{3,11},{4,12},{5,13},{6,14},{7,15},{8,0},{9,1},... | collective-permute-start | bytes 1032200 | tf_op jit(solution)/shard_map/ppermute | solution.py:48
  77.4 48.3 %collective-permute-start.19 = (bf16[4,2,192,768]{3,2,1,0:T(8,128)(2,1)S(1)}, bf16[4,2,192,768]{3,2,1,0:T(8,128)(2,1)S(1)}, u32[]{:S(2)}, u32[]{:S(2)}) collective-permute-start(bf16[4,2,192,768]{3,2,1,0:T(8,128)(2,1)S(1)} %shard_map.175.mine_ref), channel_id=1, source_target_pairs={{0,4},{1,3},{2,6},{3,1},{4,0},{5,7},{6,2},{7,5},{8,12},{9,11},{10,... | collective-permute-start | bytes 7077896 | tf_op jit(solution)/shard_map/ppermute | solution.py:81
  79.7 1.6 collective-permute-start.12
  80.5 14.5 %collective-permute-start.15 = (bf16[2,1,192,768]{3,2,1,0:T(8,128)(2,1)S(1)}, bf16[2,1,192,768]{3,2,1,0:T(8,128)(2,1)S(1)}, u32[]{:S(2)}, u32[]{:S(2)}) collective-permute-start(bf16[2,1,192,768]{3,2,1,0:T(8,128)(2,1)S(1)} %bitcast.266), channel_id=1, source_target_pairs={{0,8},{1,9},{2,10},{3,11},{4,12},{5,13},{6,14},{7,15},{8,0},{9,1},... | collective-permute-start | bytes 1769480 | tf_op jit(solution)/shard_map/ppermute | solution.py:48
  95.6 29.4 %collective-permute-start.17 = (bf16[4,1,192,768]{3,2,1,0:T(8,128)(2,1)S(1)}, bf16[4,1,192,768]{3,2,1,0:T(8,128)(2,1)S(1)}, u32[]{:S(2)}, u32[]{:S(2)}) collective-permute-start(bf16[4,1,192,768]{3,2,1,0:T(8,128)(2,1)S(1)} %bitcast.242), channel_id=1, source_target_pairs={{0,2},{1,5},{2,0},{3,7},{4,6},{5,1},{6,4},{7,3},{8,10},{9,13},{10,... | collective-permute-start | bytes 3538952 | tf_op jit(solution)/shard_map/ppermute | solution.py:81
  97.5 26.1 %collective-permute-start.18 = (bf16[4,1,112,768]{3,2,1,0:T(8,128)(2,1)S(1)}, bf16[4,1,112,768]{3,2,1,0:T(8,128)(2,1)S(1)}, u32[]{:S(2)}, u32[]{:S(2)}) collective-permute-start(bf16[4,1,112,768]{3,2,1,0:T(8,128)(2,1)S(1)} %bitcast.262), channel_id=1, source_target_pairs={{0,2},{1,5},{2,0},{3,7},{4,6},{5,1},{6,4},{7,3},{8,10},{9,13},{10,... | collective-permute-start | bytes 2064392 | tf_op jit(solution)/shard_map/ppermute | solution.py:81
  110.4 15.3 %copy-start.10 = (f32[512,128]{1,0:T(8,128)}, f32[512,128]{1,0:T(8,128)S(1)}, u32[]{:S(2)}) copy-start(f32[512,128]{1,0:T(8,128)S(1)} %get-tuple-element.298.lse_ref) | copy-start | bytes 786436
  110.4 15.3 %collective-permute-start.16 = (bf16[512,768]{1,0:T(8,128)(2,1)S(1)}, bf16[512,768]{1,0:T(8,128)(2,1)S(1)}, u32[]{:S(2)}, u32[]{:S(2)}) collective-permute-start(bf16[512,768]{1,0:T(8,128)(2,1)S(1)} %get-tuple-element.212.mine_ref), channel_id=1, source_target_pairs={{0,1},{1,0},{2,3},{3,2},{4,5},{5,4},{6,7},{7,6},{8,9},{9,8},{10,11... | collective-permute-start | bytes 2359304 | tf_op jit(solution)/shard_map/ppermute | solution.py:48
  124.2 17.5 %collective-permute-start.21 = (bf16[4,2,112,768]{3,2,1,0:T(8,128)(2,1)S(1)}, bf16[4,2,112,768]{3,2,1,0:T(8,128)(2,1)S(1)}, u32[]{:S(2)}, u32[]{:S(2)}) collective-permute-start(bf16[4,2,112,768]{3,2,1,0:T(8,128)(2,1)S(1)} %shard_map.181.mine_ref), channel_id=1, source_target_pairs={{0,4},{1,3},{2,6},{3,1},{4,0},{5,7},{6,2},{7,5},{8,12},{9,11},{10,... | collective-permute-start | bytes 4128776 | tf_op jit(solution)/shard_map/ppermute | solution.py:81
  132.0 5.1 %collective-permute-start.20 = (bf16[512,768]{1,0:T(8,128)(2,1)S(1)}, bf16[512,768]{1,0:T(8,128)(2,1)S(1)}, u32[]{:S(2)}, u32[]{:S(2)}) collective-permute-start(bf16[512,768]{1,0:T(8,128)(2,1)S(1)} %get-tuple-element.220.mine_ref), channel_id=1, source_target_pairs={{0,1},{1,0},{2,3},{3,2},{4,5},{5,4},{6,7},{7,6},{8,9},{9,8},{10,11... | collective-permute-start | bytes 2359304 | tf_op jit(solution)/shard_map/ppermute | solution.py:48
  135.1 31.9 %collective-permute-start.25 = (bf16[4,2,192,768]{3,2,1,0:T(8,128)(2,1)S(1)}, bf16[4,2,192,768]{3,2,1,0:T(8,128)(2,1)S(1)}, u32[]{:S(2)}, u32[]{:S(2)}) collective-permute-start(bf16[4,2,192,768]{3,2,1,0:T(8,128)(2,1)S(1)} %shard_map.182.mine_ref), channel_id=1, source_target_pairs={{0,4},{1,3},{2,6},{3,1},{4,0},{5,7},{6,2},{7,5},{8,12},{9,11},{10,... | collective-permute-start | bytes 7077896 | tf_op jit(solution)/shard_map/ppermute | solution.py:81
  142.5 3.5 copy-start.16
  142.7 4.4 %collective-permute-start.22 = (bf16[8,48,384]{2,1,0:T(8,128)(2,1)S(1)}, bf16[8,48,384]{2,1,0:T(8,128)(2,1)S(1)}, u32[]{:S(2)}, u32[]{:S(2)}) collective-permute-start(bf16[8,48,384]{2,1,0:T(8,128)(2,1)S(1)} %dynamic-slice_bitcast_fusion.2), channel_id=1, source_target_pairs={{0,1},{1,0},{2,3},{3,2},{4,5},{5,4},{6,7},{7,6},{8,9},{9,8},{10,11... | collective-permute-start | bytes 884744 | tf_op jit(solution)/shard_map/ppermute | solution.py:48
  146.0 13.8 %collective-permute-start.24 = (bf16[256,768]{1,0:T(8,128)(2,1)S(1)}, bf16[256,768]{1,0:T(8,128)(2,1)S(1)}, u32[]{:S(2)}, u32[]{:S(2)}) collective-permute-start(bf16[256,768]{1,0:T(8,128)(2,1)S(1)} %copy-done.16), channel_id=1, source_target_pairs={{0,1},{1,0},{2,3},{3,2},{4,5},{5,4},{6,7},{7,6},{8,9},{9,8},{10,11... | collective-permute-start | bytes 1179656 | tf_op jit(solution)/shard_map/ppermute | solution.py:48
  159.4 2.4 collective-permute-start.23
  172.6 5.1 %collective-permute-start.26 = (bf16[512,768]{1,0:T(8,128)(2,1)S(1)}, bf16[512,768]{1,0:T(8,128)(2,1)S(1)}, u32[]{:S(2)}, u32[]{:S(2)}) collective-permute-start(bf16[512,768]{1,0:T(8,128)(2,1)S(1)} %get-tuple-element.245.mine_ref), channel_id=1, source_target_pairs={{0,1},{1,0},{2,3},{3,2},{4,5},{5,4},{6,7},{7,6},{8,9},{9,8},{10,11... | collective-permute-start | bytes 2359304 | tf_op jit(solution)/shard_map/ppermute | solution.py:48
  187.4 2.8 collective-permute-start.27
  188.0 23.2 %collective-permute-start.29 = (bf16[4,2,96,768]{3,2,1,0:T(8,128)(2,1)S(1)}, bf16[4,2,96,768]{3,2,1,0:T(8,128)(2,1)S(1)}, u32[]{:S(2)}, u32[]{:S(2)}) collective-permute-start(bf16[4,2,96,768]{3,2,1,0:T(8,128)(2,1)S(1)} %shard_map.192), channel_id=1, source_target_pairs={{0,4},{1,3},{2,6},{3,1},{4,0},{5,7},{6,2},{7,5},{8,12},{9,11},{10,... | collective-permute-start | bytes 3538952 | tf_op jit(solution)/shard_map/ppermute | solution.py:81
  190.0 26.1 %collective-permute-start.30 = (bf16[4,2,96,768]{3,2,1,0:T(8,128)(2,1)S(1)}, bf16[4,2,96,768]{3,2,1,0:T(8,128)(2,1)S(1)}, u32[]{:S(2)}, u32[]{:S(2)}) collective-permute-start(bf16[4,2,96,768]{3,2,1,0:T(8,128)(2,1)S(1)} %shard_map.194), channel_id=1, source_target_pairs={{0,4},{1,3},{2,6},{3,1},{4,0},{5,7},{6,2},{7,5},{8,12},{9,11},{10,... | collective-permute-start | bytes 3538952 | tf_op jit(solution)/shard_map/ppermute | solution.py:81
  207.1 12.6 %collective-permute-start.28 = (bf16[512,768]{1,0:T(8,128)(2,1)S(1)}, bf16[512,768]{1,0:T(8,128)(2,1)S(1)}, u32[]{:S(2)}, u32[]{:S(2)}) collective-permute-start(bf16[512,768]{1,0:T(8,128)(2,1)S(1)} %get-tuple-element.281.refs_1_), channel_id=1, source_target_pairs={{0,1},{1,0},{2,3},{3,2},{4,5},{5,4},{6,7},{7,6},{8,9},{9,8},{10,11... | collective-permute-start | bytes 2359304 | tf_op jit(solution)/shard_map/ppermute | solution.py:48
  207.9 2.3 collective-permute-start.31
  217.1 31.6 %collective-permute-start.33 = (bf16[4,1,192,768]{3,2,1,0:T(8,128)(2,1)S(1)}, bf16[4,1,192,768]{3,2,1,0:T(8,128)(2,1)S(1)}, u32[]{:S(2)}, u32[]{:S(2)}) collective-permute-start(bf16[4,1,192,768]{3,2,1,0:T(8,128)(2,1)S(1)} %get-tuple-element.280), channel_id=1, source_target_pairs={{0,2},{1,5},{2,0},{3,7},{4,6},{5,1},{6,4},{7,3},{8,10},{9,13},{10,... | collective-permute-start | bytes 3538952 | tf_op jit(solution)/shard_map/ppermute | solution.py:81
  218.4 32.4 %collective-permute-start.35 = (bf16[4,2,112,768]{3,2,1,0:T(8,128)(2,1)S(1)}, bf16[4,2,112,768]{3,2,1,0:T(8,128)(2,1)S(1)}, u32[]{:S(2)}, u32[]{:S(2)}) collective-permute-start(bf16[4,2,112,768]{3,2,1,0:T(8,128)(2,1)S(1)} %shard_map.196), channel_id=1, source_target_pairs={{0,4},{1,3},{2,6},{3,1},{4,0},{5,7},{6,2},{7,5},{8,12},{9,11},{10,... | collective-permute-start | bytes 4128776 | tf_op jit(solution)/shard_map/ppermute | solution.py:81
  228.0 3.8 %collective-permute-start.32 = (bf16[512,768]{1,0:T(8,128)(2,1)S(1)}, bf16[512,768]{1,0:T(8,128)(2,1)S(1)}, u32[]{:S(2)}, u32[]{:S(2)}) collective-permute-start(bf16[512,768]{1,0:T(8,128)(2,1)S(1)} %get-tuple-element.293.mine_ref), channel_id=1, source_target_pairs={{0,1},{1,0},{2,3},{3,2},{4,5},{5,4},{6,7},{7,6},{8,9},{9,8},{10,11... | collective-permute-start | bytes 2359304 | tf_op jit(solution)/shard_map/ppermute | solution.py:48
  229.6 37.5 %collective-permute-start.37 = (bf16[4,2,96,768]{3,2,1,0:T(8,128)(2,1)S(1)}, bf16[4,2,96,768]{3,2,1,0:T(8,128)(2,1)S(1)}, u32[]{:S(2)}, u32[]{:S(2)}) collective-permute-start(bf16[4,2,96,768]{3,2,1,0:T(8,128)(2,1)S(1)} %shard_map.199), channel_id=1, source_target_pairs={{0,4},{1,3},{2,6},{3,1},{4,0},{5,7},{6,2},{7,5},{8,12},{9,11},{10,... | collective-permute-start | bytes 3538952 | tf_op jit(solution)/shard_map/ppermute | solution.py:81
  230.4 50.5 %collective-permute-start.38 = (bf16[4,2,96,768]{3,2,1,0:T(8,128)(2,1)S(1)}, bf16[4,2,96,768]{3,2,1,0:T(8,128)(2,1)S(1)}, u32[]{:S(2)}, u32[]{:S(2)}) collective-permute-start(bf16[4,2,96,768]{3,2,1,0:T(8,128)(2,1)S(1)} %shard_map.201), channel_id=1, source_target_pairs={{0,4},{1,3},{2,6},{3,1},{4,0},{5,7},{6,2},{7,5},{8,12},{9,11},{10,... | collective-permute-start | bytes 3538952 | tf_op jit(solution)/shard_map/ppermute | solution.py:81
  249.8 34.7 %collective-permute-start.34 = (bf16[2,1,192,768]{3,2,0,1:T(8,128)(2,1)S(1)}, bf16[2,1,192,768]{3,2,0,1:T(8,128)(2,1)S(1)}, u32[]{:S(2)}, u32[]{:S(2)}) collective-permute-start(bf16[2,1,192,768]{3,2,0,1:T(8,128)(2,1)S(1)} %bitcast.304), channel_id=1, source_target_pairs={{0,8},{1,9},{2,10},{3,11},{4,12},{5,13},{6,14},{7,15},{8,0},{9,1},... | collective-permute-start | bytes 1769480 | tf_op jit(solution)/shard_map/ppermute | solution.py:48
  251.6 31.5 %collective-permute-start.36 = (bf16[4,1,112,768]{3,2,1,0:T(8,128)(2,1)S(1)}, bf16[4,1,112,768]{3,2,1,0:T(8,128)(2,1)S(1)}, u32[]{:S(2)}, u32[]{:S(2)}) collective-permute-start(bf16[4,1,112,768]{3,2,1,0:T(8,128)(2,1)S(1)} %get-tuple-element.309), channel_id=1, source_target_pairs={{0,2},{1,5},{2,0},{3,7},{4,6},{5,1},{6,4},{7,3},{8,10},{9,13},{10,... | collective-permute-start | bytes 2064392 | tf_op jit(solution)/shard_map/ppermute | solution.py:81
  251.9 58.7 %collective-permute-start.48 = (bf16[256,768]{1,0:T(8,128)(2,1)}, bf16[256,768]{1,0:T(8,128)(2,1)}, u32[]{:S(2)}, u32[]{:S(2)}) collective-permute-start(bf16[256,768]{1,0:T(8,128)(2,1)} %get-tuple-element.393), channel_id=1, source_target_pairs={{0,1},{1,0},{2,3},{3,2},{4,5},{5,4},{6,7},{7,6},{8,9},{9,8},{10,11... | collective-permute-start | bytes 1179656 | tf_op jit(solution)/shard_map/ppermute | solution.py:48
  282.8 20.1 %collective-permute-start.43 = (bf16[4,1,192,768]{3,2,1,0:T(8,128)(2,1)}, bf16[4,1,192,768]{3,2,1,0:T(8,128)(2,1)}, u32[]{:S(2)}, u32[]{:S(2)}) collective-permute-start(bf16[4,1,192,768]{3,2,1,0:T(8,128)(2,1)} %get-tuple-element.312), channel_id=1, source_target_pairs={{0,2},{1,5},{2,0},{3,7},{4,6},{5,1},{6,4},{7,3},{8,10},{9,13},{10,... | collective-permute-start | bytes 3538952 | tf_op jit(solution)/shard_map/ppermute | solution.py:81
  286.0 2.1 collective-permute-start.39
  286.9 19.4 %collective-permute-start.42 = (bf16[2,1,112,768]{3,2,0,1:T(8,128)(2,1)}, bf16[2,1,112,768]{3,2,0,1:T(8,128)(2,1)}, u32[]{:S(2)}, u32[]{:S(2)}) collective-permute-start(bf16[2,1,112,768]{3,2,0,1:T(8,128)(2,1)} %bitcast.94), channel_id=1, source_target_pairs={{0,8},{1,9},{2,10},{3,11},{4,12},{5,13},{6,14},{7,15},{8,0},{9,1},... | collective-permute-start | bytes 1032200 | tf_op jit(solution)/shard_map/ppermute | solution.py:48
  290.1 25.7 %collective-permute-start.40 = (bf16[4,2,112,768]{3,2,1,0:T(8,128)(2,1)}, bf16[4,2,112,768]{3,2,1,0:T(8,128)(2,1)}, u32[]{:S(2)}, u32[]{:S(2)}) collective-permute-start(bf16[4,2,112,768]{3,2,1,0:T(8,128)(2,1)} %shard_map.208), channel_id=1, source_target_pairs={{0,4},{1,3},{2,6},{3,1},{4,0},{5,7},{6,2},{7,5},{8,12},{9,11},{10,... | collective-permute-start | bytes 4128776 | tf_op jit(solution)/shard_map/ppermute | solution.py:81
  291.1 21.5 %collective-permute-start.53 = (bf16[1,1,192,768]{3,2,1,0:T(8,128)(2,1)}, bf16[1,1,192,768]{3,2,1,0:T(8,128)(2,1)}, u32[]{:S(2)}, u32[]{:S(2)}) collective-permute-start(bf16[1,1,192,768]{3,2,1,0:T(8,128)(2,1)} %get-tuple-element.316), channel_id=1, source_target_pairs={{0,16},{1,17},{2,18},{3,19},{4,20},{5,21},{6,22},{7,23},{8,24},{9,... | collective-permute-start | bytes 884744 | tf_op jit(solution)/shard_map/ppermute | solution.py:48
  304.6 6.0 %copy-start.9 = (f32[512,768]{1,0:T(8,128)S(1)}, f32[512,768]{1,0:T(8,128)}, u32[]{:S(2)}) copy-start(f32[512,768]{1,0:T(8,128)} %copy-done.8) | copy-start | bytes 4718596
  304.6 6.0 %copy-start.14 = (bf16[256,768]{1,0:T(8,128)(2,1)S(1)}, bf16[256,768]{1,0:T(8,128)(2,1)}, u32[]{:S(2)}) copy-start(bf16[256,768]{1,0:T(8,128)(2,1)} %get-tuple-element.345) | copy-start | bytes 1179652
  306.3 6.3 %copy-start.7 = (f32[1,1,192,768]{3,2,1,0:T(8,128)S(1)}, f32[1,1,192,768]{3,2,1,0:T(8,128)}, u32[]{:S(2)}) copy-start(f32[1,1,192,768]{3,2,1,0:T(8,128)} %copy-done.6) | copy-start | bytes 1769476
  307.4 18.8 %collective-permute-start.44 = (bf16[1,1,112,768]{3,2,1,0:T(8,128)(2,1)S(1)}, bf16[1,1,112,768]{3,2,1,0:T(8,128)(2,1)S(1)}, u32[]{:S(2)}, u32[]{:S(2)}) collective-permute-start(bf16[1,1,112,768]{3,2,1,0:T(8,128)(2,1)S(1)} %get-tuple-element.332), channel_id=1, source_target_pairs={{0,16},{1,17},{2,18},{3,19},{4,20},{5,21},{6,22},{7,23},{8,24},{9,... | collective-permute-start | bytes 516104 | tf_op jit(solution)/shard_map/ppermute | solution.py:48
  307.7 18.0 %collective-permute-start.45 = (bf16[2,1,192,768]{3,2,0,1:T(8,128)(2,1)S(1)}, bf16[2,1,192,768]{3,2,0,1:T(8,128)(2,1)S(1)}, u32[]{:S(2)}, u32[]{:S(2)}) collective-permute-start(bf16[2,1,192,768]{3,2,0,1:T(8,128)(2,1)S(1)} %bitcast.305), channel_id=1, source_target_pairs={{0,8},{1,9},{2,10},{3,11},{4,12},{5,13},{6,14},{7,15},{8,0},{9,1},... | collective-permute-start | bytes 1769480 | tf_op jit(solution)/shard_map/ppermute | solution.py:48
  313.7 48.8 %collective-permute-start.54 = (f32[24,1536]{1,0:T(8,128)S(1)}, f32[24,1536]{1,0:T(8,128)S(1)}, u32[]{:S(2)}, u32[]{:S(2)}) collective-permute-start(f32[24,1536]{1,0:T(8,128)S(1)} %get-tuple-element.441), channel_id=1, source_target_pairs={{0,1},{1,0},{2,3},{3,2},{4,5},{5,4},{6,7},{7,6},{8,9},{9,8},{10,11... | collective-permute-start | bytes 442376 | tf_op jit(solution)/shard_map/ppermute | solution.py:48
  317.6 13.5 %collective-permute-start.41 = (bf16[4,1,112,768]{3,2,1,0:T(8,128)(2,1)S(1)}, bf16[4,1,112,768]{3,2,1,0:T(8,128)(2,1)S(1)}, u32[]{:S(2)}, u32[]{:S(2)}) collective-permute-start(bf16[4,1,112,768]{3,2,1,0:T(8,128)(2,1)S(1)} %get-tuple-element.325), channel_id=1, source_target_pairs={{0,2},{1,5},{2,0},{3,7},{4,6},{5,1},{6,4},{7,3},{8,10},{9,13},{10,... | collective-permute-start | bytes 2064392 | tf_op jit(solution)/shard_map/ppermute | solution.py:81
  326.4 21.7 %collective-permute-start.50 = (bf16[1,1,192,768]{3,2,1,0:T(8,128)(2,1)S(1)}, bf16[1,1,192,768]{3,2,1,0:T(8,128)(2,1)S(1)}, u32[]{:S(2)}, u32[]{:S(2)}) collective-permute-start(bf16[1,1,192,768]{3,2,1,0:T(8,128)(2,1)S(1)} %get-tuple-element.335), channel_id=1, source_target_pairs={{0,16},{1,17},{2,18},{3,19},{4,20},{5,21},{6,22},{7,23},{8,24},{9,... | collective-permute-start | bytes 884744 | tf_op jit(solution)/shard_map/ppermute | solution.py:48
  327.3 3.5 collective-permute-start.52
  331.8 15.6 %collective-permute-start.46 = (bf16[2,1,112,768]{3,2,0,1:T(8,128)(2,1)S(1)}, bf16[2,1,112,768]{3,2,0,1:T(8,128)(2,1)S(1)}, u32[]{:S(2)}, u32[]{:S(2)}) collective-permute-start(bf16[2,1,112,768]{3,2,0,1:T(8,128)(2,1)S(1)} %bitcast.306), channel_id=1, source_target_pairs={{0,8},{1,9},{2,10},{3,11},{4,12},{5,13},{6,14},{7,15},{8,0},{9,1},... | collective-permute-start | bytes 1032200 | tf_op jit(solution)/shard_map/ppermute | solution.py:48
  348.0 10.4 %collective-permute-start.47 = (bf16[1,1,112,768]{3,2,1,0:T(8,128)(2,1)S(1)}, bf16[1,1,112,768]{3,2,1,0:T(8,128)(2,1)S(1)}, u32[]{:S(2)}, u32[]{:S(2)}) collective-permute-start(bf16[1,1,112,768]{3,2,1,0:T(8,128)(2,1)S(1)} %get-tuple-element.342), channel_id=1, source_target_pairs={{0,16},{1,17},{2,18},{3,19},{4,20},{5,21},{6,22},{7,23},{8,24},{9,... | collective-permute-start | bytes 516104 | tf_op jit(solution)/shard_map/ppermute | solution.py:48
  348.3 10.8 %copy-start.13 = (bf16[512,768]{1,0:T(8,128)(2,1)S(1)}, bf16[512,768]{1,0:T(8,128)(2,1)}, u32[]{:S(2)}) copy-start(bf16[512,768]{1,0:T(8,128)(2,1)} %copy-done.12) | copy-start | bytes 2359300
  348.3 11.6 %collective-permute-start.51 = (f32[24,1536]{1,0:T(8,128)S(1)}, f32[24,1536]{1,0:T(8,128)S(1)}, u32[]{:S(2)}, u32[]{:S(2)}) collective-permute-start(f32[24,1536]{1,0:T(8,128)S(1)} %get-tuple-element.433), channel_id=1, source_target_pairs={{0,1},{1,0},{2,3},{3,2},{4,5},{5,4},{6,7},{7,6},{8,9},{9,8},{10,11... | collective-permute-start | bytes 442376 | tf_op jit(solution)/shard_map/ppermute | solution.py:48
  358.5 3.5 collective-permute-start.49
  362.5 4.9 %copy-start.1 = (bf16[2,96]{1,0:T(2,128)(2,1)S(1)}, bf16[2,96]{1,0:T(2,128)(2,1)}, u32[]{:S(2)}) copy-start(bf16[2,96]{1,0:T(2,128)(2,1)} %param.18) | copy-start | bytes 1156
  (13 other events, 24.5 us)

commit v4 on v3

--- a/solution.py
+++ b/solution.py
@@ -26,8 +26,8 @@
 LATE = (False, False, False, False)
 ORDER = (
     0, 6, 1, 2, 7, 11, 16, 8, 3, 12, 21, 9, 13, 17, 14, 10, 22, 15, 23, 18, 26, 19, 24,
-    27, 28, 20, 4, 29, 25, 5, 30, 31, 33, 34, 35, 36, 37, 47, 48, 49, 38, 42, 51, 43, 39,
-    50, 52, 44, 61, 40, 56, 53, 45, 57, 58, 54, 59, 32, 55, 60, 41, 46,
+    27, 28, 20, 4, 29, 5, 25, 30, 31, 33, 34, 35, 36, 37, 47, 48, 49, 38, 42, 51, 43, 39,
+    50, 52, 61, 40, 44, 56, 53, 45, 57, 58, 54, 59, 55, 60, 46, 41, 32,
 )
 
 

time: 373 us -> 367 us (0.984)
  waiting for transfers between devices: 156 us -> 148 us
    ppermute x18, waiting for transfers between devices: 79.1 us -> 65.2 us  [plane_swap(): return lax.ppermute(value, AXIS, pairs)]
    ppermute x37, waiting for transfers between devices: 76.5 us -> 82.6 us  [swap(): return lax.ppermute(value, AXIS, pairs)]
where the time goes in v4:
time: 367 us; the launch traced here: 362 us
  waiting for transfers between devices  148 us (40%)
  Pallas kernels  113 us (31%)
  starting transfers between devices  74.6 us (20%)
  other arithmetic  10.1 us (3%)
  local copies, waits for them, and re-layouts  9.41 us (3%)
    pallas_call x46, Pallas kernels, kernel_call(): pl.pallas_call(body, out_shape=shapes, in_specs=[in_smem if value.dtype =...  113 us
    ppermute x37, waiting for transfers between devices, swap(): return lax.ppermute(value, AXIS, pairs)  82.6 us
    ppermute x18, waiting for transfers between devices, plane_swap(): return lax.ppermute(value, AXIS, pairs)  65.2 us
    ppermute x37, starting transfers between devices, swap(): return lax.ppermute(value, AXIS, pairs)  57.1 us
    ppermute x18, starting transfers between devices, plane_swap(): return lax.ppermute(value, AXIS, pairs)  17.5 us
  transfers between devices with their start and end apart: 55, of which 26 were waited for; matrix products, arithmetic and copies ran while one was open for 3% of the time, Pallas kernels for 27%

profile of v4, /device:TPU:1, one launch (start us, length us, event | category | flops | bytes accessed | tf_op | source)
XLA Modules:
  0.0 361.8 jit_solution(4176333804991519754)
XLA Ops:
  5.1 3.5 collective-permute-start.4
  9.6 7.1 %collective-permute-done.4.theirs_ref = bf16[1,1,112,768]{3,2,1,0:T(8,128)(2,1)S(1)} collective-permute-done((bf16[1,1,112,768]{3,2,1,0:T(8,128)(2,1)S(1)}, bf16[1,1,112,768]{3,2,1,0:T(8,128)(2,1)S(1)}, u32[]{:S(2)}, u32[]{:S(2)}) %collective-permute-start.4) | collective-permute-done | bytes 172064 | tf_op jit(solution)/shard_map/ppermute | solution.py:48
  18.2 3.1 collective-permute-start.7
  21.3 11.1 %collective-permute-done.5.theirs_ref = bf16[2,1,112,768]{3,2,1,0:T(8,128)(2,1)S(1)} collective-permute-done((bf16[2,1,112,768]{3,2,1,0:T(8,128)(2,1)S(1)}, bf16[2,1,112,768]{3,2,1,0:T(8,128)(2,1)S(1)}, u32[]{:S(2)}, u32[]{:S(2)}) %collective-permute-start.5) | collective-permute-done | bytes 344096 | tf_op jit(solution)/shard_map/ppermute | solution.py:48
  34.6 1.8 collective-permute-start.9
  36.3 6.9 %collective-permute-done.6.theirs_ref = bf16[4,1,112,768]{3,2,1,0:T(8,128)(2,1)S(1)} collective-permute-done((bf16[4,1,112,768]{3,2,1,0:T(8,128)(2,1)S(1)}, bf16[4,1,112,768]{3,2,1,0:T(8,128)(2,1)S(1)}, u32[]{:S(2)}, u32[]{:S(2)}) %collective-permute-start.6) | collective-permute-done | bytes 688160 | tf_op jit(solution)/shard_map/ppermute | solution.py:81
  44.5 3.5 collective-permute-done.9.theirs_ref
  48.6 1.3 collective-permute-start.10
  49.9 1.7 collective-permute-start.11
  53.0 2.1 collective-permute-done.11.theirs_ref
  55.6 11.9 %collective-permute-start.13 = (bf16[2,1,112,768]{3,2,1,0:T(8,128)(2,1)S(1)}, bf16[2,1,112,768]{3,2,1,0:T(8,128)(2,1)S(1)}, u32[]{:S(2)}, u32[]{:S(2)}) collective-permute-start(bf16[2,1,112,768]{3,2,1,0:T(8,128)(2,1)S(1)} %bitcast.274), channel_id=1, source_target_pairs={{0,8},{1,9},{2,10},{3,11},{4,12},{5,13},{6,14},{7,15},{8,0},{9,1},... | collective-permute-start | bytes 1032200 | tf_op jit(solution)/shard_map/ppermute | solution.py:48
  67.5 9.2 %collective-permute-done.10.theirs_ref = bf16[4,1,192,768]{3,2,1,0:T(8,128)(2,1)S(1)} collective-permute-done((bf16[4,1,192,768]{3,2,1,0:T(8,128)(2,1)S(1)}, bf16[4,1,192,768]{3,2,1,0:T(8,128)(2,1)S(1)}, u32[]{:S(2)}, u32[]{:S(2)}) %collective-permute-start.10) | collective-permute-done | bytes 1179680 | tf_op jit(solution)/shard_map/ppermute | solution.py:81
  77.4 1.4 collective-permute-start.19
  81.4 13.5 %collective-permute-done.15.theirs_ref = bf16[2,1,192,768]{3,2,1,0:T(8,128)(2,1)S(1)} collective-permute-done((bf16[2,1,192,768]{3,2,1,0:T(8,128)(2,1)S(1)}, bf16[2,1,192,768]{3,2,1,0:T(8,128)(2,1)S(1)}, u32[]{:S(2)}, u32[]{:S(2)}) %collective-permute-start.15) | collective-permute-done | bytes 589856 | tf_op jit(solution)/shard_map/ppermute | solution.py:48
  95.5 1.3 collective-permute-start.17
  97.9 12.4 %shard_map.180 = (bf16[512,768]{1,0:T(8,128)(2,1)S(1)}, bf16[512,1152]{1,0:T(8,128)(2,1)S(1)}, bf16[512,384]{1,0:T(8,128)(2,1)S(1)}, f32[512,128]{1,0:T(8,128)S(1)}) custom-call(s32[1]{0:T(128)S(6)} %copy.100.kind_ref, bf16[512,768]{1,0:T(8,128)(2,1)S(1)} %get-tuple-element.205.x_ref, bf16[768,768]{1,0:T(8,128)(2,1)S(1)} %bitcast.254, ...), custom_call_target="tpu_custom_call" | custom-call | tf_op jit(solution)/shard_map/pallas_call | solution.py:642
  110.4 2.0 collective-permute-start.16
  112.3 11.3 %collective-permute-done.18.theirs_ref = bf16[4,1,112,768]{3,2,1,0:T(8,128)(2,1)S(1)} collective-permute-done((bf16[4,1,112,768]{3,2,1,0:T(8,128)(2,1)S(1)}, bf16[4,1,112,768]{3,2,1,0:T(8,128)(2,1)S(1)}, u32[]{:S(2)}, u32[]{:S(2)}) %collective-permute-start.18) | collective-permute-done | bytes 688160 | tf_op jit(solution)/shard_map/ppermute | solution.py:81
  126.5 4.5 %shard_map.184 = (f32[512,768]{1,0:T(8,128)S(1)}, f32[512,768]{1,0:T(8,128)S(1)}, bf16[512,768]{1,0:T(8,128)(2,1)S(1)}, bf16[512,1536]{1,0:T(8,128)(2,1)S(1)}, b...) custom-call(f32[512,768]{1,0:T(8,128)S(1)} %get-tuple-element.398.x_ref, ...), custom_call_target="tpu_custom_call" | custom-call | tf_op jit(solution)/shard_map/pallas_call | solution.py:642
  131.9 3.2 collective-permute-start.20
  138.1 3.7 %collective-permute-done.21.theirs_ref = bf16[4,2,112,768]{3,2,1,0:T(8,128)(2,1)S(1)} collective-permute-done((bf16[4,2,112,768]{3,2,1,0:T(8,128)(2,1)S(1)}, bf16[4,2,112,768]{3,2,1,0:T(8,128)(2,1)S(1)}, u32[]{:S(2)}, u32[]{:S(2)}) %collective-permute-start.21) | collective-permute-done | bytes 1376288 | tf_op jit(solution)/shard_map/ppermute | solution.py:81
  142.7 3.2 collective-permute-start.22
  147.4 12.0 %shard_map.187 = (bf16[512,768]{1,0:T(8,128)(2,1)S(1)}, bf16[512,1152]{1,0:T(8,128)(2,1)S(1)}, bf16[512,384]{1,0:T(8,128)(2,1)S(1)}, f32[512,128]{1,0:T(8,128)S(1)}) custom-call(s32[1]{0:T(128)S(6)} %copy.100.kind_ref, bf16[512,768]{1,0:T(8,128)(2,1)S(1)} %get-tuple-element.230.x_ref, bf16[768,768]{1,0:T(8,128)(2,1)S(1)} %bitcast.258, ...), custom_call_target="tpu_custom_call" | custom-call | tf_op jit(solution)/shard_map/pallas_call | solution.py:642
  160.0 1.8 collective-permute-done.23.theirs_ref
  161.7 5.3 %collective-permute-done.24.theirs_ref = bf16[4,2,192,768]{3,2,1,0:T(8,128)(2,1)S(1)} collective-permute-done((bf16[4,2,192,768]{3,2,1,0:T(8,128)(2,1)S(1)}, bf16[4,2,192,768]{3,2,1,0:T(8,128)(2,1)S(1)}, u32[]{:S(2)}, u32[]{:S(2)}) %collective-permute-start.24) | collective-permute-done | bytes 2359328 | tf_op jit(solution)/shard_map/ppermute | solution.py:81
  167.9 4.7 %shard_map.189 = (f32[512,768]{1,0:T(8,128)S(1)}, f32[512,768]{1,0:T(8,128)S(1)}, bf16[512,768]{1,0:T(8,128)(2,1)S(1)}, bf16[512,1536]{1,0:T(8,128)(2,1)S(1)}, b...) custom-call(f32[512,768]{1,0:T(8,128)S(1)} %get-tuple-element.222.x_ref, ...), custom_call_target="tpu_custom_call" | custom-call | tf_op jit(solution)/shard_map/pallas_call | solution.py:642
  172.6 3.2 collective-permute-start.26
  175.7 1.9 collective-permute-done.26.theirs_ref
  177.7 2.2 shard_map.190
  180.7 2.9 shard_map.191
  184.3 3.9 %shard_map.193 = (bf16[768,768]{1,0:T(8,128)(2,1)S(1)}, bf16[768,768]{1,0:T(8,128)(2,1)S(1)}, bf16[512,768]{1,0:T(8,128)(2,1)S(1)}, f32[1,1536]{1,0:T(1,128)S(1)}) custom-call(bf16[512,768]{1,0:T(8,128)(2,1)S(1)} %get-tuple-element.253.d_ffn_ref, bf16[512,1536]{1,0:T(8,128)(2,1)S(1)} %get-tuple-element.254.slope_ref, ...), custom_call_target="tpu_custom_call" | custom-call | tf_op jit(solution)/shard_map/pallas_call | solution.py:642
  188.8 1.4 collective-permute-start.27
  191.0 16.8 %shard_map.195 = (bf16[768,768]{1,0:T(8,128)(2,1)S(1)}, bf16[768,384]{1,0:T(8,128)(2,1)S(1)}, bf16[384,768]{1,0:T(8,128)(2,1)S(1)}, bf16[512,768]{1,0:T(8,128)(2...) custom-call(s32[1]{0:T(128)S(6)} %copy.100.kind_ref, ...), custom_call_target="tpu_custom_call" | custom-call | tf_op jit(solution)/shard_map/pallas_call | solution.py:642
  208.9 2.1 collective-permute-done.30
  211.9 1.4 collective-permute-start.35
  213.3 3.5 collective-permute-done.28.refs_4_
  217.9 1.3 collective-permute-start.31
  219.2 3.1 shard_map.198
  223.4 3.9 %shard_map.200 = (bf16[768,768]{1,0:T(8,128)(2,1)S(1)}, bf16[768,768]{1,0:T(8,128)(2,1)S(1)}, bf16[512,768]{1,0:T(8,128)(2,1)S(1)}, f32[1,1536]{1,0:T(1,128)S(1)}) custom-call(bf16[512,768]{1,0:T(8,128)(2,1)S(1)} %get-tuple-element.288.d_ffn_ref, bf16[512,1536]{1,0:T(8,128)(2,1)S(1)} %get-tuple-element.289.slope_ref, bf16[512,768]{1,0:T(8,128)(2,1)S(1)} %copy-done.5, ...), custom_call_target="tpu_custom_call" | custom-call | tf_op jit(solution)/shard_map/pallas_call | solution.py:642
  227.3 1.4 collective-permute-start.33
  229.6 1.4 collective-permute-start.38
  230.9 16.9 %shard_map.202 = (bf16[768,768]{1,0:T(8,128)(2,1)S(1)}, bf16[768,384]{1,0:T(8,128)(2,1)S(1)}, bf16[384,768]{1,0:T(8,128)(2,1)S(1)}, bf16[512,768]{1,0:T(8,128)(2...) custom-call(s32[1]{0:T(128)S(6)} %copy.100.kind_ref, ...), custom_call_target="tpu_custom_call" | custom-call | tf_op jit(solution)/shard_map/pallas_call | solution.py:642
  251.2 1.3 collective-permute-start.36
  252.6 6.7 %collective-permute-done.37.refs_3_ = bf16[4,2,96,768]{3,2,1,0:T(8,128)(2,1)S(1)} collective-permute-done((bf16[4,2,96,768]{3,2,1,0:T(8,128)(2,1)S(1)}, bf16[4,2,96,768]{3,2,1,0:T(8,128)(2,1)S(1)}, u32[]{:S(2)}, u32[]{:S(2)}) %collective-permute-start.37) | collective-permute-done | bytes 1179680 | tf_op jit(solution)/shard_map/ppermute | solution.py:81
  259.2 17.7 %collective-permute-done.38.refs_4_ = bf16[4,2,96,768]{3,2,1,0:T(8,128)(2,1)S(1)} collective-permute-done((bf16[4,2,96,768]{3,2,1,0:T(8,128)(2,1)S(1)}, bf16[4,2,96,768]{3,2,1,0:T(8,128)(2,1)S(1)}, u32[]{:S(2)}, u32[]{:S(2)}) %collective-permute-start.38) | collective-permute-done | bytes 1179680 | tf_op jit(solution)/shard_map/ppermute | solution.py:81
  276.9 2.0 shard_map.205
  280.1 1.4 shard_map.206
  282.2 1.4 collective-permute-start.42
  285.2 1.7 shard_map.208
  287.3 2.2 collective-permute-start.39
  289.5 1.8 constant_dynamic-slice_fusion
  291.2 7.2 %collective-permute-done.44 = bf16[2,1,112,768]{3,2,0,1:T(8,128)(2,1)} collective-permute-done((bf16[2,1,112,768]{3,2,0,1:T(8,128)(2,1)}, bf16[2,1,112,768]{3,2,0,1:T(8,128)(2,1)}, u32[]{:S(2)}, u32[]{:S(2)}) %collective-permute-start.44) | collective-permute-done | bytes 344096 | tf_op jit(solution)/shard_map/ppermute | solution.py:48
  299.6 1.7 copy-done.3
  301.2 1.6 shard_map.209
  303.4 2.0 add_add_fusion
  305.6 4.2 %collective-permute-start.43 = (f32[24,1536]{1,0:T(8,128)S(1)}, f32[24,1536]{1,0:T(8,128)S(1)}, u32[]{:S(2)}, u32[]{:S(2)}) collective-permute-start(f32[24,1536]{1,0:T(8,128)S(1)} %get-tuple-element.441), channel_id=1, source_target_pairs={{0,1},{1,0},{2,3},{3,2},{4,5},{5,4},{6,7},{7,6},{8,9},{9,8},{10,11... | collective-permute-start | bytes 442376 | tf_op jit(solution)/shard_map/ppermute | solution.py:48
  310.6 1.7 shard_map.211
  313.6 9.8 %collective-permute-done.46 = bf16[2,1,192,768]{3,2,0,1:T(8,128)(2,1)S(1)} collective-permute-done((bf16[2,1,192,768]{3,2,0,1:T(8,128)(2,1)S(1)}, bf16[2,1,192,768]{3,2,0,1:T(8,128)(2,1)S(1)}, u32[]{:S(2)}, u32[]{:S(2)}) %collective-permute-start.46) | collective-permute-done | bytes 589856 | tf_op jit(solution)/shard_map/ppermute | solution.py:48
  326.1 2.3 collective-permute-start.50
  329.6 11.7 %collective-permute-done.50 = bf16[2,1,112,768]{3,2,0,1:T(8,128)(2,1)S(1)} collective-permute-done((bf16[2,1,112,768]{3,2,0,1:T(8,128)(2,1)S(1)}, bf16[2,1,112,768]{3,2,0,1:T(8,128)(2,1)S(1)}, u32[]{:S(2)}, u32[]{:S(2)}) %collective-permute-start.50) | collective-permute-done | bytes 344096 | tf_op jit(solution)/shard_map/ppermute | solution.py:48
  342.5 1.6 collective-permute-start.54
  345.0 7.7 %collective-permute-done.51 = bf16[1,1,112,768]{3,2,1,0:T(8,128)(2,1)S(1)} collective-permute-done((bf16[1,1,112,768]{3,2,1,0:T(8,128)(2,1)S(1)}, bf16[1,1,112,768]{3,2,1,0:T(8,128)(2,1)S(1)}, u32[]{:S(2)}, u32[]{:S(2)}) %collective-permute-start.51) | collective-permute-done | bytes 172064 | tf_op jit(solution)/shard_map/ppermute | solution.py:48
  353.5 1.3 fusion.1
  356.5 1.3 fusion
  (350 shorter events, 57.8 us)
Async XLA Ops:
  2.1 1.7 collective-permute-start
  2.4 1.4 collective-permute-start.1
  4.7 4.2 %copy-start.18 = (bf16[2,96,768]{2,1,0:T(8,128)(2,1)S(1)}, bf16[2,96,768]{2,1,0:T(8,128)(2,1)}, u32[]{:S(2)}) copy-start(bf16[2,96,768]{2,1,0:T(8,128)(2,1)} %param.15) | copy-start | bytes 884740
  4.7 4.2 %copy-start.15 = (bf16[256,768]{1,0:T(8,128)(2,1)S(1)}, bf16[256,768]{1,0:T(8,128)(2,1)}, u32[]{:S(2)}) copy-start(bf16[256,768]{1,0:T(8,128)(2,1)} %param.10) | copy-start | bytes 1179652
  4.7 3.9 %collective-permute-start.2 = (bf16[192,384]{1,0:T(8,128)(2,1)S(1)}, bf16[192,384]{1,0:T(8,128)(2,1)S(1)}, u32[]{:S(2)}, u32[]{:S(2)}) collective-permute-start(bf16[192,384]{1,0:T(8,128)(2,1)S(1)} %broadcast_select_fusion.8), channel_id=1, source_target_pairs={{0,1},{1,0},{2,3},{3,2},{4,5},{5,4},{6,7},{7,6},{8,9},{9,8},{10,11... | collective-permute-start | bytes 442376 | tf_op jit(solution)/shard_map/ppermute | solution.py:48
  5.1 11.6 %collective-permute-start.4 = (bf16[1,1,112,768]{3,2,1,0:T(8,128)(2,1)S(1)}, bf16[1,1,112,768]{3,2,1,0:T(8,128)(2,1)S(1)}, u32[]{:S(2)}, u32[]{:S(2)}) collective-permute-start(bf16[1,1,112,768]{3,2,1,0:T(8,128)(2,1)S(1)} %bitcast.289), channel_id=1, source_target_pairs={{0,16},{1,17},{2,18},{3,19},{4,20},{5,21},{6,22},{7,23},{8,24},{9,... | collective-permute-start | bytes 516104 | tf_op jit(solution)/shard_map/ppermute | solution.py:48
  8.9 24.9 %collective-permute-start.3 = (bf16[256,768]{1,0:T(8,128)(2,1)S(1)}, bf16[256,768]{1,0:T(8,128)(2,1)S(1)}, u32[]{:S(2)}, u32[]{:S(2)}) collective-permute-start(bf16[256,768]{1,0:T(8,128)(2,1)S(1)} %copy-done.15), channel_id=1, source_target_pairs={{0,1},{1,0},{2,3},{3,2},{4,5},{5,4},{6,7},{7,6},{8,9},{9,8},{10,11... | collective-permute-start | bytes 1179656 | tf_op jit(solution)/shard_map/ppermute | solution.py:48
  17.3 15.1 %collective-permute-start.5 = (bf16[2,1,112,768]{3,2,1,0:T(8,128)(2,1)S(1)}, bf16[2,1,112,768]{3,2,1,0:T(8,128)(2,1)S(1)}, u32[]{:S(2)}, u32[]{:S(2)}) collective-permute-start(bf16[2,1,112,768]{3,2,1,0:T(8,128)(2,1)S(1)} %bitcast.276), channel_id=1, source_target_pairs={{0,8},{1,9},{2,10},{3,11},{4,12},{5,13},{6,14},{7,15},{8,0},{9,1},... | collective-permute-start | bytes 1032200 | tf_op jit(solution)/shard_map/ppermute | solution.py:48
  18.2 15.7 %collective-permute-start.7 = (bf16[1,1,192,768]{3,2,1,0:T(8,128)(2,1)S(1)}, bf16[1,1,192,768]{3,2,1,0:T(8,128)(2,1)S(1)}, u32[]{:S(2)}, u32[]{:S(2)}) collective-permute-start(bf16[1,1,192,768]{3,2,1,0:T(8,128)(2,1)S(1)} %bitcast.299), channel_id=1, source_target_pairs={{0,16},{1,17},{2,18},{3,19},{4,20},{5,21},{6,22},{7,23},{8,24},{9,... | collective-permute-start | bytes 884744 | tf_op jit(solution)/shard_map/ppermute | solution.py:48
  33.1 10.1 %collective-permute-start.6 = (bf16[4,1,112,768]{3,2,1,0:T(8,128)(2,1)S(1)}, bf16[4,1,112,768]{3,2,1,0:T(8,128)(2,1)S(1)}, u32[]{:S(2)}, u32[]{:S(2)}) collective-permute-start(bf16[4,1,112,768]{3,2,1,0:T(8,128)(2,1)S(1)} %bitcast.264), channel_id=1, source_target_pairs={{0,2},{1,5},{2,0},{3,7},{4,6},{5,1},{6,4},{7,3},{8,10},{9,13},{10,... | collective-permute-start | bytes 2064392 | tf_op jit(solution)/shard_map/ppermute | solution.py:81
  34.6 13.4 %collective-permute-start.9 = (bf16[2,1,192,768]{3,2,1,0:T(8,128)(2,1)S(1)}, bf16[2,1,192,768]{3,2,1,0:T(8,128)(2,1)S(1)}, u32[]{:S(2)}, u32[]{:S(2)}) collective-permute-start(bf16[2,1,192,768]{3,2,1,0:T(8,128)(2,1)S(1)} %bitcast.268), channel_id=1, source_target_pairs={{0,8},{1,9},{2,10},{3,11},{4,12},{5,13},{6,14},{7,15},{8,0},{9,1},... | collective-permute-start | bytes 1769480 | tf_op jit(solution)/shard_map/ppermute | solution.py:48
  43.8 34.9 %collective-permute-start.8 = (bf16[4,2,112,768]{3,2,1,0:T(8,128)(2,1)S(1)}, bf16[4,2,112,768]{3,2,1,0:T(8,128)(2,1)S(1)}, u32[]{:S(2)}, u32[]{:S(2)}) collective-permute-start(bf16[4,2,112,768]{3,2,1,0:T(8,128)(2,1)S(1)} %shard_map.172.mine_ref), channel_id=1, source_target_pairs={{0,4},{1,3},{2,6},{3,1},{4,0},{5,7},{6,2},{7,5},{8,12},{9,11},{10,... | collective-permute-start | bytes 4128776 | tf_op jit(solution)/shard_map/ppermute | solution.py:81
  48.6 28.1 %collective-permute-start.10 = (bf16[4,1,192,768]{3,2,1,0:T(8,128)(2,1)S(1)}, bf16[4,1,192,768]{3,2,1,0:T(8,128)(2,1)S(1)}, u32[]{:S(2)}, u32[]{:S(2)}) collective-permute-start(bf16[4,1,192,768]{3,2,1,0:T(8,128)(2,1)S(1)} %bitcast.244), channel_id=1, source_target_pairs={{0,2},{1,5},{2,0},{3,7},{4,6},{5,1},{6,4},{7,3},{8,10},{9,13},{10,... | collective-permute-start | bytes 3538952 | tf_op jit(solution)/shard_map/ppermute | solution.py:81
  49.9 5.2 %collective-permute-start.11 = (bf16[1,1,112,768]{3,2,1,0:T(8,128)(2,1)S(1)}, bf16[1,1,112,768]{3,2,1,0:T(8,128)(2,1)S(1)}, u32[]{:S(2)}, u32[]{:S(2)}) collective-permute-start(bf16[1,1,112,768]{3,2,1,0:T(8,128)(2,1)S(1)} %bitcast.287), channel_id=1, source_target_pairs={{0,16},{1,17},{2,18},{3,19},{4,20},{5,21},{6,22},{7,23},{8,24},{9,... | collective-permute-start | bytes 516104 | tf_op jit(solution)/shard_map/ppermute | solution.py:48
  52.2 27.6 %collective-permute-start.14 = (bf16[1,1,192,768]{3,2,1,0:T(8,128)(2,1)S(1)}, bf16[1,1,192,768]{3,2,1,0:T(8,128)(2,1)S(1)}, u32[]{:S(2)}, u32[]{:S(2)}) collective-permute-start(bf16[1,1,192,768]{3,2,1,0:T(8,128)(2,1)S(1)} %bitcast.301), channel_id=1, source_target_pairs={{0,16},{1,17},{2,18},{3,19},{4,20},{5,21},{6,22},{7,23},{8,24},{9,... | collective-permute-start | bytes 884744 | tf_op jit(solution)/shard_map/ppermute | solution.py:48
  55.6 41.2 %collective-permute-start.13 = (bf16[2,1,112,768]{3,2,1,0:T(8,128)(2,1)S(1)}, bf16[2,1,112,768]{3,2,1,0:T(8,128)(2,1)S(1)}, u32[]{:S(2)}, u32[]{:S(2)}) collective-permute-start(bf16[2,1,112,768]{3,2,1,0:T(8,128)(2,1)S(1)} %bitcast.274), channel_id=1, source_target_pairs={{0,8},{1,9},{2,10},{3,11},{4,12},{5,13},{6,14},{7,15},{8,0},{9,1},... | collective-permute-start | bytes 1032200 | tf_op jit(solution)/shard_map/ppermute | solution.py:48
  77.4 48.3 %collective-permute-start.19 = (bf16[4,2,192,768]{3,2,1,0:T(8,128)(2,1)S(1)}, bf16[4,2,192,768]{3,2,1,0:T(8,128)(2,1)S(1)}, u32[]{:S(2)}, u32[]{:S(2)}) collective-permute-start(bf16[4,2,192,768]{3,2,1,0:T(8,128)(2,1)S(1)} %shard_map.175.mine_ref), channel_id=1, source_target_pairs={{0,4},{1,3},{2,6},{3,1},{4,0},{5,7},{6,2},{7,5},{8,12},{9,11},{10,... | collective-permute-start | bytes 7077896 | tf_op jit(solution)/shard_map/ppermute | solution.py:81
  79.7 1.6 collective-permute-start.12
  80.5 14.5 %collective-permute-start.15 = (bf16[2,1,192,768]{3,2,1,0:T(8,128)(2,1)S(1)}, bf16[2,1,192,768]{3,2,1,0:T(8,128)(2,1)S(1)}, u32[]{:S(2)}, u32[]{:S(2)}) collective-permute-start(bf16[2,1,192,768]{3,2,1,0:T(8,128)(2,1)S(1)} %bitcast.266), channel_id=1, source_target_pairs={{0,8},{1,9},{2,10},{3,11},{4,12},{5,13},{6,14},{7,15},{8,0},{9,1},... | collective-permute-start | bytes 1769480 | tf_op jit(solution)/shard_map/ppermute | solution.py:48
  95.5 29.4 %collective-permute-start.17 = (bf16[4,1,192,768]{3,2,1,0:T(8,128)(2,1)S(1)}, bf16[4,1,192,768]{3,2,1,0:T(8,128)(2,1)S(1)}, u32[]{:S(2)}, u32[]{:S(2)}) collective-permute-start(bf16[4,1,192,768]{3,2,1,0:T(8,128)(2,1)S(1)} %bitcast.242), channel_id=1, source_target_pairs={{0,2},{1,5},{2,0},{3,7},{4,6},{5,1},{6,4},{7,3},{8,10},{9,13},{10,... | collective-permute-start | bytes 3538952 | tf_op jit(solution)/shard_map/ppermute | solution.py:81
  97.5 26.2 %collective-permute-start.18 = (bf16[4,1,112,768]{3,2,1,0:T(8,128)(2,1)S(1)}, bf16[4,1,112,768]{3,2,1,0:T(8,128)(2,1)S(1)}, u32[]{:S(2)}, u32[]{:S(2)}) collective-permute-start(bf16[4,1,112,768]{3,2,1,0:T(8,128)(2,1)S(1)} %bitcast.262), channel_id=1, source_target_pairs={{0,2},{1,5},{2,0},{3,7},{4,6},{5,1},{6,4},{7,3},{8,10},{9,13},{10,... | collective-permute-start | bytes 2064392 | tf_op jit(solution)/shard_map/ppermute | solution.py:81
  110.3 15.3 %copy-start.10 = (f32[512,128]{1,0:T(8,128)}, f32[512,128]{1,0:T(8,128)S(1)}, u32[]{:S(2)}) copy-start(f32[512,128]{1,0:T(8,128)S(1)} %get-tuple-element.299.lse_ref) | copy-start | bytes 786436
  110.4 15.3 %collective-permute-start.16 = (bf16[512,768]{1,0:T(8,128)(2,1)S(1)}, bf16[512,768]{1,0:T(8,128)(2,1)S(1)}, u32[]{:S(2)}, u32[]{:S(2)}) collective-permute-start(bf16[512,768]{1,0:T(8,128)(2,1)S(1)} %get-tuple-element.212.mine_ref), channel_id=1, source_target_pairs={{0,1},{1,0},{2,3},{3,2},{4,5},{5,4},{6,7},{7,6},{8,9},{9,8},{10,11... | collective-permute-start | bytes 2359304 | tf_op jit(solution)/shard_map/ppermute | solution.py:48
  124.3 17.5 %collective-permute-start.21 = (bf16[4,2,112,768]{3,2,1,0:T(8,128)(2,1)S(1)}, bf16[4,2,112,768]{3,2,1,0:T(8,128)(2,1)S(1)}, u32[]{:S(2)}, u32[]{:S(2)}) collective-permute-start(bf16[4,2,112,768]{3,2,1,0:T(8,128)(2,1)S(1)} %shard_map.181.mine_ref), channel_id=1, source_target_pairs={{0,4},{1,3},{2,6},{3,1},{4,0},{5,7},{6,2},{7,5},{8,12},{9,11},{10,... | collective-permute-start | bytes 4128776 | tf_op jit(solution)/shard_map/ppermute | solution.py:81
  131.9 5.1 %collective-permute-start.20 = (bf16[512,768]{1,0:T(8,128)(2,1)S(1)}, bf16[512,768]{1,0:T(8,128)(2,1)S(1)}, u32[]{:S(2)}, u32[]{:S(2)}) collective-permute-start(bf16[512,768]{1,0:T(8,128)(2,1)S(1)} %get-tuple-element.220.mine_ref), channel_id=1, source_target_pairs={{0,1},{1,0},{2,3},{3,2},{4,5},{5,4},{6,7},{7,6},{8,9},{9,8},{10,11... | collective-permute-start | bytes 2359304 | tf_op jit(solution)/shard_map/ppermute | solution.py:48
  135.1 32.0 %collective-permute-start.24 = (bf16[4,2,192,768]{3,2,1,0:T(8,128)(2,1)S(1)}, bf16[4,2,192,768]{3,2,1,0:T(8,128)(2,1)S(1)}, u32[]{:S(2)}, u32[]{:S(2)}) collective-permute-start(bf16[4,2,192,768]{3,2,1,0:T(8,128)(2,1)S(1)} %shard_map.182.mine_ref), channel_id=1, source_target_pairs={{0,4},{1,3},{2,6},{3,1},{4,0},{5,7},{6,2},{7,5},{8,12},{9,11},{10,... | collective-permute-start | bytes 7077896 | tf_op jit(solution)/shard_map/ppermute | solution.py:81
  142.5 3.5 copy-start.16
  142.7 4.4 %collective-permute-start.22 = (bf16[8,48,384]{2,1,0:T(8,128)(2,1)S(1)}, bf16[8,48,384]{2,1,0:T(8,128)(2,1)S(1)}, u32[]{:S(2)}, u32[]{:S(2)}) collective-permute-start(bf16[8,48,384]{2,1,0:T(8,128)(2,1)S(1)} %dynamic-slice_bitcast_fusion.2), channel_id=1, source_target_pairs={{0,1},{1,0},{2,3},{3,2},{4,5},{5,4},{6,7},{7,6},{8,9},{9,8},{10,11... | collective-permute-start | bytes 884744 | tf_op jit(solution)/shard_map/ppermute | solution.py:48
  146.0 13.8 %collective-permute-start.25 = (bf16[256,768]{1,0:T(8,128)(2,1)S(1)}, bf16[256,768]{1,0:T(8,128)(2,1)S(1)}, u32[]{:S(2)}, u32[]{:S(2)}) collective-permute-start(bf16[256,768]{1,0:T(8,128)(2,1)S(1)} %copy-done.16), channel_id=1, source_target_pairs={{0,1},{1,0},{2,3},{3,2},{4,5},{5,4},{6,7},{7,6},{8,9},{9,8},{10,11... | collective-permute-start | bytes 1179656 | tf_op jit(solution)/shard_map/ppermute | solution.py:48
  159.4 2.4 collective-permute-start.23
  172.6 5.1 %collective-permute-start.26 = (bf16[512,768]{1,0:T(8,128)(2,1)S(1)}, bf16[512,768]{1,0:T(8,128)(2,1)S(1)}, u32[]{:S(2)}, u32[]{:S(2)}) collective-permute-start(bf16[512,768]{1,0:T(8,128)(2,1)S(1)} %get-tuple-element.245.mine_ref), channel_id=1, source_target_pairs={{0,1},{1,0},{2,3},{3,2},{4,5},{5,4},{6,7},{7,6},{8,9},{9,8},{10,11... | collective-permute-start | bytes 2359304 | tf_op jit(solution)/shard_map/ppermute | solution.py:48
  188.2 2.8 collective-permute-start.29
  188.8 24.5 %collective-permute-start.27 = (bf16[4,2,96,768]{3,2,1,0:T(8,128)(2,1)S(1)}, bf16[4,2,96,768]{3,2,1,0:T(8,128)(2,1)S(1)}, u32[]{:S(2)}, u32[]{:S(2)}) collective-permute-start(bf16[4,2,96,768]{3,2,1,0:T(8,128)(2,1)S(1)} %shard_map.192), channel_id=1, source_target_pairs={{0,4},{1,3},{2,6},{3,1},{4,0},{5,7},{6,2},{7,5},{8,12},{9,11},{10,... | collective-permute-start | bytes 3538952 | tf_op jit(solution)/shard_map/ppermute | solution.py:81
  190.8 26.1 %collective-permute-start.28 = (bf16[4,2,96,768]{3,2,1,0:T(8,128)(2,1)S(1)}, bf16[4,2,96,768]{3,2,1,0:T(8,128)(2,1)S(1)}, u32[]{:S(2)}, u32[]{:S(2)}) collective-permute-start(bf16[4,2,96,768]{3,2,1,0:T(8,128)(2,1)S(1)} %shard_map.194), channel_id=1, source_target_pairs={{0,4},{1,3},{2,6},{3,1},{4,0},{5,7},{6,2},{7,5},{8,12},{9,11},{10,... | collective-permute-start | bytes 3538952 | tf_op jit(solution)/shard_map/ppermute | solution.py:81
  207.8 11.4 %collective-permute-start.32 = (bf16[512,768]{1,0:T(8,128)(2,1)S(1)}, bf16[512,768]{1,0:T(8,128)(2,1)S(1)}, u32[]{:S(2)}, u32[]{:S(2)}) collective-permute-start(bf16[512,768]{1,0:T(8,128)(2,1)S(1)} %get-tuple-element.282.refs_1_), channel_id=1, source_target_pairs={{0,1},{1,0},{2,3},{3,2},{4,5},{5,4},{6,7},{7,6},{8,9},{9,8},{10,11... | collective-permute-start | bytes 2359304 | tf_op jit(solution)/shard_map/ppermute | solution.py:48
  208.7 2.3 collective-permute-start.30
  211.9 38.4 %collective-permute-start.35 = (bf16[4,2,112,768]{3,2,1,0:T(8,128)(2,1)S(1)}, bf16[4,2,112,768]{3,2,1,0:T(8,128)(2,1)S(1)}, u32[]{:S(2)}, u32[]{:S(2)}) collective-permute-start(bf16[4,2,112,768]{3,2,1,0:T(8,128)(2,1)S(1)} %shard_map.196), channel_id=1, source_target_pairs={{0,4},{1,3},{2,6},{3,1},{4,0},{5,7},{6,2},{7,5},{8,12},{9,11},{10,... | collective-permute-start | bytes 4128776 | tf_op jit(solution)/shard_map/ppermute | solution.py:81
  217.9 31.6 %collective-permute-start.31 = (bf16[4,1,192,768]{3,2,1,0:T(8,128)(2,1)S(1)}, bf16[4,1,192,768]{3,2,1,0:T(8,128)(2,1)S(1)}, u32[]{:S(2)}, u32[]{:S(2)}) collective-permute-start(bf16[4,1,192,768]{3,2,1,0:T(8,128)(2,1)S(1)} %get-tuple-element.280), channel_id=1, source_target_pairs={{0,2},{1,5},{2,0},{3,7},{4,6},{5,1},{6,4},{7,3},{8,10},{9,13},{10,... | collective-permute-start | bytes 3538952 | tf_op jit(solution)/shard_map/ppermute | solution.py:81
  227.3 3.6 collective-permute-start.33
  228.7 30.5 %collective-permute-start.37 = (bf16[4,2,96,768]{3,2,1,0:T(8,128)(2,1)S(1)}, bf16[4,2,96,768]{3,2,1,0:T(8,128)(2,1)S(1)}, u32[]{:S(2)}, u32[]{:S(2)}) collective-permute-start(bf16[4,2,96,768]{3,2,1,0:T(8,128)(2,1)S(1)} %shard_map.199), channel_id=1, source_target_pairs={{0,4},{1,3},{2,6},{3,1},{4,0},{5,7},{6,2},{7,5},{8,12},{9,11},{10,... | collective-permute-start | bytes 3538952 | tf_op jit(solution)/shard_map/ppermute | solution.py:81
  229.6 47.3 %collective-permute-start.38 = (bf16[4,2,96,768]{3,2,1,0:T(8,128)(2,1)S(1)}, bf16[4,2,96,768]{3,2,1,0:T(8,128)(2,1)S(1)}, u32[]{:S(2)}, u32[]{:S(2)}) collective-permute-start(bf16[4,2,96,768]{3,2,1,0:T(8,128)(2,1)S(1)} %shard_map.201), channel_id=1, source_target_pairs={{0,4},{1,3},{2,6},{3,1},{4,0},{5,7},{6,2},{7,5},{8,12},{9,11},{10,... | collective-permute-start | bytes 3538952 | tf_op jit(solution)/shard_map/ppermute | solution.py:81
  248.9 54.0 %collective-permute-start.40 = (bf16[256,768]{1,0:T(8,128)(2,1)}, bf16[256,768]{1,0:T(8,128)(2,1)}, u32[]{:S(2)}, u32[]{:S(2)}) collective-permute-start(bf16[256,768]{1,0:T(8,128)(2,1)} %get-tuple-element.393), channel_id=1, source_target_pairs={{0,1},{1,0},{2,3},{3,2},{4,5},{5,4},{6,7},{7,6},{8,9},{9,8},{10,11... | collective-permute-start | bytes 1179656 | tf_op jit(solution)/shard_map/ppermute | solution.py:48
  250.2 31.3 %collective-permute-start.34 = (bf16[2,1,192,768]{3,2,0,1:T(8,128)(2,1)S(1)}, bf16[2,1,192,768]{3,2,0,1:T(8,128)(2,1)S(1)}, u32[]{:S(2)}, u32[]{:S(2)}) collective-permute-start(bf16[2,1,192,768]{3,2,0,1:T(8,128)(2,1)S(1)} %bitcast.304), channel_id=1, source_target_pairs={{0,8},{1,9},{2,10},{3,11},{4,12},{5,13},{6,14},{7,15},{8,0},{9,1},... | collective-permute-start | bytes 1769480 | tf_op jit(solution)/shard_map/ppermute | solution.py:48
  251.2 28.9 %collective-permute-start.36 = (bf16[4,1,112,768]{3,2,1,0:T(8,128)(2,1)S(1)}, bf16[4,1,112,768]{3,2,1,0:T(8,128)(2,1)S(1)}, u32[]{:S(2)}, u32[]{:S(2)}) collective-permute-start(bf16[4,1,112,768]{3,2,1,0:T(8,128)(2,1)S(1)} %get-tuple-element.306), channel_id=1, source_target_pairs={{0,2},{1,5},{2,0},{3,7},{4,6},{5,1},{6,4},{7,3},{8,10},{9,13},{10,... | collective-permute-start | bytes 2064392 | tf_op jit(solution)/shard_map/ppermute | solution.py:81
  278.9 3.3 copy-start.2
  278.9 20.7 %collective-permute-start.41 = (bf16[4,1,192,768]{3,2,1,0:T(8,128)(2,1)}, bf16[4,1,192,768]{3,2,1,0:T(8,128)(2,1)}, u32[]{:S(2)}, u32[]{:S(2)}) collective-permute-start(bf16[4,1,192,768]{3,2,1,0:T(8,128)(2,1)} %get-tuple-element.309), channel_id=1, source_target_pairs={{0,2},{1,5},{2,0},{3,7},{4,6},{5,1},{6,4},{7,3},{8,10},{9,13},{10,... | collective-permute-start | bytes 3538952 | tf_op jit(solution)/shard_map/ppermute | solution.py:81
  282.2 2.8 copy-start.6
  282.2 2.8 copy-start.13
  282.2 2.6 collective-permute-start.42
  283.7 14.7 %collective-permute-start.44 = (bf16[2,1,112,768]{3,2,0,1:T(8,128)(2,1)}, bf16[2,1,112,768]{3,2,0,1:T(8,128)(2,1)}, u32[]{:S(2)}, u32[]{:S(2)}) collective-permute-start(bf16[2,1,112,768]{3,2,0,1:T(8,128)(2,1)} %bitcast.99), channel_id=1, source_target_pairs={{0,8},{1,9},{2,10},{3,11},{4,12},{5,13},{6,14},{7,15},{8,0},{9,1},... | collective-permute-start | bytes 1032200 | tf_op jit(solution)/shard_map/ppermute | solution.py:48
  286.9 23.7 %collective-permute-start.47 = (bf16[4,2,112,768]{3,2,1,0:T(8,128)(2,1)}, bf16[4,2,112,768]{3,2,1,0:T(8,128)(2,1)}, u32[]{:S(2)}, u32[]{:S(2)}) collective-permute-start(bf16[4,2,112,768]{3,2,1,0:T(8,128)(2,1)} %shard_map.208), channel_id=1, source_target_pairs={{0,4},{1,3},{2,6},{3,1},{4,0},{5,7},{6,2},{7,5},{8,12},{9,11},{10,... | collective-permute-start | bytes 4128776 | tf_op jit(solution)/shard_map/ppermute | solution.py:81
  287.3 18.1 %collective-permute-start.39 = (bf16[1,1,192,768]{3,2,1,0:T(8,128)(2,1)}, bf16[1,1,192,768]{3,2,1,0:T(8,128)(2,1)S(1)}, u32[]{:S(2)}, u32[]{:S(2)}) collective-permute-start(bf16[1,1,192,768]{3,2,1,0:T(8,128)(2,1)} %copy-done.13), channel_id=1, source_target_pairs={{0,16},{1,17},{2,18},{3,19},{4,20},{5,21},{6,22},{7,23},{8,24},{9,... | collective-permute-start | bytes 884744 | tf_op jit(solution)/shard_map/ppermute | solution.py:48
  299.5 25.8 %collective-permute-start.45 = (bf16[1,1,112,768]{3,2,1,0:T(8,128)(2,1)S(1)}, bf16[1,1,112,768]{3,2,1,0:T(8,128)(2,1)S(1)}, u32[]{:S(2)}, u32[]{:S(2)}) collective-permute-start(bf16[1,1,112,768]{3,2,1,0:T(8,128)(2,1)S(1)} %get-tuple-element.334), channel_id=1, source_target_pairs={{0,16},{1,17},{2,18},{3,19},{4,20},{5,21},{6,22},{7,23},{8,24},{9,... | collective-permute-start | bytes 516104 | tf_op jit(solution)/shard_map/ppermute | solution.py:48
  302.8 2.6 copy-start.7
  302.9 20.5 %collective-permute-start.46 = (bf16[2,1,192,768]{3,2,0,1:T(8,128)(2,1)S(1)}, bf16[2,1,192,768]{3,2,0,1:T(8,128)(2,1)S(1)}, u32[]{:S(2)}, u32[]{:S(2)}) collective-permute-start(bf16[2,1,192,768]{3,2,0,1:T(8,128)(2,1)S(1)} %bitcast.305), channel_id=1, source_target_pairs={{0,8},{1,9},{2,10},{3,11},{4,12},{5,13},{6,14},{7,15},{8,0},{9,1},... | collective-permute-start | bytes 1769480 | tf_op jit(solution)/shard_map/ppermute | solution.py:48
  305.6 50.9 %collective-permute-start.43 = (f32[24,1536]{1,0:T(8,128)S(1)}, f32[24,1536]{1,0:T(8,128)S(1)}, u32[]{:S(2)}, u32[]{:S(2)}) collective-permute-start(f32[24,1536]{1,0:T(8,128)S(1)} %get-tuple-element.441), channel_id=1, source_target_pairs={{0,1},{1,0},{2,3},{3,2},{4,5},{5,4},{6,7},{7,6},{8,9},{9,8},{10,11... | collective-permute-start | bytes 442376 | tf_op jit(solution)/shard_map/ppermute | solution.py:48
  312.3 13.1 %collective-permute-start.49 = (bf16[4,1,112,768]{3,2,1,0:T(8,128)(2,1)S(1)}, bf16[4,1,112,768]{3,2,1,0:T(8,128)(2,1)S(1)}, u32[]{:S(2)}, u32[]{:S(2)}) collective-permute-start(bf16[4,1,112,768]{3,2,1,0:T(8,128)(2,1)S(1)} %get-tuple-element.337), channel_id=1, source_target_pairs={{0,2},{1,5},{2,0},{3,7},{4,6},{5,1},{6,4},{7,3},{8,10},{9,13},{10,... | collective-permute-start | bytes 2064392 | tf_op jit(solution)/shard_map/ppermute | solution.py:81
  324.0 18.4 %collective-permute-start.53 = (bf16[1,1,192,768]{3,2,1,0:T(8,128)(2,1)S(1)}, bf16[1,1,192,768]{3,2,1,0:T(8,128)(2,1)S(1)}, u32[]{:S(2)}, u32[]{:S(2)}) collective-permute-start(bf16[1,1,192,768]{3,2,1,0:T(8,128)(2,1)S(1)} %get-tuple-element.339), channel_id=1, source_target_pairs={{0,16},{1,17},{2,18},{3,19},{4,20},{5,21},{6,22},{7,23},{8,24},{9,... | collective-permute-start | bytes 884744 | tf_op jit(solution)/shard_map/ppermute | solution.py:48
  326.1 15.2 %collective-permute-start.50 = (bf16[2,1,112,768]{3,2,0,1:T(8,128)(2,1)S(1)}, bf16[2,1,112,768]{3,2,0,1:T(8,128)(2,1)S(1)}, u32[]{:S(2)}, u32[]{:S(2)}) collective-permute-start(bf16[2,1,112,768]{3,2,0,1:T(8,128)(2,1)S(1)} %bitcast.306), channel_id=1, source_target_pairs={{0,8},{1,9},{2,10},{3,11},{4,12},{5,13},{6,14},{7,15},{8,0},{9,1},... | collective-permute-start | bytes 1032200 | tf_op jit(solution)/shard_map/ppermute | solution.py:48
  328.4 27.5 %collective-permute-start.48 = (f32[32,1152]{1,0:T(8,128)S(1)}, f32[32,1152]{1,0:T(8,128)S(1)}, u32[]{:S(2)}, u32[]{:S(2)}) collective-permute-start(f32[32,1152]{1,0:T(8,128)S(1)} %select_maximum_fusion.1), channel_id=1, source_target_pairs={{0,1},{1,0},{2,3},{3,2},{4,5},{5,4},{6,7},{7,6},{8,9},{9,8},{10,11... | collective-permute-start | bytes 442376 | tf_op jit(solution)/shard_map/ppermute | solution.py:48
  342.0 10.8 %collective-permute-start.51 = (bf16[1,1,112,768]{3,2,1,0:T(8,128)(2,1)S(1)}, bf16[1,1,112,768]{3,2,1,0:T(8,128)(2,1)S(1)}, u32[]{:S(2)}, u32[]{:S(2)}) collective-permute-start(bf16[1,1,112,768]{3,2,1,0:T(8,128)(2,1)S(1)} %get-tuple-element.347), channel_id=1, source_target_pairs={{0,16},{1,17},{2,18},{3,19},{4,20},{5,21},{6,22},{7,23},{8,24},{9,... | collective-permute-start | bytes 516104 | tf_op jit(solution)/shard_map/ppermute | solution.py:48
  342.5 10.9 %collective-permute-start.54 = (f32[24,1536]{1,0:T(8,128)S(1)}, f32[24,1536]{1,0:T(8,128)S(1)}, u32[]{:S(2)}, u32[]{:S(2)}) collective-permute-start(f32[24,1536]{1,0:T(8,128)S(1)} %get-tuple-element.433), channel_id=1, source_target_pairs={{0,1},{1,0},{2,3},{3,2},{4,5},{5,4},{6,7},{7,6},{8,9},{9,8},{10,11... | collective-permute-start | bytes 442376 | tf_op jit(solution)/shard_map/ppermute | solution.py:48
  352.9 2.7 collective-permute-start.52
  356.5 4.9 %copy-start.1 = (bf16[2,96]{1,0:T(2,128)(2,1)S(1)}, bf16[2,96]{1,0:T(2,128)(2,1)}, u32[]{:S(2)}) copy-start(bf16[2,96]{1,0:T(2,128)(2,1)} %param.18) | copy-start | bytes 1156
  (13 other events, 22.7 us)

commit v5 on v4

--- a/solution.py
+++ b/solution.py
@@ -26,7 +26,7 @@
 LATE = (False, False, False, False)
 ORDER = (
     0, 6, 1, 2, 7, 11, 16, 8, 3, 12, 21, 9, 13, 17, 14, 10, 22, 15, 23, 18, 26, 19, 24,
-    27, 28, 20, 4, 29, 5, 25, 30, 31, 33, 34, 35, 36, 37, 47, 48, 49, 38, 42, 51, 43, 39,
+    27, 28, 20, 4, 29, 5, 25, 30, 31, 33, 34, 35, 36, 37, 47, 48, 49, 38, 42, 51, 39, 43,
     50, 52, 61, 40, 44, 56, 53, 45, 57, 58, 54, 59, 55, 60, 46, 41, 32,
 )
 

time: 367 us -> 368 us (level)
  no operation moved by 1% of the time
where the time goes in v5:
time: 368 us; the launch traced here: 363 us
  waiting for transfers between devices  148 us (40%)
  Pallas kernels  113 us (31%)
  starting transfers between devices  74.5 us (20%)
  local copies, waits for them, and re-layouts  10.2 us (3%)
  other arithmetic  10.2 us (3%)
    pallas_call x46, Pallas kernels, kernel_call(): pl.pallas_call(body, out_shape=shapes, in_specs=[in_smem if value.dtype =...  113 us
    ppermute x37, waiting for transfers between devices, swap(): return lax.ppermute(value, AXIS, pairs)  83.3 us
    ppermute x18, waiting for transfers between devices, plane_swap(): return lax.ppermute(value, AXIS, pairs)  64.5 us
    ppermute x37, starting transfers between devices, swap(): return lax.ppermute(value, AXIS, pairs)  57 us
    ppermute x18, starting transfers between devices, plane_swap(): return lax.ppermute(value, AXIS, pairs)  17.5 us
  transfers between devices with their start and end apart: 55, of which 26 were waited for; matrix products, arithmetic and copies ran while one was open for 3% of the time, Pallas kernels for 27%

profile of v5, /device:TPU:1, one launch (start us, length us, event | category | flops | bytes accessed | tf_op | source)
XLA Modules:
  0.0 362.6 jit_solution(11999861933646719846)
XLA Ops:
  5.1 3.5 collective-permute-start.4
  9.6 7.1 %collective-permute-done.4.theirs_ref = bf16[1,1,112,768]{3,2,1,0:T(8,128)(2,1)S(1)} collective-permute-done((bf16[1,1,112,768]{3,2,1,0:T(8,128)(2,1)S(1)}, bf16[1,1,112,768]{3,2,1,0:T(8,128)(2,1)S(1)}, u32[]{:S(2)}, u32[]{:S(2)}) %collective-permute-start.4) | collective-permute-done | bytes 172064 | tf_op jit(solution)/shard_map/ppermute | solution.py:48
  18.2 3.1 collective-permute-start.7
  21.3 11.1 %collective-permute-done.5.theirs_ref = bf16[2,1,112,768]{3,2,1,0:T(8,128)(2,1)S(1)} collective-permute-done((bf16[2,1,112,768]{3,2,1,0:T(8,128)(2,1)S(1)}, bf16[2,1,112,768]{3,2,1,0:T(8,128)(2,1)S(1)}, u32[]{:S(2)}, u32[]{:S(2)}) %collective-permute-start.5) | collective-permute-done | bytes 344096 | tf_op jit(solution)/shard_map/ppermute | solution.py:48
  34.6 1.8 collective-permute-start.9
  36.3 6.9 %collective-permute-done.6.theirs_ref = bf16[4,1,112,768]{3,2,1,0:T(8,128)(2,1)S(1)} collective-permute-done((bf16[4,1,112,768]{3,2,1,0:T(8,128)(2,1)S(1)}, bf16[4,1,112,768]{3,2,1,0:T(8,128)(2,1)S(1)}, u32[]{:S(2)}, u32[]{:S(2)}) %collective-permute-start.6) | collective-permute-done | bytes 688160 | tf_op jit(solution)/shard_map/ppermute | solution.py:81
  44.5 3.5 collective-permute-done.9.theirs_ref
  48.6 1.3 collective-permute-start.10
  49.9 1.7 collective-permute-start.11
  53.0 2.1 collective-permute-done.11.theirs_ref
  55.6 11.9 %collective-permute-start.13 = (bf16[2,1,112,768]{3,2,1,0:T(8,128)(2,1)S(1)}, bf16[2,1,112,768]{3,2,1,0:T(8,128)(2,1)S(1)}, u32[]{:S(2)}, u32[]{:S(2)}) collective-permute-start(bf16[2,1,112,768]{3,2,1,0:T(8,128)(2,1)S(1)} %bitcast.274), channel_id=1, source_target_pairs={{0,8},{1,9},{2,10},{3,11},{4,12},{5,13},{6,14},{7,15},{8,0},{9,1},... | collective-permute-start | bytes 1032200 | tf_op jit(solution)/shard_map/ppermute | solution.py:48
  67.5 9.2 %collective-permute-done.10.theirs_ref = bf16[4,1,192,768]{3,2,1,0:T(8,128)(2,1)S(1)} collective-permute-done((bf16[4,1,192,768]{3,2,1,0:T(8,128)(2,1)S(1)}, bf16[4,1,192,768]{3,2,1,0:T(8,128)(2,1)S(1)}, u32[]{:S(2)}, u32[]{:S(2)}) %collective-permute-start.10) | collective-permute-done | bytes 1179680 | tf_op jit(solution)/shard_map/ppermute | solution.py:81
  77.4 1.4 collective-permute-start.19
  81.4 13.5 %collective-permute-done.15.theirs_ref = bf16[2,1,192,768]{3,2,1,0:T(8,128)(2,1)S(1)} collective-permute-done((bf16[2,1,192,768]{3,2,1,0:T(8,128)(2,1)S(1)}, bf16[2,1,192,768]{3,2,1,0:T(8,128)(2,1)S(1)}, u32[]{:S(2)}, u32[]{:S(2)}) %collective-permute-start.15) | collective-permute-done | bytes 589856 | tf_op jit(solution)/shard_map/ppermute | solution.py:48
  95.5 1.3 collective-permute-start.17
  97.9 12.4 %shard_map.180 = (bf16[512,768]{1,0:T(8,128)(2,1)S(1)}, bf16[512,1152]{1,0:T(8,128)(2,1)S(1)}, bf16[512,384]{1,0:T(8,128)(2,1)S(1)}, f32[512,128]{1,0:T(8,128)S(1)}) custom-call(s32[1]{0:T(128)S(6)} %copy.100.kind_ref, bf16[512,768]{1,0:T(8,128)(2,1)S(1)} %get-tuple-element.205.x_ref, bf16[768,768]{1,0:T(8,128)(2,1)S(1)} %bitcast.254, ...), custom_call_target="tpu_custom_call" | custom-call | tf_op jit(solution)/shard_map/pallas_call | solution.py:642
  110.4 2.0 collective-permute-start.16
  112.3 11.3 %collective-permute-done.18.theirs_ref = bf16[4,1,112,768]{3,2,1,0:T(8,128)(2,1)S(1)} collective-permute-done((bf16[4,1,112,768]{3,2,1,0:T(8,128)(2,1)S(1)}, bf16[4,1,112,768]{3,2,1,0:T(8,128)(2,1)S(1)}, u32[]{:S(2)}, u32[]{:S(2)}) %collective-permute-start.18) | collective-permute-done | bytes 688160 | tf_op jit(solution)/shard_map/ppermute | solution.py:81
  126.5 4.5 %shard_map.184 = (f32[512,768]{1,0:T(8,128)S(1)}, f32[512,768]{1,0:T(8,128)S(1)}, bf16[512,768]{1,0:T(8,128)(2,1)S(1)}, bf16[512,1536]{1,0:T(8,128)(2,1)S(1)}, b...) custom-call(f32[512,768]{1,0:T(8,128)S(1)} %get-tuple-element.398.x_ref, ...), custom_call_target="tpu_custom_call" | custom-call | tf_op jit(solution)/shard_map/pallas_call | solution.py:642
  131.9 3.2 collective-permute-start.20
  138.1 3.7 %collective-permute-done.21.theirs_ref = bf16[4,2,112,768]{3,2,1,0:T(8,128)(2,1)S(1)} collective-permute-done((bf16[4,2,112,768]{3,2,1,0:T(8,128)(2,1)S(1)}, bf16[4,2,112,768]{3,2,1,0:T(8,128)(2,1)S(1)}, u32[]{:S(2)}, u32[]{:S(2)}) %collective-permute-start.21) | collective-permute-done | bytes 1376288 | tf_op jit(solution)/shard_map/ppermute | solution.py:81
  142.7 3.2 collective-permute-start.22
  147.4 12.0 %shard_map.187 = (bf16[512,768]{1,0:T(8,128)(2,1)S(1)}, bf16[512,1152]{1,0:T(8,128)(2,1)S(1)}, bf16[512,384]{1,0:T(8,128)(2,1)S(1)}, f32[512,128]{1,0:T(8,128)S(1)}) custom-call(s32[1]{0:T(128)S(6)} %copy.100.kind_ref, bf16[512,768]{1,0:T(8,128)(2,1)S(1)} %get-tuple-element.230.x_ref, bf16[768,768]{1,0:T(8,128)(2,1)S(1)} %bitcast.258, ...), custom_call_target="tpu_custom_call" | custom-call | tf_op jit(solution)/shard_map/pallas_call | solution.py:642
  160.0 1.8 collective-permute-done.23.theirs_ref
  161.7 5.3 %collective-permute-done.24.theirs_ref = bf16[4,2,192,768]{3,2,1,0:T(8,128)(2,1)S(1)} collective-permute-done((bf16[4,2,192,768]{3,2,1,0:T(8,128)(2,1)S(1)}, bf16[4,2,192,768]{3,2,1,0:T(8,128)(2,1)S(1)}, u32[]{:S(2)}, u32[]{:S(2)}) %collective-permute-start.24) | collective-permute-done | bytes 2359328 | tf_op jit(solution)/shard_map/ppermute | solution.py:81
  167.9 4.7 %shard_map.189 = (f32[512,768]{1,0:T(8,128)S(1)}, f32[512,768]{1,0:T(8,128)S(1)}, bf16[512,768]{1,0:T(8,128)(2,1)S(1)}, bf16[512,1536]{1,0:T(8,128)(2,1)S(1)}, b...) custom-call(f32[512,768]{1,0:T(8,128)S(1)} %get-tuple-element.222.x_ref, ...), custom_call_target="tpu_custom_call" | custom-call | tf_op jit(solution)/shard_map/pallas_call | solution.py:642
  172.6 3.2 collective-permute-start.26
  175.7 1.9 collective-permute-done.26.theirs_ref
  177.7 2.2 shard_map.190
  180.7 2.9 shard_map.191
  184.3 3.9 %shard_map.193 = (bf16[768,768]{1,0:T(8,128)(2,1)S(1)}, bf16[768,768]{1,0:T(8,128)(2,1)S(1)}, bf16[512,768]{1,0:T(8,128)(2,1)S(1)}, f32[1,1536]{1,0:T(1,128)S(1)}) custom-call(bf16[512,768]{1,0:T(8,128)(2,1)S(1)} %get-tuple-element.253.d_ffn_ref, bf16[512,1536]{1,0:T(8,128)(2,1)S(1)} %get-tuple-element.254.slope_ref, ...), custom_call_target="tpu_custom_call" | custom-call | tf_op jit(solution)/shard_map/pallas_call | solution.py:642
  188.8 1.4 collective-permute-start.27
  191.0 16.8 %shard_map.195 = (bf16[768,768]{1,0:T(8,128)(2,1)S(1)}, bf16[768,384]{1,0:T(8,128)(2,1)S(1)}, bf16[384,768]{1,0:T(8,128)(2,1)S(1)}, bf16[512,768]{1,0:T(8,128)(2...) custom-call(s32[1]{0:T(128)S(6)} %copy.100.kind_ref, ...), custom_call_target="tpu_custom_call" | custom-call | tf_op jit(solution)/shard_map/pallas_call | solution.py:642
  208.9 2.1 collective-permute-done.30
  211.9 1.4 collective-permute-start.37
  213.3 3.5 collective-permute-done.28.refs_4_
  217.9 1.3 collective-permute-start.31
  219.2 3.1 shard_map.198
  223.4 3.9 %shard_map.200 = (bf16[768,768]{1,0:T(8,128)(2,1)S(1)}, bf16[768,768]{1,0:T(8,128)(2,1)S(1)}, bf16[512,768]{1,0:T(8,128)(2,1)S(1)}, f32[1,1536]{1,0:T(1,128)S(1)}) custom-call(bf16[512,768]{1,0:T(8,128)(2,1)S(1)} %get-tuple-element.288.d_ffn_ref, bf16[512,1536]{1,0:T(8,128)(2,1)S(1)} %get-tuple-element.289.slope_ref, bf16[512,768]{1,0:T(8,128)(2,1)S(1)} %copy-done.5, ...), custom_call_target="tpu_custom_call" | custom-call | tf_op jit(solution)/shard_map/pallas_call | solution.py:642
  227.3 1.4 collective-permute-start.33
  229.6 1.4 collective-permute-start.36
  230.9 16.9 %shard_map.202 = (bf16[768,768]{1,0:T(8,128)(2,1)S(1)}, bf16[768,384]{1,0:T(8,128)(2,1)S(1)}, bf16[384,768]{1,0:T(8,128)(2,1)S(1)}, bf16[512,768]{1,0:T(8,128)(2...) custom-call(s32[1]{0:T(128)S(6)} %copy.100.kind_ref, ...), custom_call_target="tpu_custom_call" | custom-call | tf_op jit(solution)/shard_map/pallas_call | solution.py:642
  251.2 1.3 collective-permute-start.41
  252.6 6.7 %collective-permute-done.35.refs_3_ = bf16[4,2,96,768]{3,2,1,0:T(8,128)(2,1)S(1)} collective-permute-done((bf16[4,2,96,768]{3,2,1,0:T(8,128)(2,1)S(1)}, bf16[4,2,96,768]{3,2,1,0:T(8,128)(2,1)S(1)}, u32[]{:S(2)}, u32[]{:S(2)}) %collective-permute-start.35) | collective-permute-done | bytes 1179680 | tf_op jit(solution)/shard_map/ppermute | solution.py:81
  259.2 17.7 %collective-permute-done.36.refs_4_ = bf16[4,2,96,768]{3,2,1,0:T(8,128)(2,1)S(1)} collective-permute-done((bf16[4,2,96,768]{3,2,1,0:T(8,128)(2,1)S(1)}, bf16[4,2,96,768]{3,2,1,0:T(8,128)(2,1)S(1)}, u32[]{:S(2)}, u32[]{:S(2)}) %collective-permute-start.36) | collective-permute-done | bytes 1179680 | tf_op jit(solution)/shard_map/ppermute | solution.py:81
  276.9 2.0 shard_map.205
  281.6 1.4 shard_map.207
  283.0 1.4 collective-permute-start.42
  285.9 1.7 shard_map.208
  288.0 2.2 collective-permute-start.38
  290.2 1.8 constant_dynamic-slice_fusion
  292.0 7.2 %collective-permute-done.44 = bf16[2,1,112,768]{3,2,0,1:T(8,128)(2,1)} collective-permute-done((bf16[2,1,112,768]{3,2,0,1:T(8,128)(2,1)}, bf16[2,1,112,768]{3,2,0,1:T(8,128)(2,1)}, u32[]{:S(2)}, u32[]{:S(2)}) %collective-permute-start.44) | collective-permute-done | bytes 344096 | tf_op jit(solution)/shard_map/ppermute | solution.py:48
  300.4 1.7 copy-done.3
  302.0 1.6 shard_map.209
  304.2 2.0 add_add_fusion
  306.4 4.1 %collective-permute-start.43 = (f32[24,1536]{1,0:T(8,128)S(1)}, f32[24,1536]{1,0:T(8,128)S(1)}, u32[]{:S(2)}, u32[]{:S(2)}) collective-permute-start(f32[24,1536]{1,0:T(8,128)S(1)} %get-tuple-element.441), channel_id=1, source_target_pairs={{0,1},{1,0},{2,3},{3,2},{4,5},{5,4},{6,7},{7,6},{8,9},{9,8},{10,11... | collective-permute-start | bytes 442376 | tf_op jit(solution)/shard_map/ppermute | solution.py:48
  310.6 1.7 shard_map.211
  313.6 10.5 %collective-permute-done.46 = bf16[2,1,192,768]{3,2,0,1:T(8,128)(2,1)S(1)} collective-permute-done((bf16[2,1,192,768]{3,2,0,1:T(8,128)(2,1)S(1)}, bf16[2,1,192,768]{3,2,0,1:T(8,128)(2,1)S(1)}, u32[]{:S(2)}, u32[]{:S(2)}) %collective-permute-start.46) | collective-permute-done | bytes 589856 | tf_op jit(solution)/shard_map/ppermute | solution.py:48
  326.9 2.3 collective-permute-start.50
  330.4 11.7 %collective-permute-done.50 = bf16[2,1,112,768]{3,2,0,1:T(8,128)(2,1)S(1)} collective-permute-done((bf16[2,1,112,768]{3,2,0,1:T(8,128)(2,1)S(1)}, bf16[2,1,112,768]{3,2,0,1:T(8,128)(2,1)S(1)}, u32[]{:S(2)}, u32[]{:S(2)}) %collective-permute-start.50) | collective-permute-done | bytes 344096 | tf_op jit(solution)/shard_map/ppermute | solution.py:48
  343.3 1.6 collective-permute-start.54
  345.8 7.7 %collective-permute-done.51 = bf16[1,1,112,768]{3,2,1,0:T(8,128)(2,1)S(1)} collective-permute-done((bf16[1,1,112,768]{3,2,1,0:T(8,128)(2,1)S(1)}, bf16[1,1,112,768]{3,2,1,0:T(8,128)(2,1)S(1)}, u32[]{:S(2)}, u32[]{:S(2)}) %collective-permute-start.51) | collective-permute-done | bytes 172064 | tf_op jit(solution)/shard_map/ppermute | solution.py:48
  354.2 1.3 fusion.1
  357.3 1.3 fusion
  (350 shorter events, 57.9 us)
Async XLA Ops:
  2.1 1.7 collective-permute-start
  2.4 1.4 collective-permute-start.1
  4.7 4.2 %copy-start.18 = (bf16[2,96,768]{2,1,0:T(8,128)(2,1)S(1)}, bf16[2,96,768]{2,1,0:T(8,128)(2,1)}, u32[]{:S(2)}) copy-start(bf16[2,96,768]{2,1,0:T(8,128)(2,1)} %param.15) | copy-start | bytes 884740
  4.7 4.2 %copy-start.15 = (bf16[256,768]{1,0:T(8,128)(2,1)S(1)}, bf16[256,768]{1,0:T(8,128)(2,1)}, u32[]{:S(2)}) copy-start(bf16[256,768]{1,0:T(8,128)(2,1)} %param.10) | copy-start | bytes 1179652
  4.7 3.9 %collective-permute-start.2 = (bf16[192,384]{1,0:T(8,128)(2,1)S(1)}, bf16[192,384]{1,0:T(8,128)(2,1)S(1)}, u32[]{:S(2)}, u32[]{:S(2)}) collective-permute-start(bf16[192,384]{1,0:T(8,128)(2,1)S(1)} %broadcast_select_fusion.8), channel_id=1, source_target_pairs={{0,1},{1,0},{2,3},{3,2},{4,5},{5,4},{6,7},{7,6},{8,9},{9,8},{10,11... | collective-permute-start | bytes 442376 | tf_op jit(solution)/shard_map/ppermute | solution.py:48
  5.1 11.6 %collective-permute-start.4 = (bf16[1,1,112,768]{3,2,1,0:T(8,128)(2,1)S(1)}, bf16[1,1,112,768]{3,2,1,0:T(8,128)(2,1)S(1)}, u32[]{:S(2)}, u32[]{:S(2)}) collective-permute-start(bf16[1,1,112,768]{3,2,1,0:T(8,128)(2,1)S(1)} %bitcast.289), channel_id=1, source_target_pairs={{0,16},{1,17},{2,18},{3,19},{4,20},{5,21},{6,22},{7,23},{8,24},{9,... | collective-permute-start | bytes 516104 | tf_op jit(solution)/shard_map/ppermute | solution.py:48
  8.9 24.9 %collective-permute-start.3 = (bf16[256,768]{1,0:T(8,128)(2,1)S(1)}, bf16[256,768]{1,0:T(8,128)(2,1)S(1)}, u32[]{:S(2)}, u32[]{:S(2)}) collective-permute-start(bf16[256,768]{1,0:T(8,128)(2,1)S(1)} %copy-done.15), channel_id=1, source_target_pairs={{0,1},{1,0},{2,3},{3,2},{4,5},{5,4},{6,7},{7,6},{8,9},{9,8},{10,11... | collective-permute-start | bytes 1179656 | tf_op jit(solution)/shard_map/ppermute | solution.py:48
  17.3 15.1 %collective-permute-start.5 = (bf16[2,1,112,768]{3,2,1,0:T(8,128)(2,1)S(1)}, bf16[2,1,112,768]{3,2,1,0:T(8,128)(2,1)S(1)}, u32[]{:S(2)}, u32[]{:S(2)}) collective-permute-start(bf16[2,1,112,768]{3,2,1,0:T(8,128)(2,1)S(1)} %bitcast.276), channel_id=1, source_target_pairs={{0,8},{1,9},{2,10},{3,11},{4,12},{5,13},{6,14},{7,15},{8,0},{9,1},... | collective-permute-start | bytes 1032200 | tf_op jit(solution)/shard_map/ppermute | solution.py:48
  18.2 15.7 %collective-permute-start.7 = (bf16[1,1,192,768]{3,2,1,0:T(8,128)(2,1)S(1)}, bf16[1,1,192,768]{3,2,1,0:T(8,128)(2,1)S(1)}, u32[]{:S(2)}, u32[]{:S(2)}) collective-permute-start(bf16[1,1,192,768]{3,2,1,0:T(8,128)(2,1)S(1)} %bitcast.299), channel_id=1, source_target_pairs={{0,16},{1,17},{2,18},{3,19},{4,20},{5,21},{6,22},{7,23},{8,24},{9,... | collective-permute-start | bytes 884744 | tf_op jit(solution)/shard_map/ppermute | solution.py:48
  33.1 10.1 %collective-permute-start.6 = (bf16[4,1,112,768]{3,2,1,0:T(8,128)(2,1)S(1)}, bf16[4,1,112,768]{3,2,1,0:T(8,128)(2,1)S(1)}, u32[]{:S(2)}, u32[]{:S(2)}) collective-permute-start(bf16[4,1,112,768]{3,2,1,0:T(8,128)(2,1)S(1)} %bitcast.264), channel_id=1, source_target_pairs={{0,2},{1,5},{2,0},{3,7},{4,6},{5,1},{6,4},{7,3},{8,10},{9,13},{10,... | collective-permute-start | bytes 2064392 | tf_op jit(solution)/shard_map/ppermute | solution.py:81
  34.6 13.4 %collective-permute-start.9 = (bf16[2,1,192,768]{3,2,1,0:T(8,128)(2,1)S(1)}, bf16[2,1,192,768]{3,2,1,0:T(8,128)(2,1)S(1)}, u32[]{:S(2)}, u32[]{:S(2)}) collective-permute-start(bf16[2,1,192,768]{3,2,1,0:T(8,128)(2,1)S(1)} %bitcast.268), channel_id=1, source_target_pairs={{0,8},{1,9},{2,10},{3,11},{4,12},{5,13},{6,14},{7,15},{8,0},{9,1},... | collective-permute-start | bytes 1769480 | tf_op jit(solution)/shard_map/ppermute | solution.py:48
  43.8 34.9 %collective-permute-start.8 = (bf16[4,2,112,768]{3,2,1,0:T(8,128)(2,1)S(1)}, bf16[4,2,112,768]{3,2,1,0:T(8,128)(2,1)S(1)}, u32[]{:S(2)}, u32[]{:S(2)}) collective-permute-start(bf16[4,2,112,768]{3,2,1,0:T(8,128)(2,1)S(1)} %shard_map.172.mine_ref), channel_id=1, source_target_pairs={{0,4},{1,3},{2,6},{3,1},{4,0},{5,7},{6,2},{7,5},{8,12},{9,11},{10,... | collective-permute-start | bytes 4128776 | tf_op jit(solution)/shard_map/ppermute | solution.py:81
  48.6 28.1 %collective-permute-start.10 = (bf16[4,1,192,768]{3,2,1,0:T(8,128)(2,1)S(1)}, bf16[4,1,192,768]{3,2,1,0:T(8,128)(2,1)S(1)}, u32[]{:S(2)}, u32[]{:S(2)}) collective-permute-start(bf16[4,1,192,768]{3,2,1,0:T(8,128)(2,1)S(1)} %bitcast.244), channel_id=1, source_target_pairs={{0,2},{1,5},{2,0},{3,7},{4,6},{5,1},{6,4},{7,3},{8,10},{9,13},{10,... | collective-permute-start | bytes 3538952 | tf_op jit(solution)/shard_map/ppermute | solution.py:81
  49.9 5.2 %collective-permute-start.11 = (bf16[1,1,112,768]{3,2,1,0:T(8,128)(2,1)S(1)}, bf16[1,1,112,768]{3,2,1,0:T(8,128)(2,1)S(1)}, u32[]{:S(2)}, u32[]{:S(2)}) collective-permute-start(bf16[1,1,112,768]{3,2,1,0:T(8,128)(2,1)S(1)} %bitcast.287), channel_id=1, source_target_pairs={{0,16},{1,17},{2,18},{3,19},{4,20},{5,21},{6,22},{7,23},{8,24},{9,... | collective-permute-start | bytes 516104 | tf_op jit(solution)/shard_map/ppermute | solution.py:48
  52.2 27.6 %collective-permute-start.14 = (bf16[1,1,192,768]{3,2,1,0:T(8,128)(2,1)S(1)}, bf16[1,1,192,768]{3,2,1,0:T(8,128)(2,1)S(1)}, u32[]{:S(2)}, u32[]{:S(2)}) collective-permute-start(bf16[1,1,192,768]{3,2,1,0:T(8,128)(2,1)S(1)} %bitcast.301), channel_id=1, source_target_pairs={{0,16},{1,17},{2,18},{3,19},{4,20},{5,21},{6,22},{7,23},{8,24},{9,... | collective-permute-start | bytes 884744 | tf_op jit(solution)/shard_map/ppermute | solution.py:48
  55.6 41.2 %collective-permute-start.13 = (bf16[2,1,112,768]{3,2,1,0:T(8,128)(2,1)S(1)}, bf16[2,1,112,768]{3,2,1,0:T(8,128)(2,1)S(1)}, u32[]{:S(2)}, u32[]{:S(2)}) collective-permute-start(bf16[2,1,112,768]{3,2,1,0:T(8,128)(2,1)S(1)} %bitcast.274), channel_id=1, source_target_pairs={{0,8},{1,9},{2,10},{3,11},{4,12},{5,13},{6,14},{7,15},{8,0},{9,1},... | collective-permute-start | bytes 1032200 | tf_op jit(solution)/shard_map/ppermute | solution.py:48
  77.4 48.3 %collective-permute-start.19 = (bf16[4,2,192,768]{3,2,1,0:T(8,128)(2,1)S(1)}, bf16[4,2,192,768]{3,2,1,0:T(8,128)(2,1)S(1)}, u32[]{:S(2)}, u32[]{:S(2)}) collective-permute-start(bf16[4,2,192,768]{3,2,1,0:T(8,128)(2,1)S(1)} %shard_map.175.mine_ref), channel_id=1, source_target_pairs={{0,4},{1,3},{2,6},{3,1},{4,0},{5,7},{6,2},{7,5},{8,12},{9,11},{10,... | collective-permute-start | bytes 7077896 | tf_op jit(solution)/shard_map/ppermute | solution.py:81
  79.7 1.6 collective-permute-start.12
  80.5 14.5 %collective-permute-start.15 = (bf16[2,1,192,768]{3,2,1,0:T(8,128)(2,1)S(1)}, bf16[2,1,192,768]{3,2,1,0:T(8,128)(2,1)S(1)}, u32[]{:S(2)}, u32[]{:S(2)}) collective-permute-start(bf16[2,1,192,768]{3,2,1,0:T(8,128)(2,1)S(1)} %bitcast.266), channel_id=1, source_target_pairs={{0,8},{1,9},{2,10},{3,11},{4,12},{5,13},{6,14},{7,15},{8,0},{9,1},... | collective-permute-start | bytes 1769480 | tf_op jit(solution)/shard_map/ppermute | solution.py:48
  95.5 29.4 %collective-permute-start.17 = (bf16[4,1,192,768]{3,2,1,0:T(8,128)(2,1)S(1)}, bf16[4,1,192,768]{3,2,1,0:T(8,128)(2,1)S(1)}, u32[]{:S(2)}, u32[]{:S(2)}) collective-permute-start(bf16[4,1,192,768]{3,2,1,0:T(8,128)(2,1)S(1)} %bitcast.242), channel_id=1, source_target_pairs={{0,2},{1,5},{2,0},{3,7},{4,6},{5,1},{6,4},{7,3},{8,10},{9,13},{10,... | collective-permute-start | bytes 3538952 | tf_op jit(solution)/shard_map/ppermute | solution.py:81
  97.5 26.2 %collective-permute-start.18 = (bf16[4,1,112,768]{3,2,1,0:T(8,128)(2,1)S(1)}, bf16[4,1,112,768]{3,2,1,0:T(8,128)(2,1)S(1)}, u32[]{:S(2)}, u32[]{:S(2)}) collective-permute-start(bf16[4,1,112,768]{3,2,1,0:T(8,128)(2,1)S(1)} %bitcast.262), channel_id=1, source_target_pairs={{0,2},{1,5},{2,0},{3,7},{4,6},{5,1},{6,4},{7,3},{8,10},{9,13},{10,... | collective-permute-start | bytes 2064392 | tf_op jit(solution)/shard_map/ppermute | solution.py:81
  110.3 15.3 %copy-start.10 = (f32[512,128]{1,0:T(8,128)}, f32[512,128]{1,0:T(8,128)S(1)}, u32[]{:S(2)}) copy-start(f32[512,128]{1,0:T(8,128)S(1)} %get-tuple-element.299.lse_ref) | copy-start | bytes 786436
  110.4 15.3 %collective-permute-start.16 = (bf16[512,768]{1,0:T(8,128)(2,1)S(1)}, bf16[512,768]{1,0:T(8,128)(2,1)S(1)}, u32[]{:S(2)}, u32[]{:S(2)}) collective-permute-start(bf16[512,768]{1,0:T(8,128)(2,1)S(1)} %get-tuple-element.212.mine_ref), channel_id=1, source_target_pairs={{0,1},{1,0},{2,3},{3,2},{4,5},{5,4},{6,7},{7,6},{8,9},{9,8},{10,11... | collective-permute-start | bytes 2359304 | tf_op jit(solution)/shard_map/ppermute | solution.py:48
  124.3 17.5 %collective-permute-start.21 = (bf16[4,2,112,768]{3,2,1,0:T(8,128)(2,1)S(1)}, bf16[4,2,112,768]{3,2,1,0:T(8,128)(2,1)S(1)}, u32[]{:S(2)}, u32[]{:S(2)}) collective-permute-start(bf16[4,2,112,768]{3,2,1,0:T(8,128)(2,1)S(1)} %shard_map.181.mine_ref), channel_id=1, source_target_pairs={{0,4},{1,3},{2,6},{3,1},{4,0},{5,7},{6,2},{7,5},{8,12},{9,11},{10,... | collective-permute-start | bytes 4128776 | tf_op jit(solution)/shard_map/ppermute | solution.py:81
  131.9 5.1 %collective-permute-start.20 = (bf16[512,768]{1,0:T(8,128)(2,1)S(1)}, bf16[512,768]{1,0:T(8,128)(2,1)S(1)}, u32[]{:S(2)}, u32[]{:S(2)}) collective-permute-start(bf16[512,768]{1,0:T(8,128)(2,1)S(1)} %get-tuple-element.220.mine_ref), channel_id=1, source_target_pairs={{0,1},{1,0},{2,3},{3,2},{4,5},{5,4},{6,7},{7,6},{8,9},{9,8},{10,11... | collective-permute-start | bytes 2359304 | tf_op jit(solution)/shard_map/ppermute | solution.py:48
  135.1 32.0 %collective-permute-start.24 = (bf16[4,2,192,768]{3,2,1,0:T(8,128)(2,1)S(1)}, bf16[4,2,192,768]{3,2,1,0:T(8,128)(2,1)S(1)}, u32[]{:S(2)}, u32[]{:S(2)}) collective-permute-start(bf16[4,2,192,768]{3,2,1,0:T(8,128)(2,1)S(1)} %shard_map.182.mine_ref), channel_id=1, source_target_pairs={{0,4},{1,3},{2,6},{3,1},{4,0},{5,7},{6,2},{7,5},{8,12},{9,11},{10,... | collective-permute-start | bytes 7077896 | tf_op jit(solution)/shard_map/ppermute | solution.py:81
  142.5 3.5 copy-start.16
  142.7 4.4 %collective-permute-start.22 = (bf16[8,48,384]{2,1,0:T(8,128)(2,1)S(1)}, bf16[8,48,384]{2,1,0:T(8,128)(2,1)S(1)}, u32[]{:S(2)}, u32[]{:S(2)}) collective-permute-start(bf16[8,48,384]{2,1,0:T(8,128)(2,1)S(1)} %dynamic-slice_bitcast_fusion.2), channel_id=1, source_target_pairs={{0,1},{1,0},{2,3},{3,2},{4,5},{5,4},{6,7},{7,6},{8,9},{9,8},{10,11... | collective-permute-start | bytes 884744 | tf_op jit(solution)/shard_map/ppermute | solution.py:48
  146.0 13.8 %collective-permute-start.25 = (bf16[256,768]{1,0:T(8,128)(2,1)S(1)}, bf16[256,768]{1,0:T(8,128)(2,1)S(1)}, u32[]{:S(2)}, u32[]{:S(2)}) collective-permute-start(bf16[256,768]{1,0:T(8,128)(2,1)S(1)} %copy-done.16), channel_id=1, source_target_pairs={{0,1},{1,0},{2,3},{3,2},{4,5},{5,4},{6,7},{7,6},{8,9},{9,8},{10,11... | collective-permute-start | bytes 1179656 | tf_op jit(solution)/shard_map/ppermute | solution.py:48
  159.4 2.4 collective-permute-start.23
  172.6 5.1 %collective-permute-start.26 = (bf16[512,768]{1,0:T(8,128)(2,1)S(1)}, bf16[512,768]{1,0:T(8,128)(2,1)S(1)}, u32[]{:S(2)}, u32[]{:S(2)}) collective-permute-start(bf16[512,768]{1,0:T(8,128)(2,1)S(1)} %get-tuple-element.245.mine_ref), channel_id=1, source_target_pairs={{0,1},{1,0},{2,3},{3,2},{4,5},{5,4},{6,7},{7,6},{8,9},{9,8},{10,11... | collective-permute-start | bytes 2359304 | tf_op jit(solution)/shard_map/ppermute | solution.py:48
  188.2 2.8 collective-permute-start.29
  188.8 24.5 %collective-permute-start.27 = (bf16[4,2,96,768]{3,2,1,0:T(8,128)(2,1)S(1)}, bf16[4,2,96,768]{3,2,1,0:T(8,128)(2,1)S(1)}, u32[]{:S(2)}, u32[]{:S(2)}) collective-permute-start(bf16[4,2,96,768]{3,2,1,0:T(8,128)(2,1)S(1)} %shard_map.192), channel_id=1, source_target_pairs={{0,4},{1,3},{2,6},{3,1},{4,0},{5,7},{6,2},{7,5},{8,12},{9,11},{10,... | collective-permute-start | bytes 3538952 | tf_op jit(solution)/shard_map/ppermute | solution.py:81
  190.8 26.1 %collective-permute-start.28 = (bf16[4,2,96,768]{3,2,1,0:T(8,128)(2,1)S(1)}, bf16[4,2,96,768]{3,2,1,0:T(8,128)(2,1)S(1)}, u32[]{:S(2)}, u32[]{:S(2)}) collective-permute-start(bf16[4,2,96,768]{3,2,1,0:T(8,128)(2,1)S(1)} %shard_map.194), channel_id=1, source_target_pairs={{0,4},{1,3},{2,6},{3,1},{4,0},{5,7},{6,2},{7,5},{8,12},{9,11},{10,... | collective-permute-start | bytes 3538952 | tf_op jit(solution)/shard_map/ppermute | solution.py:81
  207.8 11.4 %collective-permute-start.32 = (bf16[512,768]{1,0:T(8,128)(2,1)S(1)}, bf16[512,768]{1,0:T(8,128)(2,1)S(1)}, u32[]{:S(2)}, u32[]{:S(2)}) collective-permute-start(bf16[512,768]{1,0:T(8,128)(2,1)S(1)} %get-tuple-element.282.refs_1_), channel_id=1, source_target_pairs={{0,1},{1,0},{2,3},{3,2},{4,5},{5,4},{6,7},{7,6},{8,9},{9,8},{10,11... | collective-permute-start | bytes 2359304 | tf_op jit(solution)/shard_map/ppermute | solution.py:48
  208.7 2.3 collective-permute-start.30
  211.9 38.4 %collective-permute-start.37 = (bf16[4,2,112,768]{3,2,1,0:T(8,128)(2,1)S(1)}, bf16[4,2,112,768]{3,2,1,0:T(8,128)(2,1)S(1)}, u32[]{:S(2)}, u32[]{:S(2)}) collective-permute-start(bf16[4,2,112,768]{3,2,1,0:T(8,128)(2,1)S(1)} %shard_map.196), channel_id=1, source_target_pairs={{0,4},{1,3},{2,6},{3,1},{4,0},{5,7},{6,2},{7,5},{8,12},{9,11},{10,... | collective-permute-start | bytes 4128776 | tf_op jit(solution)/shard_map/ppermute | solution.py:81
  217.9 31.6 %collective-permute-start.31 = (bf16[4,1,192,768]{3,2,1,0:T(8,128)(2,1)S(1)}, bf16[4,1,192,768]{3,2,1,0:T(8,128)(2,1)S(1)}, u32[]{:S(2)}, u32[]{:S(2)}) collective-permute-start(bf16[4,1,192,768]{3,2,1,0:T(8,128)(2,1)S(1)} %get-tuple-element.280), channel_id=1, source_target_pairs={{0,2},{1,5},{2,0},{3,7},{4,6},{5,1},{6,4},{7,3},{8,10},{9,13},{10,... | collective-permute-start | bytes 3538952 | tf_op jit(solution)/shard_map/ppermute | solution.py:81
  227.3 3.6 collective-permute-start.33
  228.7 30.5 %collective-permute-start.35 = (bf16[4,2,96,768]{3,2,1,0:T(8,128)(2,1)S(1)}, bf16[4,2,96,768]{3,2,1,0:T(8,128)(2,1)S(1)}, u32[]{:S(2)}, u32[]{:S(2)}) collective-permute-start(bf16[4,2,96,768]{3,2,1,0:T(8,128)(2,1)S(1)} %shard_map.199), channel_id=1, source_target_pairs={{0,4},{1,3},{2,6},{3,1},{4,0},{5,7},{6,2},{7,5},{8,12},{9,11},{10,... | collective-permute-start | bytes 3538952 | tf_op jit(solution)/shard_map/ppermute | solution.py:81
  229.6 47.3 %collective-permute-start.36 = (bf16[4,2,96,768]{3,2,1,0:T(8,128)(2,1)S(1)}, bf16[4,2,96,768]{3,2,1,0:T(8,128)(2,1)S(1)}, u32[]{:S(2)}, u32[]{:S(2)}) collective-permute-start(bf16[4,2,96,768]{3,2,1,0:T(8,128)(2,1)S(1)} %shard_map.201), channel_id=1, source_target_pairs={{0,4},{1,3},{2,6},{3,1},{4,0},{5,7},{6,2},{7,5},{8,12},{9,11},{10,... | collective-permute-start | bytes 3538952 | tf_op jit(solution)/shard_map/ppermute | solution.py:81
  247.8 2.4 copy-start.8
  248.9 54.8 %collective-permute-start.39 = (bf16[256,768]{1,0:T(8,128)(2,1)}, bf16[256,768]{1,0:T(8,128)(2,1)}, u32[]{:S(2)}, u32[]{:S(2)}) collective-permute-start(bf16[256,768]{1,0:T(8,128)(2,1)} %get-tuple-element.393), channel_id=1, source_target_pairs={{0,1},{1,0},{2,3},{3,2},{4,5},{5,4},{6,7},{7,6},{8,9},{9,8},{10,11... | collective-permute-start | bytes 1179656 | tf_op jit(solution)/shard_map/ppermute | solution.py:48
  250.2 29.9 %collective-permute-start.34 = (bf16[2,1,192,768]{3,2,0,1:T(8,128)(2,1)S(1)}, bf16[2,1,192,768]{3,2,0,1:T(8,128)(2,1)S(1)}, u32[]{:S(2)}, u32[]{:S(2)}) collective-permute-start(bf16[2,1,192,768]{3,2,0,1:T(8,128)(2,1)S(1)} %bitcast.304), channel_id=1, source_target_pairs={{0,8},{1,9},{2,10},{3,11},{4,12},{5,13},{6,14},{7,15},{8,0},{9,1},... | collective-permute-start | bytes 1769480 | tf_op jit(solution)/shard_map/ppermute | solution.py:48
  251.2 30.4 %collective-permute-start.41 = (bf16[4,1,112,768]{3,2,1,0:T(8,128)(2,1)S(1)}, bf16[4,1,112,768]{3,2,1,0:T(8,128)(2,1)S(1)}, u32[]{:S(2)}, u32[]{:S(2)}) collective-permute-start(bf16[4,1,112,768]{3,2,1,0:T(8,128)(2,1)S(1)} %get-tuple-element.305), channel_id=1, source_target_pairs={{0,2},{1,5},{2,0},{3,7},{4,6},{5,1},{6,4},{7,3},{8,10},{9,13},{10,... | collective-permute-start | bytes 2064392 | tf_op jit(solution)/shard_map/ppermute | solution.py:81
  278.9 4.1 %copy-start.2 = (f32[4,1,192,768]{3,2,1,0:T(8,128)}, f32[4,1,192,768]{3,2,1,0:T(8,128)S(1)}, u32[]{:S(2)}) copy-start(f32[4,1,192,768]{3,2,1,0:T(8,128)S(1)} %get-tuple-element.313) | copy-start | bytes 7077892
  278.9 21.5 %collective-permute-start.40 = (bf16[4,1,192,768]{3,2,1,0:T(8,128)(2,1)}, bf16[4,1,192,768]{3,2,1,0:T(8,128)(2,1)}, u32[]{:S(2)}, u32[]{:S(2)}) collective-permute-start(bf16[4,1,192,768]{3,2,1,0:T(8,128)(2,1)} %get-tuple-element.308), channel_id=1, source_target_pairs={{0,2},{1,5},{2,0},{3,7},{4,6},{5,1},{6,4},{7,3},{8,10},{9,13},{10,... | collective-permute-start | bytes 3538952 | tf_op jit(solution)/shard_map/ppermute | solution.py:81
  281.6 2.9 copy-start.13
  283.0 2.6 collective-permute-start.42
  284.5 14.7 %collective-permute-start.44 = (bf16[2,1,112,768]{3,2,0,1:T(8,128)(2,1)}, bf16[2,1,112,768]{3,2,0,1:T(8,128)(2,1)}, u32[]{:S(2)}, u32[]{:S(2)}) collective-permute-start(bf16[2,1,112,768]{3,2,0,1:T(8,128)(2,1)} %bitcast.99), channel_id=1, source_target_pairs={{0,8},{1,9},{2,10},{3,11},{4,12},{5,13},{6,14},{7,15},{8,0},{9,1},... | collective-permute-start | bytes 1032200 | tf_op jit(solution)/shard_map/ppermute | solution.py:48
  287.7 23.0 %collective-permute-start.47 = (bf16[4,2,112,768]{3,2,1,0:T(8,128)(2,1)}, bf16[4,2,112,768]{3,2,1,0:T(8,128)(2,1)}, u32[]{:S(2)}, u32[]{:S(2)}) collective-permute-start(bf16[4,2,112,768]{3,2,1,0:T(8,128)(2,1)} %shard_map.208), channel_id=1, source_target_pairs={{0,4},{1,3},{2,6},{3,1},{4,0},{5,7},{6,2},{7,5},{8,12},{9,11},{10,... | collective-permute-start | bytes 4128776 | tf_op jit(solution)/shard_map/ppermute | solution.py:81
  288.0 18.2 %collective-permute-start.38 = (bf16[1,1,192,768]{3,2,1,0:T(8,128)(2,1)}, bf16[1,1,192,768]{3,2,1,0:T(8,128)(2,1)S(1)}, u32[]{:S(2)}, u32[]{:S(2)}) collective-permute-start(bf16[1,1,192,768]{3,2,1,0:T(8,128)(2,1)} %copy-done.13), channel_id=1, source_target_pairs={{0,16},{1,17},{2,18},{3,19},{4,20},{5,21},{6,22},{7,23},{8,24},{9,... | collective-permute-start | bytes 884744 | tf_op jit(solution)/shard_map/ppermute | solution.py:48
  300.3 25.8 %collective-permute-start.45 = (bf16[1,1,112,768]{3,2,1,0:T(8,128)(2,1)S(1)}, bf16[1,1,112,768]{3,2,1,0:T(8,128)(2,1)S(1)}, u32[]{:S(2)}, u32[]{:S(2)}) collective-permute-start(bf16[1,1,112,768]{3,2,1,0:T(8,128)(2,1)S(1)} %get-tuple-element.334), channel_id=1, source_target_pairs={{0,16},{1,17},{2,18},{3,19},{4,20},{5,21},{6,22},{7,23},{8,24},{9,... | collective-permute-start | bytes 516104 | tf_op jit(solution)/shard_map/ppermute | solution.py:48
  303.7 2.6 copy-start.7
  303.7 20.4 %collective-permute-start.46 = (bf16[2,1,192,768]{3,2,0,1:T(8,128)(2,1)S(1)}, bf16[2,1,192,768]{3,2,0,1:T(8,128)(2,1)S(1)}, u32[]{:S(2)}, u32[]{:S(2)}) collective-permute-start(bf16[2,1,192,768]{3,2,0,1:T(8,128)(2,1)S(1)} %bitcast.305), channel_id=1, source_target_pairs={{0,8},{1,9},{2,10},{3,11},{4,12},{5,13},{6,14},{7,15},{8,0},{9,1},... | collective-permute-start | bytes 1769480 | tf_op jit(solution)/shard_map/ppermute | solution.py:48
  306.4 50.8 %collective-permute-start.43 = (f32[24,1536]{1,0:T(8,128)S(1)}, f32[24,1536]{1,0:T(8,128)S(1)}, u32[]{:S(2)}, u32[]{:S(2)}) collective-permute-start(f32[24,1536]{1,0:T(8,128)S(1)} %get-tuple-element.441), channel_id=1, source_target_pairs={{0,1},{1,0},{2,3},{3,2},{4,5},{5,4},{6,7},{7,6},{8,9},{9,8},{10,11... | collective-permute-start | bytes 442376 | tf_op jit(solution)/shard_map/ppermute | solution.py:48
  312.3 13.9 %collective-permute-start.49 = (bf16[4,1,112,768]{3,2,1,0:T(8,128)(2,1)S(1)}, bf16[4,1,112,768]{3,2,1,0:T(8,128)(2,1)S(1)}, u32[]{:S(2)}, u32[]{:S(2)}) collective-permute-start(bf16[4,1,112,768]{3,2,1,0:T(8,128)(2,1)S(1)} %get-tuple-element.337), channel_id=1, source_target_pairs={{0,2},{1,5},{2,0},{3,7},{4,6},{5,1},{6,4},{7,3},{8,10},{9,13},{10,... | collective-permute-start | bytes 2064392 | tf_op jit(solution)/shard_map/ppermute | solution.py:81
  324.7 18.4 %collective-permute-start.53 = (bf16[1,1,192,768]{3,2,1,0:T(8,128)(2,1)S(1)}, bf16[1,1,192,768]{3,2,1,0:T(8,128)(2,1)S(1)}, u32[]{:S(2)}, u32[]{:S(2)}) collective-permute-start(bf16[1,1,192,768]{3,2,1,0:T(8,128)(2,1)S(1)} %get-tuple-element.339), channel_id=1, source_target_pairs={{0,16},{1,17},{2,18},{3,19},{4,20},{5,21},{6,22},{7,23},{8,24},{9,... | collective-permute-start | bytes 884744 | tf_op jit(solution)/shard_map/ppermute | solution.py:48
  326.9 15.2 %collective-permute-start.50 = (bf16[2,1,112,768]{3,2,0,1:T(8,128)(2,1)S(1)}, bf16[2,1,112,768]{3,2,0,1:T(8,128)(2,1)S(1)}, u32[]{:S(2)}, u32[]{:S(2)}) collective-permute-start(bf16[2,1,112,768]{3,2,0,1:T(8,128)(2,1)S(1)} %bitcast.306), channel_id=1, source_target_pairs={{0,8},{1,9},{2,10},{3,11},{4,12},{5,13},{6,14},{7,15},{8,0},{9,1},... | collective-permute-start | bytes 1032200 | tf_op jit(solution)/shard_map/ppermute | solution.py:48
  329.1 27.5 %collective-permute-start.48 = (f32[32,1152]{1,0:T(8,128)S(1)}, f32[32,1152]{1,0:T(8,128)S(1)}, u32[]{:S(2)}, u32[]{:S(2)}) collective-permute-start(f32[32,1152]{1,0:T(8,128)S(1)} %select_maximum_fusion.1), channel_id=1, source_target_pairs={{0,1},{1,0},{2,3},{3,2},{4,5},{5,4},{6,7},{7,6},{8,9},{9,8},{10,11... | collective-permute-start | bytes 442376 | tf_op jit(solution)/shard_map/ppermute | solution.py:48
  342.7 10.8 %collective-permute-start.51 = (bf16[1,1,112,768]{3,2,1,0:T(8,128)(2,1)S(1)}, bf16[1,1,112,768]{3,2,1,0:T(8,128)(2,1)S(1)}, u32[]{:S(2)}, u32[]{:S(2)}) collective-permute-start(bf16[1,1,112,768]{3,2,1,0:T(8,128)(2,1)S(1)} %get-tuple-element.347), channel_id=1, source_target_pairs={{0,16},{1,17},{2,18},{3,19},{4,20},{5,21},{6,22},{7,23},{8,24},{9,... | collective-permute-start | bytes 516104 | tf_op jit(solution)/shard_map/ppermute | solution.py:48
  343.3 10.9 %collective-permute-start.54 = (f32[24,1536]{1,0:T(8,128)S(1)}, f32[24,1536]{1,0:T(8,128)S(1)}, u32[]{:S(2)}, u32[]{:S(2)}) collective-permute-start(f32[24,1536]{1,0:T(8,128)S(1)} %get-tuple-element.433), channel_id=1, source_target_pairs={{0,1},{1,0},{2,3},{3,2},{4,5},{5,4},{6,7},{7,6},{8,9},{9,8},{10,11... | collective-permute-start | bytes 442376 | tf_op jit(solution)/shard_map/ppermute | solution.py:48
  353.6 2.7 collective-permute-start.52
  357.3 4.9 %copy-start.1 = (bf16[2,96]{1,0:T(2,128)(2,1)S(1)}, bf16[2,96]{1,0:T(2,128)(2,1)}, u32[]{:S(2)}) copy-start(bf16[2,96]{1,0:T(2,128)(2,1)} %param.18) | copy-start | bytes 1156
  (13 other events, 21.1 us)
